TPU v7x, 32 devices: a whole 2x2x4 slice. The times are simulated.
32 devices in a mesh: row: 8 (over z, x), col: 4 (over y, core).
Axes of the slice: x: 2, y: 2, z: 4, core: 2. Of those that a mesh axis runs over, the one named last changes fastest.
Arguments:
- qkv: bfloat16 [3, 1408, 16384], P(None, 'col', 'row'), may hold values from -12.1 to 12.1
- residual_in: bfloat16 [1408, 16384], P('col', 'row'), may hold values from -3 to 3
- out_weight: bfloat16 [1408, 1408], replicated, may hold values from -0.625 to 0.625
- merge_weight: bfloat16 [1408, 5632], P('col'), may hold values from -0.078125 to 0.078125
- merge_gain: float32 [1408], replicated, may hold values from 0.1 to 1.9
- image_groups: int32 [32], replicated, may hold values from 1 to 256, 4096 in all
- dest_row: int32 [4096], P('row'), may hold values from 0 to 4095, as said below
Outputs:
- layer_out: bfloat16 [1408, 16384], P('col', 'row')
- image_rows: bfloat16 [1408, 4096], P('col', 'row')
Inputs may be any that keep to these rules, and one draw needn't show every extreme that they name: dest_row is a permutation of 0 to 4095. Of the 512 entries held by each index of row, exactly 64 fall in each aligned block of 512 output rows.
All inputs are finite; a program needn't handle non-finite values.
Results may differ from a plain program's by a relative error of at most 0.0064.
Values may be sent and summed in bfloat16 or wider, within the bound.
No kernel may reach another device: no remote copies, remote signals or barrier semaphores. Data moves between devices by JAX's collectives and lax.ppermute only.
A program may use at most 128 MiB of HBM per device.

v0:
```python
import functools
import math

import jax
import jax.numpy as jnp
from jax import lax
from jax.experimental import pallas as pl
from jax.experimental.pallas import tpu as pltpu
from jax.sharding import PartitionSpec as P

HEAD_DIM = 88
TILE = 256
FAR = -1e30
BF = jnp.bfloat16
F32 = jnp.float32


def params(mib):
    return pltpu.CompilerParams(vmem_limit_bytes=mib * 1024 * 1024)


def cost(flops, bytes_accessed):
    return pl.CostEstimate(flops=int(flops), bytes_accessed=int(bytes_accessed), transcendentals=0)


def round_up(value, unit):
    return -(-value // unit) * unit


def key_tile(keys, label, images, depth, kt_ref):
    heads = keys.shape[0] // HEAD_DIM
    tail = depth - HEAD_DIM
    at = lax.broadcasted_iota(jnp.int32, (tail, TILE), 0)
    mask = jnp.where((at == label) | (at >= images), 0.0, FAR)
    for head in range(heads):
        whole = jnp.concatenate([keys[head * HEAD_DIM : (head + 1) * HEAD_DIM], mask], axis=0)
        kt_ref[0, head] = jnp.transpose(whole).astype(BF)


def value_tile(values, v_ref):
    heads = values.shape[0] // HEAD_DIM
    ones = jnp.where(lax.broadcasted_iota(jnp.int32, (8, TILE), 0) == 0, 1.0, 0.0)
    for head in range(heads):
        v_ref[0, head] = jnp.concatenate(
            [values[head * HEAD_DIM : (head + 1) * HEAD_DIM], ones], axis=0
        ).astype(BF)


def prepare_own(images, depth, label_ref, qkv_ref, q_ref, kt_ref, v_ref):
    label = label_ref[0]
    queries = qkv_ref[0].astype(F32)
    heads = queries.shape[0] // HEAD_DIM
    at = lax.broadcasted_iota(jnp.int32, (depth - HEAD_DIM, TILE), 0)
    mark = jnp.where(at == label, 1.0, 0.0)
    for head in range(heads):
        q_ref[0, head] = jnp.concatenate(
            [queries[head * HEAD_DIM : (head + 1) * HEAD_DIM], mark], axis=0
        ).astype(BF)
    key_tile(qkv_ref[1].astype(F32), label, images, depth, kt_ref)
    value_tile(qkv_ref[2].astype(F32), v_ref)


def reorder_residual(perm_ref, low_ref, high_ref, out_ref):
    both = jnp.concatenate([low_ref[...], high_ref[...]], axis=1)
    out_ref[0] = jnp.dot(both, perm_ref[...], preferred_element_type=F32).astype(BF)


def attend(own, halos, images, base, rate, q_tiles, bounds, label_ref, perm_ref, *refs):
    count = len(halos)
    q_refs, refs = refs[: len(q_tiles)], refs[len(q_tiles) :]
    kt_ref, v_ref, chunk_refs = refs[0], refs[1], refs[2 : 2 + count]
    refs = refs[-(9 + count) :]
    out_ref, kt_s, v_s, scores_s, acc, top, att = refs[:7]
    raw_s, sems, own_sems = refs[7 : 7 + count], refs[-2], refs[-1]
    heads = q_refs[0].shape[1]
    depth = kt_s.shape[3]
    slots = pl.ds(own[0] - base, len(own))
    chunk_copies = [
        pltpu.make_async_copy(chunk_ref, raw, sems.at[at])
        for at, (chunk_ref, raw) in enumerate(zip(chunk_refs, raw_s))
    ]
    kt_copy = pltpu.make_async_copy(kt_ref, kt_s.at[slots], own_sems.at[0])
    v_copy = pltpu.make_async_copy(v_ref, v_s.at[slots], own_sems.at[1])
    for copy in chunk_copies + [kt_copy, v_copy]:
        copy.start()
    for tiles, copy, raw in zip(halos, chunk_copies, raw_s):
        copy.wait()
        for at, tile in enumerate(tiles):
            lanes = slice(at * TILE, (at + 1) * TILE)
            slot = pl.ds(tile - base, 1)
            key_tile(raw[0, :, lanes].astype(F32), label_ref[tile], images, depth, kt_s.at[slot])
            value_tile(raw[1, :, lanes].astype(F32), v_s.at[slot])
    kt_copy.wait()
    for side, q_ref in enumerate(q_refs):
        begin, end = bounds[0, q_tiles[side]], bounds[1, q_tiles[side]]
        acc[...] = jnp.zeros_like(acc)
        top[...] = jnp.full_like(top, FAR)

        def sweep(step):
            pairs = (end - begin) // 2

            def pair(index, carry):
                step(begin + 2 * index, 2)
                return carry

            def single(index, carry):
                step(end - 1, 1)
                return carry

            lax.fori_loop(0, pairs, pair, 0)
            lax.fori_loop(0, end - begin - 2 * pairs, single, 0)

        def score(tile, span):
            for head in range(heads):
                keys = kt_s[pl.ds(tile - base, span), head].reshape(span * TILE, -1)
                scores = jnp.dot(keys, q_ref[0, head], preferred_element_type=F32)
                scores_s[pl.ds(tile - begin, span), head] = scores.reshape(span, TILE, TILE)
                highest = jnp.max(scores.reshape(span * TILE // 8, 8, TILE), axis=0)
                top[head] = jnp.maximum(top[head], highest)

        sweep(score)
        if side == 0:
            v_copy.wait()
        tops = [jnp.max(top[head], axis=0, keepdims=True) for head in range(heads)]
        for head in range(heads):
            top[head, 0:1] = tops[head]

        def weigh(tile, span):
            for head in range(heads):
                scores = scores_s[pl.ds(tile - begin, span), head].reshape(span * TILE, TILE)
                weights = jnp.exp2((scores - top[head, 0:1]) * rate).astype(BF)
                values = [v_s[tile - base + at, head] for at in range(span)]
                values = values[0] if span == 1 else jnp.concatenate(values, axis=1)
                acc[head] += jnp.dot(values, weights, preferred_element_type=F32)

        sweep(weigh)
        whole = jnp.concatenate(
            [acc[head, :HEAD_DIM] / acc[head, HEAD_DIM : HEAD_DIM + 1] for head in range(heads)], axis=0
        )
        att[:, side * TILE : (side + 1) * TILE] = whole.astype(BF)
        if side % 2:
            lanes = slice((side - 1) * TILE, (side + 1) * TILE)
            out_ref[:, lanes] = jnp.dot(
                att[:, lanes], perm_ref[...], preferred_element_type=F32
            ).astype(BF)


def project(order, last, paired, col_ref, perm_ref, gain_ref, res_ref, wt_ref, mw_ref, *refs):
    count = len(order)
    att_refs, refs = refs[:count], refs[count:]
    if paired:
        before_ref = refs[0]
    refs = refs[-9:]
    layer_ref, out_ref, gathered, layer_s, wt_s, mw_s, att_sem, wt_sem, mw_sem = refs
    width = att_refs[0].shape[0]
    full = wt_ref.shape[0]
    block = 2 * TILE
    blocks = layer_s.shape[1] // block
    groups = block // 4
    col = col_ref[0]
    att_copies, wt_copies = [], []
    for part, (bit, att_ref) in enumerate(zip(order, att_refs)):
        row = pl.multiple_of((col ^ bit) * width, 16)
        att_copies.append(
            pltpu.make_async_copy(att_ref, gathered.at[pl.ds(row, width), :], att_sem.at[part])
        )
        rows = pl.ds(part * width, width)
        wt_copies.append(
            pltpu.make_async_copy(wt_ref.at[rows, :], wt_s.at[rows, :], wt_sem.at[part])
        )
    mw_copy = pltpu.make_async_copy(mw_ref, mw_s, mw_sem.at[0])
    for copy in att_copies + wt_copies + [mw_copy] * last:
        copy.start()
    for copy in att_copies:
        copy.wait()
    for part in range(count):
        rows = slice(part * width, (part + 1) * width)
        wt_copies[part].wait()
        for at in range(blocks):
            lanes = slice(at * block, (at + 1) * block)
            projected = jnp.dot(wt_s[rows, :], gathered[:, lanes], preferred_element_type=F32)
            layer_s[rows, lanes] = (res_ref[part, at].astype(F32) + projected).astype(BF)
    own = pl.ds(pl.multiple_of(col * width, 16), width)
    for at in range(blocks):
        lanes = slice(at * block, (at + 1) * block)
        layer_ref[:, lanes] = lax.dot_general(
            layer_s[own, lanes], perm_ref[...], (((1,), (1,)), ((), ())), preferred_element_type=F32
        ).astype(BF)
    if last:
        mw_copy.wait()
    merged = None
    for j in range(4):
        columns = []
        for at in range(blocks):
            lanes = slice(at * block + j * groups, at * block + (j + 1) * groups)
            values = layer_s[:, lanes].astype(F32)
            values = values - jnp.sum(values, axis=0, keepdims=True) / full
            spread = jnp.sum(jnp.square(values), axis=0, keepdims=True) / full
            normed = (values * lax.rsqrt(spread + 1e-06) * gain_ref[...]).astype(BF)
            if last:
                columns.append(normed)
            else:
                out_ref[:, lanes] = normed
        if last:
            if paired:
                columns = [before_ref[:, j * groups : (j + 1) * groups]] + columns
            both = jnp.concatenate(columns, axis=1)
            term = jnp.dot(mw_s[:, j * full : (j + 1) * full], both, preferred_element_type=F32)
            merged = term if merged is None else merged + term
    if last:
        out_ref[...] = merged.astype(BF)


def outgoing(pieces, slot_ref, place_ref, *refs):
    merged_refs, out_refs = refs[:-pieces], refs[-pieces:]
    total = None
    share, wide = out_refs[0].shape
    for part, merged_ref in enumerate(merged_refs):
        groups = merged_ref.shape[1]
        row = lax.broadcasted_iota(jnp.int32, (share * pieces, groups), 0)
        pick = jnp.where(row == slot_ref[part], 1.0, 0.0).astype(BF)
        rows = jnp.concatenate([merged_ref[...], place_ref[part]], axis=0)
        term = lax.dot_general(pick, rows, (((1,), (1,)), ((), ())), preferred_element_type=F32)
        total = term if total is None else total + term
    for piece, out_ref in enumerate(out_refs):
        out_ref[...] = total[piece * share : (piece + 1) * share].astype(BF)


def incoming(width, base, *refs):
    in_refs, out_ref = refs[:-1], refs[-1]
    rows = jnp.concatenate([in_ref[...] for in_ref in in_refs], axis=0)
    place = rows[:, width : width + 2].astype(F32)
    target = (place[:, 0:1] * base + place[:, 1:2]).astype(jnp.int32)
    slots = rows.shape[0]
    lane = lax.broadcasted_iota(jnp.int32, (slots, slots), 1)
    pick = jnp.where(lane == target, 1.0, 0.0).astype(BF)
    out_ref[...] = lax.dot_general(
        rows[:, :width], pick, (((0,), (0,)), ((), ())), preferred_element_type=F32
    ).astype(BF)


def body(qkv, residual_in, out_weight, merge_weight, merge_gain, image_groups, dest_row):
    width = qkv.shape[1]
    tokens = qkv.shape[2]
    heads = width // HEAD_DIM
    full = out_weight.shape[0]
    images = image_groups.shape[0]
    reach = tokens // 2
    own_tiles = tokens // TILE
    far_tiles = reach // TILE
    half = own_tiles // 2
    plan = [half // 2] + [1] * (half - half // 2)
    begins = [sum(plan[:s]) for s in range(len(plan))]
    stages = len(plan)
    depth = round_up(HEAD_DIM + images, 128)
    rate = math.log2(math.e) / math.sqrt(HEAD_DIM)
    rows, cols = lax.axis_size("row"), lax.axis_size("col")
    row_id, col_id = lax.axis_index("row"), lax.axis_index("col")
    forward = [(i, (i + 1) % rows) for i in range(rows)]
    backward = [((i + 1) % rows, i) for i in range(rows)]

    lefts, rights = [], []

    def send_chunk(stage, after):
        source = qkv
        if after is not None:
            source, _ = lax.optimization_barrier((qkv, after))
        near, far = begins[stage] * TILE, (begins[stage] + plan[stage]) * TILE
        tail = lax.slice(source, (1, 0, tokens - far), (3, width, tokens - near))
        head = lax.slice(source, (1, 0, near), (3, width, far))
        lefts.append(lax.ppermute(tail, "row", forward))
        rights.append(lax.ppermute(head, "row", backward))
        return tail, head

    first_chunk = send_chunk(0, None)

    image_ends = jnp.cumsum(image_groups) * 4
    window_tiles = own_tiles + 2 * far_tiles
    positions = row_id * tokens - reach + jnp.arange(window_tiles * TILE, dtype=jnp.int32)
    labels = jnp.sum((positions[:, None] >= image_ends[None, :]).astype(jnp.int32), axis=1)
    labels = jnp.where(positions >= 0, labels, -1).reshape(window_tiles, 1, TILE)
    starts = row_id * tokens + jnp.arange(own_tiles, dtype=jnp.int32) * TILE
    ends = starts + TILE - 1
    low = jnp.max(jnp.where(image_ends[None, :] <= starts[:, None], image_ends[None, :], 0), axis=1)
    high = jnp.min(
        jnp.where(image_ends[None, :] > ends[:, None], image_ends[None, :], rows * tokens), axis=1
    )
    window_start = row_id * tokens - reach
    low = (low - window_start) // TILE
    high = (high - window_start + TILE - 1) // TILE
    tile_at = jnp.arange(own_tiles, dtype=jnp.int32)
    low = jnp.maximum(low, tile_at)
    high = jnp.minimum(high, tile_at + 2 * far_tiles + 1)

    inner = plan[0]

    def pair_tile(block, which):
        near = half - inner + 2 * block + which
        mirrored = half + block if which else half - 1 - block
        if isinstance(block, int):
            return near if block < inner else mirrored
        return jnp.where(block < inner, near, mirrored)

    at = jnp.arange(2 * TILE, dtype=jnp.int32)
    perm = (((at % 4) * (TILE // 2) + at // 4)[:, None] == at[None, :]).astype(BF)

    qkv_after, _ = lax.optimization_barrier((qkv, first_chunk))
    kt_shape, v_shape = (heads, TILE, depth), (heads, HEAD_DIM + 8, TILE)
    q_tiles, kt_own, v_own = pl.pallas_call(
        functools.partial(prepare_own, images, depth),
        grid=(own_tiles,),
        in_specs=[
            pl.BlockSpec((1, 1, TILE), lambda i: (i + far_tiles, 0, 0)),
            pl.BlockSpec((3, width, TILE), lambda i: (0, 0, i)),
        ],
        out_specs=[
            pl.BlockSpec((1, heads, depth, TILE), lambda i: (i, 0, 0, 0)),
            pl.BlockSpec((1,) + kt_shape, lambda i: (i, 0, 0, 0)),
            pl.BlockSpec((1,) + v_shape, lambda i: (i, 0, 0, 0)),
        ],
        out_shape=[
            jax.ShapeDtypeStruct((own_tiles, heads, depth, TILE), BF),
            jax.ShapeDtypeStruct((own_tiles,) + kt_shape, BF),
            jax.ShapeDtypeStruct((own_tiles,) + v_shape, BF),
        ],
        compiler_params=params(16),
        cost_estimate=cost(2e9, 1e5),
        name="prepare_own",
    )(labels, qkv_after)

    residual_in, _ = lax.optimization_barrier((residual_in, first_chunk))
    blocks = own_tiles // 2
    residual = pl.pallas_call(
        reorder_residual,
        grid=(blocks,),
        in_specs=[
            pl.BlockSpec((2 * TILE, 2 * TILE), lambda i: (0, 0)),
            pl.BlockSpec((width, TILE), lambda i: (0, pair_tile(i, 0))),
            pl.BlockSpec((width, TILE), lambda i: (0, pair_tile(i, 1))),
        ],
        out_specs=pl.BlockSpec((1, width, 2 * TILE), lambda i: (i, 0, 0)),
        out_shape=jax.ShapeDtypeStruct((blocks, width, 2 * TILE), BF),
        compiler_params=params(16),
        cost_estimate=cost(2e9, 1e5),
        name="reorder_residual",
    )(perm, residual_in, residual_in)
    residual = lax.all_gather(residual, "col", axis=0)
    out_weight_t = jnp.transpose(out_weight)
    key_bounds = jnp.stack([low, high])
    gain = merge_gain[:, None]
    bits = []
    span = cols // 2
    while span:
        bits.append(span)
        span //= 2
    order = [0]
    for bit in bits:
        order = order + [bit ^ other for other in order]
    col_value = col_id.astype(jnp.int32).reshape(1)

    layers, parts, gathers = [], [], []
    any_spec = pl.BlockSpec(memory_space=pl.ANY)
    smem_spec = pl.BlockSpec(memory_space=pltpu.SMEM)
    vmem_spec = pl.BlockSpec(memory_space=pltpu.VMEM)
    def spread_pieces(stage, some_bits, after):
        pieces = gathers[stage]
        for bit in some_bits:
            pairs = [(i, i ^ bit) for i in range(cols)]
            sources = pieces
            if after is not None:
                sources, _ = lax.optimization_barrier((pieces, after))
            pieces = pieces + [lax.ppermute(piece, "col", pairs) for piece in sources]
        gathers[stage] = pieces

    def run_project(stage):
        size = plan[stage]
        paired = stage == stages - 1 and stages - 1 > 1
        last = stage == 0 or stage == stages - 1
        before = [parts[stage - 1]] if paired else []
        columns = 2 * size * TILE
        after = [gathers[-1][0]] if stage == 0 else [layers[stage - 1]]
        layer, part = pl.pallas_call(
            functools.partial(project, order, last, paired),
            grid=(1,),
            in_specs=[
                smem_spec,
                vmem_spec,
                vmem_spec,
                pl.BlockSpec(
                    (cols, size, width, 2 * TILE),
                    functools.partial(lambda s, i: (0, s, 0, 0), begins[stage] // size),
                ),
                any_spec,
                any_spec,
            ]
            + [any_spec] * cols
            + [vmem_spec] * paired
            + [any_spec] * len(after),
            out_specs=[vmem_spec, vmem_spec],
            out_shape=[
                jax.ShapeDtypeStruct((width, columns), BF),
                jax.ShapeDtypeStruct(
                    (width, (size + paired) * TILE // 2) if last else (full, columns), BF
                ),
            ],
            scratch_shapes=[
                pltpu.VMEM((full, columns), BF),
                pltpu.VMEM((full, columns), BF),
                pltpu.VMEM((full, full), BF),
                pltpu.VMEM((width, 4 * full), BF),
                pltpu.SemaphoreType.DMA((cols,)),
                pltpu.SemaphoreType.DMA((cols,)),
                pltpu.SemaphoreType.DMA((1,)),
            ],
            compiler_params=params(62),
            cost_estimate=cost((4 + 4 * size) * 1e9, 1e5),
            name="project",
        )(col_value, perm, gain, residual, out_weight_t, merge_weight, *gathers[stage], *before, *after)
        layers.append(layer)
        parts.append(part)

    for stage in range(stages):
        if stage + 1 < stages:
            send_chunk(stage + 1, (lefts[stage], rights[stage]))
        size, near = plan[stage], begins[stage]
        own = list(range(far_tiles, far_tiles + own_tiles))
        base_tile = far_tiles - near - size
        tiles = own_tiles + 2 * (near + size)
        halos, chunks = [], []
        for before in range(stage + 1):
            inner_edge, outer_edge = begins[before], begins[before] + plan[before]
            halos.append(list(range(far_tiles - outer_edge, far_tiles - inner_edge)))
            halos.append([far_tiles + own_tiles + at for at in range(inner_edge, outer_edge)])
            chunks += [lefts[before], rights[before]]
        queries = [pair_tile(block, which) for block in range(near, near + size) for which in range(2)]
        q_spec = lambda tile: pl.BlockSpec((1, heads, depth, TILE), lambda i: (tile, 0, 0, 0))
        after = [out_weight_t] if stage == 0 else [gathers[stage - 1][0]]
        attended = pl.pallas_call(
            functools.partial(attend, own, halos, images, base_tile, rate, queries),
            grid=(1,),
            in_specs=[smem_spec, vmem_spec, vmem_spec]
            + [q_spec(tile) for tile in queries]
            + [any_spec] * (2 + len(chunks) + len(after)),
            out_specs=vmem_spec,
            out_shape=jax.ShapeDtypeStruct((width, 2 * size * TILE), BF),
            scratch_shapes=[
                pltpu.VMEM((tiles,) + kt_shape, BF),
                pltpu.VMEM((tiles,) + v_shape, BF),
                pltpu.VMEM((2 * far_tiles + 1, heads, TILE, TILE), F32),
                pltpu.VMEM((heads, HEAD_DIM + 8, TILE), F32),
                pltpu.VMEM((heads, 8, TILE), F32),
                pltpu.VMEM((width, 2 * size * TILE), BF),
            ]
            + [pltpu.VMEM(chunk.shape, BF) for chunk in chunks]
            + [pltpu.SemaphoreType.DMA((len(chunks),)), pltpu.SemaphoreType.DMA((2,))],
            compiler_params=params(62),
            cost_estimate=cost((5 + 4 * size) * 1e9, 1e5),
            name="attend",
        )(key_bounds, labels, perm, *([q_tiles] * len(queries)), kt_own, v_own, *chunks, *after)

        gathers.append([attended])
        spread_pieces(stage, bits[:1], None)
        if stage >= 1:
            spread_pieces(stage - 1, bits[1:], attended)
    for stage in range(stages):
        if stage == 1:
            spread_pieces(stages - 1, bits[1:], layers[0])
        run_project(stage)

    tiles_out = [None] * own_tiles
    for stage in range(stages):
        for block in range(plan[stage]):
            for which in range(2):
                lane = (2 * block + which) * TILE
                tile = pair_tile(begins[stage] + block, which)
                tiles_out[tile] = layers[stage][:, lane : lane + TILE]
    layer_out = jnp.concatenate(tiles_out, axis=1)

    groups = tokens // 4
    share = groups // rows
    piece_groups = TILE // 4
    owner = dest_row // groups
    place = dest_row % groups
    index = jnp.arange(groups, dtype=jnp.int32)
    rank = jnp.sum(
        ((owner[:, None] == owner[None, :]) & (index[None, :] < index[:, None])).astype(jnp.int32),
        axis=1,
    )
    base = 32
    away = (owner - row_id) % rows
    info = jnp.stack([away * share + rank, place // base, place % base])
    info = info.reshape(3, own_tiles, piece_groups)
    halves = 2
    info = jnp.stack(
        [
            jnp.concatenate(
                [
                    info[:, pair_tile(block, which)]
                    for block in range(h * blocks // 2, (h + 1) * blocks // 2)
                    for which in range(2)
                ],
                axis=1,
            )
            for h in range(halves)
        ],
        axis=1,
    )
    slots = info[0][:, None, :]
    wide = round_up(width + 2, 128)
    places = jnp.concatenate(
        [
            jnp.stack([info[1], info[2]], axis=1).astype(BF),
            jnp.zeros((halves, wide - width - 2, 4 * piece_groups), BF),
        ],
        axis=1,
    )
    sent = pl.pallas_call(
        functools.partial(outgoing, rows),
        out_shape=[jax.ShapeDtypeStruct((share, wide), BF)] * rows,
        compiler_params=params(16),
        cost_estimate=cost(1e9, 1e5),
        name="outgoing",
    )(slots, places, parts[0], parts[-1])
    received = [sent[0]] + [
        lax.ppermute(sent[step], "row", [(i, (i + step) % rows) for i in range(rows)])
        for step in range(1, rows)
    ]
    image_rows = pl.pallas_call(
        functools.partial(incoming, width, base),
        out_shape=jax.ShapeDtypeStruct((width, groups), BF),
        compiler_params=params(16),
        cost_estimate=cost(1e9, 1e5),
        name="incoming",
    )(*received)
    return (layer_out, image_rows)


def solution(mesh):
    return jax.shard_map(
        body,
        mesh=mesh,
        in_specs=(P(None, "col", "row"), P("col", "row"), P(), P("col", None), P(), P(), P("row")),
        out_specs=(P("col", "row"), P("col", "row")),
        check_vma=False,
    )
```

profile of v0, /device:TPU:0, one launch (start us, length us, event | category | flops | bytes accessed | tf_op | source)
XLA Modules:
  0.0 161.2 jit_solution(1502641799572782612)
XLA Ops:
  7.2 0.0 all-gather.3.cloned.1.call-start
  7.2 0.0 copy-start.3
  7.2 1.5 fusion.24
  8.8 0.2 fusion.perm_ref
  8.9 0.1 copy-done.3
  9.0 2.7 %reorder_residual.1 = bf16[4,352,512]{2,1,0:T(8,128)(2,1)} custom-call(bf16[512,512]{1,0:T(8,128)(2,1)S(1)} %fusion.perm_ref, bf16[352,2048]{1,0:T(8,128)(2,1)S(1)} %copy-done.3, bf16[352,2048]{1,0:T(8,128)(2,1)S(1)} %copy-done.3), custom_call_target="tpu_custom_call" | custom-call | flops 2000000000 | bytes 100000 | tf_op jit(solution)/shard_map/reorder_residual/pallas_call | solution.py:333
  11.8 0.0 all-gather.3.cloned.1.call-update
  11.8 3.0 %collective-permute-start = (bf16[2,352,512]{2,1,0:T(8,128)(2,1)S(1)}, bf16[2,352,512]{2,1,0:T(8,128)(2,1)S(1)}, u32[]{:S(2)}, u32[]{:S(2)}) collective-permute-start(bf16[2,352,512]{2,1,0:T(8,128)(2,1)S(1)} %get-tuple-element.63), channel_id=1, source_target_pairs={{0,4},{4,8},{8,12},{12,16},{16,20},{20,24},{24,28},{28,0},{1,5},{5... | collective-permute-start | bytes 2162696 | tf_op jit(solution)/shard_map/ppermute | solution.py:271
  14.8 3.1 %collective-permute-start.1 = (bf16[2,352,512]{2,1,0:T(8,128)(2,1)S(1)}, bf16[2,352,512]{2,1,0:T(8,128)(2,1)}, u32[]{:S(2)}, u32[]{:S(2)}) collective-permute-start(bf16[2,352,512]{2,1,0:T(8,128)(2,1)S(1)} %get-tuple-element.62), channel_id=1, source_target_pairs={{4,0},{8,4},{12,8},{16,12},{20,16},{24,20},{28,24},{0,28},{5,1},{9... | collective-permute-start | bytes 2162696 | tf_op jit(solution)/shard_map/ppermute | solution.py:272
  17.9 0.1 copy.37
  18.0 6.4 %copy.36 = bf16[1408,1408]{0,1:T(8,128)(2,1)} copy(bf16[1408,1408]{1,0:T(8,128)(2,1)} %param.9) | data formatting | bytes 7929856 | tf_op args[2]
  24.4 1.1 broadcast_in_dim.42.gain_ref
  25.5 0.2 convert_reduce_fusion
  25.8 0.1 stack.31
  25.9 0.1 stack.32
  25.9 0.1 stack.33
  26.0 0.1 reduce-window.8
  26.1 0.1 add_bitcast_fusion
  26.2 0.1 multiply_reduce_fusion
  26.4 0.2 select_reduce_fusion.1
  26.6 0.6 pad_add_fusion.2.bounds
  27.2 0.1 convert_reduce_fusion.1
  27.4 0.0 copy-start
  27.4 2.2 %copy-done = bf16[3,352,2048]{2,1,0:T(8,128)(2,1)S(1)} copy-done((bf16[3,352,2048]{2,1,0:T(8,128)(2,1)S(1)}, bf16[3,352,2048]{2,1,0:T(8,128)(2,1)}, u32[]{:S(2)}) %copy-start) | copy-done | bytes 4325400
  29.7 1.8 %prepare_own.1 = (bf16[8,4,128,256]{3,2,1,0:T(8,128)(2,1)S(1)}, bf16[8,4,256,128]{3,2,1,0:T(8,128)(2,1)S(1)}, bf16[8,4,96,256]{3,2,1,0:T(8,128)(2,1)S(1)}) custom-call(s32[16,1,256]{2,1,0:T(1,128)S(1)} %compare_select_fusion.label_ref, bf16[3,352,2048]{2,1,0:T(8,128)(2,1)S(1)} %copy-done), custom_call_target="tpu_custom_call" | custom-call | flops 2000000000 | bytes 100000 | tf_op jit(solution)/shard_map/prepare_own/pallas_call | solution.py:309
  31.5 1.3 copy-done.4
  32.8 1.4 copy-done.5
  34.2 1.2 copy-done.6
  35.3 10.3 %collective-permute-done.refs_6_.refs_4_ = bf16[2,352,512]{2,1,0:T(8,128)(2,1)S(1)} collective-permute-done((bf16[2,352,512]{2,1,0:T(8,128)(2,1)S(1)}, bf16[2,352,512]{2,1,0:T(8,128)(2,1)S(1)}, u32[]{:S(2)}, u32[]{:S(2)}) %collective-permute-start) | collective-permute-done | bytes 720928 | tf_op jit(solution)/shard_map/ppermute | solution.py:271
  45.6 2.3 %collective-permute-done.1.refs_7_.refs_5_ = bf16[2,352,512]{2,1,0:T(8,128)(2,1)} collective-permute-done((bf16[2,352,512]{2,1,0:T(8,128)(2,1)S(1)}, bf16[2,352,512]{2,1,0:T(8,128)(2,1)}, u32[]{:S(2)}, u32[]{:S(2)}) %collective-permute-start.1) | collective-permute-done | bytes 720928 | tf_op jit(solution)/shard_map/ppermute | solution.py:272
  47.9 0.1 fusion.23
  48.0 0.2 collective-permute-start.2
  48.2 4.5 %collective-permute-start.3 = (bf16[2,352,256]{2,1,0:T(8,128)(2,1)S(1)}, bf16[2,352,256]{2,1,0:T(8,128)(2,1)}, u32[]{:S(2)}, u32[]{:S(2)}) collective-permute-start(bf16[2,352,256]{2,1,0:T(8,128)(2,1)S(1)} %get-tuple-element.60), channel_id=1, source_target_pairs={{4,0},{8,4},{12,8},{16,12},{20,16},{24,20},{28,24},{0,28},{5,1},{9... | collective-permute-start | bytes 1081352 | tf_op jit(solution)/shard_map/ppermute | solution.py:272
  52.8 13.4 %attend.3.refs_8_.refs_0_ = bf16[352,1024]{1,0:T(8,128)(2,1)} custom-call(s32[2,8]{1,0:T(2,128)} %pad_add_fusion.2.bounds, s32[16,1,256]{2,1,0:T(1,128)} %copy-done.2, bf16[512,512]{1,0:T(8,128)(2,1)} %copy-done.1, bf16[8,4,128,256]{3,2,1,0:T(8,128)(2,1)} %copy-done.4, bf16[8,4,128,256]{3,2,1,0:T(8,128)(2,1)} %copy-done.4, ...), custom_call_target="tpu_custom_call" | custom-call | flops 12999999488 | bytes 100000 | tf_op jit(solution)/shard_map/attend/pallas_call | solution.py:438
  66.2 1.5 collective-permute-start.7
  67.8 1.3 fusion.22
  69.1 0.1 collective-permute-start.4
  69.2 4.6 %collective-permute-start.5 = (bf16[2,352,256]{2,1,0:T(8,128)(2,1)S(1)}, bf16[2,352,256]{2,1,0:T(8,128)(2,1)}, u32[]{:S(2)}, u32[]{:S(2)}) collective-permute-start(bf16[2,352,256]{2,1,0:T(8,128)(2,1)S(1)} %get-tuple-element.58), channel_id=1, source_target_pairs={{4,0},{8,4},{12,8},{16,12},{20,16},{24,20},{28,24},{0,28},{5,1},{9... | collective-permute-start | bytes 1081352 | tf_op jit(solution)/shard_map/ppermute | solution.py:272
  73.8 8.5 %attend.4.refs_10_.refs_0_ = bf16[352,512]{1,0:T(8,128)(2,1)} custom-call(s32[2,8]{1,0:T(2,128)} %pad_add_fusion.2.bounds, s32[16,1,256]{2,1,0:T(1,128)} %copy-done.2, bf16[512,512]{1,0:T(8,128)(2,1)} %copy-done.1, bf16[8,4,128,256]{3,2,1,0:T(8,128)(2,1)} %copy-done.4, bf16[8,4,128,256]{3,2,1,0:T(8,128)(2,1)} %copy-done.4, ...), custom_call_target="tpu_custom_call" | custom-call | flops 8999999488 | bytes 100000 | tf_op jit(solution)/shard_map/attend/pallas_call | solution.py:438
  82.4 0.6 collective-permute-start.12
  83.0 0.5 collective-permute-start.9
  83.5 0.7 collective-permute-done.4.refs_8_
  84.2 3.0 %collective-permute-done.5.refs_9_ = bf16[2,352,256]{2,1,0:T(8,128)(2,1)} collective-permute-done((bf16[2,352,256]{2,1,0:T(8,128)(2,1)S(1)}, bf16[2,352,256]{2,1,0:T(8,128)(2,1)}, u32[]{:S(2)}, u32[]{:S(2)}) %collective-permute-start.5) | collective-permute-done | bytes 360480 | tf_op jit(solution)/shard_map/ppermute | solution.py:272
  87.2 7.7 %attend.5.refs_4_.refs_0_ = bf16[352,512]{1,0:T(8,128)(2,1)} custom-call(s32[2,8]{1,0:T(2,128)} %pad_add_fusion.2.bounds, s32[16,1,256]{2,1,0:T(1,128)} %copy-done.2, bf16[512,512]{1,0:T(8,128)(2,1)} %copy-done.1, bf16[8,4,128,256]{3,2,1,0:T(8,128)(2,1)} %copy-done.4, bf16[8,4,128,256]{3,2,1,0:T(8,128)(2,1)} %copy-done.4, ...), custom_call_target="tpu_custom_call" | custom-call | flops 8999999488 | bytes 100000 | tf_op jit(solution)/shard_map/attend/pallas_call | solution.py:438
  94.9 1.6 collective-permute-start.6
  96.4 0.5 collective-permute-start.14
  97.0 15.3 %project.3 = (bf16[352,1024]{1,0:T(8,128)(2,1)}, bf16[352,256]{1,0:T(8,128)(2,1)}) custom-call(s32[1]{0:T(128)} %bitcast.col_ref, bf16[512,512]{1,0:T(8,128)(2,1)} %copy-done.1, f32[1408,1]{1,0:T(8,128)} %broadcast_in_dim.42.gain_ref, bf16[4,4,352,512]{3,2,1,0:T(8,128)(2,1)} %bitcast.57, bf16[1408,1408]{1,0:T(8,128)(2,1)} %bitcast.52, ...), custom_call_target="tpu_custom_call" | custom-call | flops 12000000000 | bytes 100000 | tf_op jit(solution)/shard_map/project/pallas_call | solution.py:382
  112.3 0.1 collective-permute-start.10
  112.4 0.4 collective-permute-start.11
  112.9 9.4 %project.4 = (bf16[352,512]{1,0:T(8,128)(2,1)}, bf16[1408,512]{1,0:T(8,128)(2,1)}) custom-call(s32[1]{0:T(128)} %bitcast.col_ref, bf16[512,512]{1,0:T(8,128)(2,1)} %copy-done.1, f32[1408,1]{1,0:T(8,128)} %broadcast_in_dim.42.gain_ref, bf16[4,4,352,512]{3,2,1,0:T(8,128)(2,1)} %bitcast.58, bf16[1408,1408]{1,0:T(8,128)(2,1)} %bitcast.53, ...), custom_call_target="tpu_custom_call" | custom-call | flops 8000000000 | bytes 100000 | tf_op jit(solution)/shard_map/project/pallas_call | solution.py:382
  122.3 0.0 copy-start.21
  122.3 0.7 copy-done.21
  123.0 0.1 copy-done.22
  123.2 12.6 %project.5 = (bf16[352,512]{1,0:T(8,128)(2,1)}, bf16[352,256]{1,0:T(8,128)(2,1)}) custom-call(s32[1]{0:T(128)} %bitcast.col_ref, bf16[512,512]{1,0:T(8,128)(2,1)} %copy-done.1, f32[1408,1]{1,0:T(8,128)} %broadcast_in_dim.42.gain_ref, bf16[4,4,352,512]{3,2,1,0:T(8,128)(2,1)} %bitcast.59, bf16[1408,1408]{1,0:T(8,128)(2,1)} %bitcast.54, ...), custom_call_target="tpu_custom_call" | custom-call | flops 8000000000 | bytes 100000 | tf_op jit(solution)/shard_map/project/pallas_call | solution.py:382
  135.8 0.9 copy-done.8
  136.7 0.5 outgoing.1
  137.1 3.1 %collective-permute-start.15 = (bf16[64,384]{1,0:T(8,128)(2,1)S(1)}, bf16[64,384]{1,0:T(8,128)(2,1)S(1)}, u32[]{:S(2)}, u32[]{:S(2)}) collective-permute-start(bf16[64,384]{1,0:T(8,128)(2,1)S(1)} %get-tuple-element.49), channel_id=1, source_target_pairs={{0,4},{4,8},{8,12},{12,16},{16,20},{20,24},{24,28},{28,0},{1,5},{5... | collective-permute-start | bytes 147464 | tf_op jit(solution)/shard_map/ppermute | solution.py:525
  140.2 2.7 %collective-permute-start.17 = (bf16[64,384]{1,0:T(8,128)(2,1)S(1)}, bf16[64,384]{1,0:T(8,128)(2,1)S(1)}, u32[]{:S(2)}, u32[]{:S(2)}) collective-permute-start(bf16[64,384]{1,0:T(8,128)(2,1)S(1)} %get-tuple-element.51), channel_id=1, source_target_pairs={{0,12},{4,16},{8,20},{12,24},{16,28},{20,0},{24,4},{28,8},{1,13},{... | collective-permute-start | bytes 147464 | tf_op jit(solution)/shard_map/ppermute | solution.py:525
  142.9 2.3 %collective-permute-start.18 = (bf16[64,384]{1,0:T(8,128)(2,1)S(1)}, bf16[64,384]{1,0:T(8,128)(2,1)S(1)}, u32[]{:S(2)}, u32[]{:S(2)}) collective-permute-start(bf16[64,384]{1,0:T(8,128)(2,1)S(1)} %get-tuple-element.52), channel_id=1, source_target_pairs={{0,16},{4,20},{8,24},{12,28},{16,0},{20,4},{24,8},{28,12},{1,17},{... | collective-permute-start | bytes 147464 | tf_op jit(solution)/shard_map/ppermute | solution.py:525
  145.1 0.7 collective-permute-start.19
  145.9 2.5 %collective-permute-start.20 = (bf16[64,384]{1,0:T(8,128)(2,1)S(1)}, bf16[64,384]{1,0:T(8,128)(2,1)S(1)}, u32[]{:S(2)}, u32[]{:S(2)}) collective-permute-start(bf16[64,384]{1,0:T(8,128)(2,1)S(1)} %get-tuple-element.54), channel_id=1, source_target_pairs={{0,24},{4,28},{8,0},{12,4},{16,8},{20,12},{24,16},{28,20},{1,25},{... | collective-permute-start | bytes 147464 | tf_op jit(solution)/shard_map/ppermute | solution.py:525
  148.4 2.8 %collective-permute-start.21 = (bf16[64,384]{1,0:T(8,128)(2,1)S(1)}, bf16[64,384]{1,0:T(8,128)(2,1)S(1)}, u32[]{:S(2)}, u32[]{:S(2)}) collective-permute-start(bf16[64,384]{1,0:T(8,128)(2,1)S(1)} %get-tuple-element.55), channel_id=1, source_target_pairs={{0,28},{4,0},{8,4},{12,8},{16,12},{20,16},{24,20},{28,24},{1,29},{... | collective-permute-start | bytes 147464 | tf_op jit(solution)/shard_map/ppermute | solution.py:525
  151.3 1.7 %collective-permute-done.21.refs_7_ = bf16[64,384]{1,0:T(8,128)(2,1)S(1)} collective-permute-done((bf16[64,384]{1,0:T(8,128)(2,1)S(1)}, bf16[64,384]{1,0:T(8,128)(2,1)S(1)}, u32[]{:S(2)}, u32[]{:S(2)}) %collective-permute-start.21) | collective-permute-done | bytes 49184 | tf_op jit(solution)/shard_map/ppermute | solution.py:525
  153.0 1.3 incoming.1
  (75 shorter events, 0.4 us)
Async XLA Ops:
  7.2 89.8 %all-gather.3.cloned.1.call-start = ((), (), s32[]{:S(2)}) async-start(), calls=%async_computation | async-start | bytes 7208960 | tf_op jit(solution)/shard_map/all_gather | solution.py:347
  7.2 1.8 %copy-start.3 = (bf16[352,2048]{1,0:T(8,128)(2,1)S(1)}, bf16[352,2048]{1,0:T(8,128)(2,1)}, u32[]{:S(2)}) copy-start(bf16[352,2048]{1,0:T(8,128)(2,1)} %high_ref) | copy-start | bytes 4325380
  8.9 2.8 %copy-start.1 = (bf16[512,512]{1,0:T(8,128)(2,1)}, bf16[512,512]{1,0:T(8,128)(2,1)S(1)}, u32[]{:S(2)}) copy-start(bf16[512,512]{1,0:T(8,128)(2,1)S(1)} %fusion.perm_ref) | copy-start | bytes 1572868
  11.7 6.1 %copy-start.15 = (s32[32]{0:T(128)S(1)}, s32[32]{0:T(128)}, u32[]{:S(2)}) copy-start(s32[32]{0:T(128)} %param.12) | copy-start | bytes 388
  11.8 33.8 %collective-permute-start = (bf16[2,352,512]{2,1,0:T(8,128)(2,1)S(1)}, bf16[2,352,512]{2,1,0:T(8,128)(2,1)S(1)}, u32[]{:S(2)}, u32[]{:S(2)}) collective-permute-start(bf16[2,352,512]{2,1,0:T(8,128)(2,1)S(1)} %get-tuple-element.63), channel_id=1, source_target_pairs={{0,4},{4,8},{8,12},{12,16},{16,20},{20,24},{24,28},{28,0},{1,5},{5... | collective-permute-start | bytes 2162696 | tf_op jit(solution)/shard_map/ppermute | solution.py:271
  14.8 33.2 %collective-permute-start.1 = (bf16[2,352,512]{2,1,0:T(8,128)(2,1)S(1)}, bf16[2,352,512]{2,1,0:T(8,128)(2,1)}, u32[]{:S(2)}, u32[]{:S(2)}) collective-permute-start(bf16[2,352,512]{2,1,0:T(8,128)(2,1)S(1)} %get-tuple-element.62), channel_id=1, source_target_pairs={{4,0},{8,4},{12,8},{16,12},{20,16},{24,20},{28,24},{0,28},{5,1},{9... | collective-permute-start | bytes 2162696 | tf_op jit(solution)/shard_map/ppermute | solution.py:272
  18.0 6.4 %copy-start.13 = (f32[1408]{0:T(1024)S(1)}, f32[1408]{0:T(1024)}, u32[]{:S(2)}) copy-start(f32[1408]{0:T(1024)} %param.11) | copy-start | bytes 16900
  18.0 7.5 %copy-start.14 = (s32[512]{0:T(512)S(1)}, s32[512]{0:T(512)}, u32[]{:S(2)}) copy-start(s32[512]{0:T(512)} %param.13) | copy-start | bytes 6148
  27.4 2.2 %copy-start = (bf16[3,352,2048]{2,1,0:T(8,128)(2,1)S(1)}, bf16[3,352,2048]{2,1,0:T(8,128)(2,1)}, u32[]{:S(2)}) copy-start(bf16[3,352,2048]{2,1,0:T(8,128)(2,1)} %qkv_ref) | copy-start | bytes 12976132
  29.7 1.8 %copy-start.2 = (s32[16,1,256]{2,1,0:T(1,128)}, s32[16,1,256]{2,1,0:T(1,128)S(1)}, u32[]{:S(2)}) copy-start(s32[16,1,256]{2,1,0:T(1,128)S(1)} %compare_select_fusion.label_ref) | copy-start | bytes 49156
  31.5 1.3 copy-start.4
  32.8 1.4 copy-start.5
  34.2 1.2 copy-start.6
  45.6 7.1 %copy-start.16 = (bf16[2,352,512]{2,1,0:T(8,128)(2,1)}, bf16[2,352,512]{2,1,0:T(8,128)(2,1)S(1)}, u32[]{:S(2)}) copy-start(bf16[2,352,512]{2,1,0:T(8,128)(2,1)S(1)} %collective-permute-done.refs_6_.refs_4_) | copy-start | bytes 2162692
  48.0 19.8 %collective-permute-start.2 = (bf16[2,352,256]{2,1,0:T(8,128)(2,1)S(1)}, bf16[2,352,256]{2,1,0:T(8,128)(2,1)S(1)}, u32[]{:S(2)}, u32[]{:S(2)}) collective-permute-start(bf16[2,352,256]{2,1,0:T(8,128)(2,1)S(1)} %get-tuple-element.61), channel_id=1, source_target_pairs={{0,4},{4,8},{8,12},{12,16},{16,20},{20,24},{24,28},{28,0},{1,5},{5... | collective-permute-start | bytes 1081352 | tf_op jit(solution)/shard_map/ppermute | solution.py:271
  48.2 19.6 %collective-permute-start.3 = (bf16[2,352,256]{2,1,0:T(8,128)(2,1)S(1)}, bf16[2,352,256]{2,1,0:T(8,128)(2,1)}, u32[]{:S(2)}, u32[]{:S(2)}) collective-permute-start(bf16[2,352,256]{2,1,0:T(8,128)(2,1)S(1)} %get-tuple-element.60), channel_id=1, source_target_pairs={{4,0},{8,4},{12,8},{16,12},{20,16},{24,20},{28,24},{0,28},{5,1},{9... | collective-permute-start | bytes 1081352 | tf_op jit(solution)/shard_map/ppermute | solution.py:272
  66.2 16.8 %collective-permute-start.7 = (bf16[352,1024]{1,0:T(8,128)(2,1)}, bf16[352,1024]{1,0:T(8,128)(2,1)}, u32[]{:S(2)}, u32[]{:S(2)}) collective-permute-start(bf16[352,1024]{1,0:T(8,128)(2,1)} %attend.3.refs_8_.refs_0_), channel_id=1, source_target_pairs={{0,2},{1,3},{2,0},{3,1},{4,6},{5,7},{6,4},{7,5},{8,10},{9,11},{10,... | collective-permute-start | bytes 2162696 | tf_op jit(solution)/shard_map/ppermute | solution.py:372
  67.8 6.1 %copy-start.20 = (bf16[2,352,256]{2,1,0:T(8,128)(2,1)}, bf16[2,352,256]{2,1,0:T(8,128)(2,1)S(1)}, u32[]{:S(2)}) copy-start(bf16[2,352,256]{2,1,0:T(8,128)(2,1)S(1)} %collective-permute-done.2.refs_6_) | copy-start | bytes 1081348
  69.1 15.2 %collective-permute-start.4 = (bf16[2,352,256]{2,1,0:T(8,128)(2,1)S(1)}, bf16[2,352,256]{2,1,0:T(8,128)(2,1)}, u32[]{:S(2)}, u32[]{:S(2)}) collective-permute-start(bf16[2,352,256]{2,1,0:T(8,128)(2,1)S(1)} %get-tuple-element.59), channel_id=1, source_target_pairs={{0,4},{4,8},{8,12},{12,16},{16,20},{20,24},{24,28},{28,0},{1,5},{5... | collective-permute-start | bytes 1081352 | tf_op jit(solution)/shard_map/ppermute | solution.py:271
  69.2 13.8 %copy-start.17 = (bf16[352,1024]{1,0:T(8,128)(2,1)S(1)}, bf16[352,1024]{1,0:T(8,128)(2,1)}, u32[]{:S(2)}) copy-start(bf16[352,1024]{1,0:T(8,128)(2,1)} %attend.3.refs_8_.refs_0_) | copy-start | bytes 2162692
  69.2 18.0 %collective-permute-start.5 = (bf16[2,352,256]{2,1,0:T(8,128)(2,1)S(1)}, bf16[2,352,256]{2,1,0:T(8,128)(2,1)}, u32[]{:S(2)}, u32[]{:S(2)}) collective-permute-start(bf16[2,352,256]{2,1,0:T(8,128)(2,1)S(1)} %get-tuple-element.58), channel_id=1, source_target_pairs={{4,0},{8,4},{12,8},{16,12},{20,16},{24,20},{28,24},{0,28},{5,1},{9... | collective-permute-start | bytes 1081352 | tf_op jit(solution)/shard_map/ppermute | solution.py:272
  82.4 14.1 %copy-start.18 = (bf16[352,512]{1,0:T(8,128)(2,1)S(1)}, bf16[352,512]{1,0:T(8,128)(2,1)}, u32[]{:S(2)}) copy-start(bf16[352,512]{1,0:T(8,128)(2,1)} %attend.4.refs_10_.refs_0_) | copy-start | bytes 1081348
  82.4 14.1 %collective-permute-start.12 = (bf16[352,512]{1,0:T(8,128)(2,1)}, bf16[352,512]{1,0:T(8,128)(2,1)}, u32[]{:S(2)}, u32[]{:S(2)}) collective-permute-start(bf16[352,512]{1,0:T(8,128)(2,1)} %attend.4.refs_10_.refs_0_), channel_id=1, source_target_pairs={{0,2},{1,3},{2,0},{3,1},{4,6},{5,7},{6,4},{7,5},{8,10},{9,11},{10,... | collective-permute-start | bytes 1081352 | tf_op jit(solution)/shard_map/ppermute | solution.py:372
  83.0 14.0 %collective-permute-start.8 = (bf16[352,1024]{1,0:T(8,128)(2,1)S(1)}, bf16[352,1024]{1,0:T(8,128)(2,1)}, u32[]{:S(2)}, u32[]{:S(2)}) collective-permute-start(bf16[352,1024]{1,0:T(8,128)(2,1)S(1)} %copy-done.17), channel_id=1, source_target_pairs={{0,1},{1,0},{2,3},{3,2},{4,5},{5,4},{6,7},{7,6},{8,9},{9,8},{10,11... | collective-permute-start | bytes 2162696 | tf_op jit(solution)/shard_map/ppermute | solution.py:372
  83.0 14.0 %collective-permute-start.9 = (bf16[352,1024]{1,0:T(8,128)(2,1)}, bf16[352,1024]{1,0:T(8,128)(2,1)}, u32[]{:S(2)}, u32[]{:S(2)}) collective-permute-start(bf16[352,1024]{1,0:T(8,128)(2,1)} %collective-permute-done.7.refs_1_), channel_id=1, source_target_pairs={{0,1},{1,0},{2,3},{3,2},{4,5},{5,4},{6,7},{7,6},{8,9},{9,8},{10,11... | collective-permute-start | bytes 2162696 | tf_op jit(solution)/shard_map/ppermute | solution.py:372
  94.9 17.4 %collective-permute-start.6 = (bf16[352,512]{1,0:T(8,128)(2,1)}, bf16[352,512]{1,0:T(8,128)(2,1)}, u32[]{:S(2)}, u32[]{:S(2)}) collective-permute-start(bf16[352,512]{1,0:T(8,128)(2,1)} %attend.5.refs_4_.refs_0_), channel_id=1, source_target_pairs={{0,2},{1,3},{2,0},{3,1},{4,6},{5,7},{6,4},{7,5},{8,10},{9,11},{10,... | collective-permute-start | bytes 1081352 | tf_op jit(solution)/shard_map/ppermute | solution.py:372
  96.4 16.4 %collective-permute-start.13 = (bf16[352,512]{1,0:T(8,128)(2,1)S(1)}, bf16[352,512]{1,0:T(8,128)(2,1)}, u32[]{:S(2)}, u32[]{:S(2)}) collective-permute-start(bf16[352,512]{1,0:T(8,128)(2,1)S(1)} %copy-done.18), channel_id=1, source_target_pairs={{0,1},{1,0},{2,3},{3,2},{4,5},{5,4},{6,7},{7,6},{8,9},{9,8},{10,11... | collective-permute-start | bytes 1081352 | tf_op jit(solution)/shard_map/ppermute | solution.py:372
  96.4 16.4 %collective-permute-start.14 = (bf16[352,512]{1,0:T(8,128)(2,1)}, bf16[352,512]{1,0:T(8,128)(2,1)}, u32[]{:S(2)}, u32[]{:S(2)}) collective-permute-start(bf16[352,512]{1,0:T(8,128)(2,1)} %collective-permute-done.12.refs_1_), channel_id=1, source_target_pairs={{0,1},{1,0},{2,3},{3,2},{4,5},{5,4},{6,7},{7,6},{8,9},{9,8},{10,11... | collective-permute-start | bytes 1081352 | tf_op jit(solution)/shard_map/ppermute | solution.py:372
  97.0 15.3 %copy-start.19 = (bf16[352,512]{1,0:T(8,128)(2,1)S(1)}, bf16[352,512]{1,0:T(8,128)(2,1)}, u32[]{:S(2)}) copy-start(bf16[352,512]{1,0:T(8,128)(2,1)} %attend.5.refs_4_.refs_0_) | copy-start | bytes 1081348
  112.3 10.0 %collective-permute-start.10 = (bf16[352,512]{1,0:T(8,128)(2,1)S(1)}, bf16[352,512]{1,0:T(8,128)(2,1)S(1)}, u32[]{:S(2)}, u32[]{:S(2)}) collective-permute-start(bf16[352,512]{1,0:T(8,128)(2,1)S(1)} %copy-done.19), channel_id=1, source_target_pairs={{0,1},{1,0},{2,3},{3,2},{4,5},{5,4},{6,7},{7,6},{8,9},{9,8},{10,11... | collective-permute-start | bytes 1081352 | tf_op jit(solution)/shard_map/ppermute | solution.py:372
  112.4 9.9 %collective-permute-start.11 = (bf16[352,512]{1,0:T(8,128)(2,1)}, bf16[352,512]{1,0:T(8,128)(2,1)S(1)}, u32[]{:S(2)}, u32[]{:S(2)}) collective-permute-start(bf16[352,512]{1,0:T(8,128)(2,1)} %collective-permute-done.6.refs_1_), channel_id=1, source_target_pairs={{0,1},{1,0},{2,3},{3,2},{4,5},{5,4},{6,7},{7,6},{8,9},{9,8},{10,11... | collective-permute-start | bytes 1081352 | tf_op jit(solution)/shard_map/ppermute | solution.py:372
  122.3 0.7 copy-start.21
  122.3 0.8 copy-start.22
  123.2 12.6 %copy-start.7 = (bf16[352,256]{1,0:T(8,128)(2,1)S(1)}, bf16[352,256]{1,0:T(8,128)(2,1)}, u32[]{:S(2)}) copy-start(bf16[352,256]{1,0:T(8,128)(2,1)} %get-tuple-element.46.refs_0_) | copy-start | bytes 540676
  135.7 0.9 copy-start.8
  136.7 9.1 %copy-start.10 = (bf16[352,512]{1,0:T(8,128)(2,1)S(1)}, bf16[352,512]{1,0:T(8,128)(2,1)}, u32[]{:S(2)}) copy-start(bf16[352,512]{1,0:T(8,128)(2,1)} %get-tuple-element.45) | copy-start | bytes 1081348
  136.7 9.1 %copy-start.11 = (bf16[352,512]{1,0:T(8,128)(2,1)S(1)}, bf16[352,512]{1,0:T(8,128)(2,1)}, u32[]{:S(2)}) copy-start(bf16[352,512]{1,0:T(8,128)(2,1)} %get-tuple-element.44.refs_5_) | copy-start | bytes 1081348
  136.7 9.2 %copy-start.9 = (bf16[352,1024]{1,0:T(8,128)(2,1)S(1)}, bf16[352,1024]{1,0:T(8,128)(2,1)}, u32[]{:S(2)}) copy-start(bf16[352,1024]{1,0:T(8,128)(2,1)} %get-tuple-element.38.refs_4_) | copy-start | bytes 2162692
  137.1 8.8 %collective-permute-start.15 = (bf16[64,384]{1,0:T(8,128)(2,1)S(1)}, bf16[64,384]{1,0:T(8,128)(2,1)S(1)}, u32[]{:S(2)}, u32[]{:S(2)}) collective-permute-start(bf16[64,384]{1,0:T(8,128)(2,1)S(1)} %get-tuple-element.49), channel_id=1, source_target_pairs={{0,4},{4,8},{8,12},{12,16},{16,20},{20,24},{24,28},{28,0},{1,5},{5... | collective-permute-start | bytes 147464 | tf_op jit(solution)/shard_map/ppermute | solution.py:525
  140.2 8.2 %collective-permute-start.16 = (bf16[64,384]{1,0:T(8,128)(2,1)S(1)}, bf16[64,384]{1,0:T(8,128)(2,1)S(1)}, u32[]{:S(2)}, u32[]{:S(2)}) collective-permute-start(bf16[64,384]{1,0:T(8,128)(2,1)S(1)} %get-tuple-element.50), channel_id=1, source_target_pairs={{0,8},{4,12},{8,16},{12,20},{16,24},{20,28},{24,0},{28,4},{1,9},{5... | collective-permute-start | bytes 147464 | tf_op jit(solution)/shard_map/ppermute | solution.py:525
  140.2 11.1 %collective-permute-start.17 = (bf16[64,384]{1,0:T(8,128)(2,1)S(1)}, bf16[64,384]{1,0:T(8,128)(2,1)S(1)}, u32[]{:S(2)}, u32[]{:S(2)}) collective-permute-start(bf16[64,384]{1,0:T(8,128)(2,1)S(1)} %get-tuple-element.51), channel_id=1, source_target_pairs={{0,12},{4,16},{8,20},{12,24},{16,28},{20,0},{24,4},{28,8},{1,13},{... | collective-permute-start | bytes 147464 | tf_op jit(solution)/shard_map/ppermute | solution.py:525
  142.9 8.5 %collective-permute-start.18 = (bf16[64,384]{1,0:T(8,128)(2,1)S(1)}, bf16[64,384]{1,0:T(8,128)(2,1)S(1)}, u32[]{:S(2)}, u32[]{:S(2)}) collective-permute-start(bf16[64,384]{1,0:T(8,128)(2,1)S(1)} %get-tuple-element.52), channel_id=1, source_target_pairs={{0,16},{4,20},{8,24},{12,28},{16,0},{20,4},{24,8},{28,12},{1,17},{... | collective-permute-start | bytes 147464 | tf_op jit(solution)/shard_map/ppermute | solution.py:525
  145.1 6.2 %collective-permute-start.19 = (bf16[64,384]{1,0:T(8,128)(2,1)S(1)}, bf16[64,384]{1,0:T(8,128)(2,1)S(1)}, u32[]{:S(2)}, u32[]{:S(2)}) collective-permute-start(bf16[64,384]{1,0:T(8,128)(2,1)S(1)} %get-tuple-element.53), channel_id=1, source_target_pairs={{0,20},{4,24},{8,28},{12,0},{16,4},{20,8},{24,12},{28,16},{1,21},{... | collective-permute-start | bytes 147464 | tf_op jit(solution)/shard_map/ppermute | solution.py:525
  145.9 5.4 %collective-permute-start.20 = (bf16[64,384]{1,0:T(8,128)(2,1)S(1)}, bf16[64,384]{1,0:T(8,128)(2,1)S(1)}, u32[]{:S(2)}, u32[]{:S(2)}) collective-permute-start(bf16[64,384]{1,0:T(8,128)(2,1)S(1)} %get-tuple-element.54), channel_id=1, source_target_pairs={{0,24},{4,28},{8,0},{12,4},{16,8},{20,12},{24,16},{28,20},{1,25},{... | collective-permute-start | bytes 147464 | tf_op jit(solution)/shard_map/ppermute | solution.py:525
  148.4 4.6 %collective-permute-start.21 = (bf16[64,384]{1,0:T(8,128)(2,1)S(1)}, bf16[64,384]{1,0:T(8,128)(2,1)S(1)}, u32[]{:S(2)}, u32[]{:S(2)}) collective-permute-start(bf16[64,384]{1,0:T(8,128)(2,1)S(1)} %get-tuple-element.55), channel_id=1, source_target_pairs={{0,28},{4,0},{8,4},{12,8},{16,12},{20,16},{24,20},{28,24},{1,29},{... | collective-permute-start | bytes 147464 | tf_op jit(solution)/shard_map/ppermute | solution.py:525
  151.3 3.1 %copy-start.12 = (bf16[352,2048]{1,0:T(8,128)(2,1)}, bf16[352,2048]{1,0:T(8,128)(2,1)S(1)}, u32[]{:S(2)}) copy-start(bf16[352,2048]{1,0:T(8,128)(2,1)S(1)} %slice_dynamic-update-slice_fusion) | copy-start | bytes 4325380
Sparse Core Ops, SparseCore 0:
  11.9 46.0 all-gather.2
where the time goes:
time: 163 us; the launch traced here: 161 us
  Pallas kernels  73.2 us (45%)
  starting transfers between devices  35 us (21%)
  local copies, waits for them, and re-layouts  18.8 us (12%)
  waiting for transfers between devices  18 us (11%)
  between operations  14.4 us (9%)
  other arithmetic  1.76 us (1%)
    pallas_call x3, Pallas kernels, run_project(): pl.pallas_call(functools.partial(project, order, last, paired), grid=(1,)...  37.3 us
    pallas_call x3, Pallas kernels, body(): pl.pallas_call(functools.partial(attend, own, halos, images, base_tile, r...  29.6 us
    unnamed x51, local copies, waits for them, and re-layouts  14.4 us
    ppermute x7, starting transfers between devices, body(): lax.ppermute(sent[step], 'row', [(i, (i + step) % rows) for i in range(ro...  14 us
    ppermute x3, starting transfers between devices, send_chunk(): rights.append(lax.ppermute(head, 'row', backward))  12.3 us
    ppermute x3, waiting for transfers between devices, send_chunk(): lefts.append(lax.ppermute(tail, 'row', forward))  11 us
    ppermute x9, starting transfers between devices, spread_pieces(): pieces = pieces + [lax.ppermute(piece, 'col', pairs) for piece in sources]  5.32 us
    ppermute x3, waiting for transfers between devices, send_chunk(): rights.append(lax.ppermute(head, 'row', backward))  5.28 us
  transfers between devices with their start and end apart: 23, of which 5 were waited for; matrix products, arithmetic and copies ran while one was open for 7% of the time, Pallas kernels for 35%

commit v1 on v0

--- a/solution.py
+++ b/solution.py
@@ -65,14 +65,13 @@
     out_ref[0] = jnp.dot(both, perm_ref[...], preferred_element_type=F32).astype(BF)
 
 
-def attend(own, halos, images, base, rate, q_tiles, bounds, label_ref, perm_ref, *refs):
+def attend(own, halos, images, base, rate, first_query, bounds, label_ref, perm_ref, *refs):
     count = len(halos)
-    q_refs, refs = refs[: len(q_tiles)], refs[len(q_tiles) :]
-    kt_ref, v_ref, chunk_refs = refs[0], refs[1], refs[2 : 2 + count]
+    q_ref, kt_ref, v_ref, chunk_refs = refs[0], refs[1], refs[2], refs[3 : 3 + count]
     refs = refs[-(9 + count) :]
     out_ref, kt_s, v_s, scores_s, acc, top, att = refs[:7]
     raw_s, sems, own_sems = refs[7 : 7 + count], refs[-2], refs[-1]
-    heads = q_refs[0].shape[1]
+    queries, heads = q_ref.shape[:2]
     depth = kt_s.shape[3]
     slots = pl.ds(own[0] - base, len(own))
     chunk_copies = [
@@ -91,8 +90,9 @@
             key_tile(raw[0, :, lanes].astype(F32), label_ref[tile], images, depth, kt_s.at[slot])
             value_tile(raw[1, :, lanes].astype(F32), v_s.at[slot])
     kt_copy.wait()
-    for side, q_ref in enumerate(q_refs):
-        begin, end = bounds[0, q_tiles[side]], bounds[1, q_tiles[side]]
+
+    def attend_tile(side, carry):
+        begin, end = bounds[0, first_query + side], bounds[1, first_query + side]
         acc[...] = jnp.zeros_like(acc)
         top[...] = jnp.full_like(top, FAR)
 
@@ -113,14 +113,17 @@
         def score(tile, span):
             for head in range(heads):
                 keys = kt_s[pl.ds(tile - base, span), head].reshape(span * TILE, -1)
-                scores = jnp.dot(keys, q_ref[0, head], preferred_element_type=F32)
+                scores = jnp.dot(keys, q_ref[side, head], preferred_element_type=F32)
                 scores_s[pl.ds(tile - begin, span), head] = scores.reshape(span, TILE, TILE)
                 highest = jnp.max(scores.reshape(span * TILE // 8, 8, TILE), axis=0)
                 top[head] = jnp.maximum(top[head], highest)
 
         sweep(score)
-        if side == 0:
+
+        @pl.when(side == 0)
+        def _():
             v_copy.wait()
+
         tops = [jnp.max(top[head], axis=0, keepdims=True) for head in range(heads)]
         for head in range(heads):
             top[head, 0:1] = tops[head]
@@ -137,78 +140,77 @@
         whole = jnp.concatenate(
             [acc[head, :HEAD_DIM] / acc[head, HEAD_DIM : HEAD_DIM + 1] for head in range(heads)], axis=0
         )
-        att[:, side * TILE : (side + 1) * TILE] = whole.astype(BF)
-        if side % 2:
-            lanes = slice((side - 1) * TILE, (side + 1) * TILE)
-            out_ref[:, lanes] = jnp.dot(
-                att[:, lanes], perm_ref[...], preferred_element_type=F32
-            ).astype(BF)
-
-
-def project(order, last, paired, col_ref, perm_ref, gain_ref, res_ref, wt_ref, mw_ref, *refs):
+        att[:, pl.ds(pl.multiple_of(side * TILE, TILE), TILE)] = whole.astype(BF)
+        return carry
+
+    lax.fori_loop(0, queries, attend_tile, 0)
+    for at in range(queries // 2):
+        lanes = slice(2 * at * TILE, 2 * (at + 1) * TILE)
+        out_ref[:, lanes] = jnp.dot(
+            att[:, lanes], perm_ref[...], preferred_element_type=F32
+        ).astype(BF)
+
+
+def project(order, last, col_ref, perm_ref, gain_ref, res_ref, wt_ref, mw_ref, *refs):
     count = len(order)
     att_refs, refs = refs[:count], refs[count:]
-    if paired:
+    if last:
         before_ref = refs[0]
-    refs = refs[-9:]
-    layer_ref, out_ref, gathered, layer_s, wt_s, mw_s, att_sem, wt_sem, mw_sem = refs
+    layer_ref, out_ref, gathered, layer_s, wt_s, mw_s, merged_s, att_sem, wt_sem, mw_sem = refs[-10:]
     width = att_refs[0].shape[0]
     full = wt_ref.shape[0]
-    block = 2 * TILE
-    blocks = layer_s.shape[1] // block
-    groups = block // 4
+    groups = layer_s.shape[1] // 4
     col = col_ref[0]
-    att_copies, wt_copies = [], []
+
+    def wt_copy(part):
+        rows = pl.ds(pl.multiple_of(part * width, 16), width)
+        return pltpu.make_async_copy(wt_ref.at[rows, :], wt_s.at[rows, :], wt_sem.at[part])
+
+    att_copies = []
     for part, (bit, att_ref) in enumerate(zip(order, att_refs)):
         row = pl.multiple_of((col ^ bit) * width, 16)
         att_copies.append(
             pltpu.make_async_copy(att_ref, gathered.at[pl.ds(row, width), :], att_sem.at[part])
         )
-        rows = pl.ds(part * width, width)
-        wt_copies.append(
-            pltpu.make_async_copy(wt_ref.at[rows, :], wt_s.at[rows, :], wt_sem.at[part])
-        )
     mw_copy = pltpu.make_async_copy(mw_ref, mw_s, mw_sem.at[0])
-    for copy in att_copies + wt_copies + [mw_copy] * last:
+    for copy in att_copies + [wt_copy(part) for part in range(count)] + [mw_copy] * last:
         copy.start()
     for copy in att_copies:
         copy.wait()
-    for part in range(count):
-        rows = slice(part * width, (part + 1) * width)
-        wt_copies[part].wait()
-        for at in range(blocks):
-            lanes = slice(at * block, (at + 1) * block)
-            projected = jnp.dot(wt_s[rows, :], gathered[:, lanes], preferred_element_type=F32)
-            layer_s[rows, lanes] = (res_ref[part, at].astype(F32) + projected).astype(BF)
+
+    def project_part(part, carry):
+        rows = pl.ds(pl.multiple_of(part * width, 16), width)
+        wt_copy(part).wait()
+        projected = jnp.dot(wt_s[rows, :], gathered[...], preferred_element_type=F32)
+        layer_s[rows, :] = (res_ref[part, 0].astype(F32) + projected).astype(BF)
+        return carry
+
+    lax.fori_loop(0, count, project_part, 0)
     own = pl.ds(pl.multiple_of(col * width, 16), width)
-    for at in range(blocks):
-        lanes = slice(at * block, (at + 1) * block)
-        layer_ref[:, lanes] = lax.dot_general(
-            layer_s[own, lanes], perm_ref[...], (((1,), (1,)), ((), ())), preferred_element_type=F32
-        ).astype(BF)
+    layer_ref[...] = lax.dot_general(
+        layer_s[own, :], perm_ref[...], (((1,), (1,)), ((), ())), preferred_element_type=F32
+    ).astype(BF)
     if last:
         mw_copy.wait()
-    merged = None
-    for j in range(4):
-        columns = []
-        for at in range(blocks):
-            lanes = slice(at * block + j * groups, at * block + (j + 1) * groups)
-            values = layer_s[:, lanes].astype(F32)
-            values = values - jnp.sum(values, axis=0, keepdims=True) / full
-            spread = jnp.sum(jnp.square(values), axis=0, keepdims=True) / full
-            normed = (values * lax.rsqrt(spread + 1e-06) * gain_ref[...]).astype(BF)
-            if last:
-                columns.append(normed)
-            else:
-                out_ref[:, lanes] = normed
+        merged_s[...] = jnp.zeros_like(merged_s)
+
+    def merge_part(j, carry):
+        lanes = pl.ds(pl.multiple_of(j * groups, groups), groups)
+        values = layer_s[:, lanes].astype(F32)
+        values = values - jnp.sum(values, axis=0, keepdims=True) / full
+        spread = jnp.sum(jnp.square(values), axis=0, keepdims=True) / full
+        normed = (values * lax.rsqrt(spread + 1e-06) * gain_ref[...]).astype(BF)
         if last:
-            if paired:
-                columns = [before_ref[:, j * groups : (j + 1) * groups]] + columns
-            both = jnp.concatenate(columns, axis=1)
-            term = jnp.dot(mw_s[:, j * full : (j + 1) * full], both, preferred_element_type=F32)
-            merged = term if merged is None else merged + term
+            both = jnp.concatenate([before_ref[:, lanes], normed], axis=1)
+            weights = mw_s[:, pl.ds(pl.multiple_of(j * full, 128), full)]
+            merged_s[...] += jnp.dot(weights, both, preferred_element_type=F32)
+        else:
+            out_ref[:, lanes] = normed
+        return carry
+
+    lax.fori_loop(0, 4, merge_part, 0)
     if last:
-        out_ref[...] = merged.astype(BF)
+        out_ref[...] = merged_s[...].astype(BF)
 
 
 def outgoing(pieces, slot_ref, place_ref, *refs):
@@ -249,7 +251,7 @@
     own_tiles = tokens // TILE
     far_tiles = reach // TILE
     half = own_tiles // 2
-    plan = [half // 2] + [1] * (half - half // 2)
+    plan = [1] * half
     begins = [sum(plan[:s]) for s in range(len(plan))]
     stages = len(plan)
     depth = round_up(HEAD_DIM + images, 128)
@@ -301,6 +303,9 @@
             return near if block < inner else mirrored
         return jnp.where(block < inner, near, mirrored)
 
+    def stage_order(tile):
+        return jnp.where(tile >= half, 2 * (tile - half) + 1, 2 * (half - 1 - tile))
+
     at = jnp.arange(2 * TILE, dtype=jnp.int32)
     perm = (((at % 4) * (TILE // 2) + at // 4)[:, None] == at[None, :]).astype(BF)
 
@@ -314,7 +319,7 @@
             pl.BlockSpec((3, width, TILE), lambda i: (0, 0, i)),
         ],
         out_specs=[
-            pl.BlockSpec((1, heads, depth, TILE), lambda i: (i, 0, 0, 0)),
+            pl.BlockSpec((1, heads, depth, TILE), lambda i: (stage_order(i), 0, 0, 0)),
             pl.BlockSpec((1,) + kt_shape, lambda i: (i, 0, 0, 0)),
             pl.BlockSpec((1,) + v_shape, lambda i: (i, 0, 0, 0)),
         ],
@@ -345,8 +350,9 @@
         name="reorder_residual",
     )(perm, residual_in, residual_in)
     residual = lax.all_gather(residual, "col", axis=0)
-    out_weight_t = jnp.transpose(out_weight)
+    tile_order = [pair_tile(block, which) for block in range(blocks) for which in range(2)]
     key_bounds = jnp.stack([low, high])
+    key_bounds = jnp.stack([key_bounds[:, tile] for tile in tile_order], axis=1)
     gain = merge_gain[:, None]
     bits = []
     span = cols // 2
@@ -374,13 +380,12 @@
 
     def run_project(stage):
         size = plan[stage]
-        paired = stage == stages - 1 and stages - 1 > 1
-        last = stage == 0 or stage == stages - 1
-        before = [parts[stage - 1]] if paired else []
+        last = stage % 2 == 1
+        before = [parts[stage - 1]] if last else []
         columns = 2 * size * TILE
-        after = [gathers[-1][0]] if stage == 0 else [layers[stage - 1]]
+        after = [gathers[-1][0]] + layers[-1:]
         layer, part = pl.pallas_call(
-            functools.partial(project, order, last, paired),
+            functools.partial(project, order, last),
             grid=(1,),
             in_specs=[
                 smem_spec,
@@ -394,20 +399,19 @@
                 any_spec,
             ]
             + [any_spec] * cols
-            + [vmem_spec] * paired
+            + [vmem_spec] * last
             + [any_spec] * len(after),
             out_specs=[vmem_spec, vmem_spec],
             out_shape=[
                 jax.ShapeDtypeStruct((width, columns), BF),
-                jax.ShapeDtypeStruct(
-                    (width, (size + paired) * TILE // 2) if last else (full, columns), BF
-                ),
+                jax.ShapeDtypeStruct((width, TILE) if last else (full, columns), BF),
             ],
             scratch_shapes=[
                 pltpu.VMEM((full, columns), BF),
                 pltpu.VMEM((full, columns), BF),
                 pltpu.VMEM((full, full), BF),
                 pltpu.VMEM((width, 4 * full), BF),
+                pltpu.VMEM((width, TILE), F32),
                 pltpu.SemaphoreType.DMA((cols,)),
                 pltpu.SemaphoreType.DMA((cols,)),
                 pltpu.SemaphoreType.DMA((1,)),
@@ -432,14 +436,19 @@
             halos.append(list(range(far_tiles - outer_edge, far_tiles - inner_edge)))
             halos.append([far_tiles + own_tiles + at for at in range(inner_edge, outer_edge)])
             chunks += [lefts[before], rights[before]]
-        queries = [pair_tile(block, which) for block in range(near, near + size) for which in range(2)]
-        q_spec = lambda tile: pl.BlockSpec((1, heads, depth, TILE), lambda i: (tile, 0, 0, 0))
-        after = [out_weight_t] if stage == 0 else [gathers[stage - 1][0]]
+        after = [g[0] for g in gathers[-1:]] + layers[-1:]
         attended = pl.pallas_call(
-            functools.partial(attend, own, halos, images, base_tile, rate, queries),
+            functools.partial(attend, own, halos, images, base_tile, rate, 2 * near),
             grid=(1,),
-            in_specs=[smem_spec, vmem_spec, vmem_spec]
-            + [q_spec(tile) for tile in queries]
+            in_specs=[
+                smem_spec,
+                vmem_spec,
+                vmem_spec,
+                pl.BlockSpec(
+                    (2 * size, heads, depth, TILE),
+                    functools.partial(lambda s, i: (s, 0, 0, 0), near // size),
+                ),
+            ]
             + [any_spec] * (2 + len(chunks) + len(after)),
             out_specs=vmem_spec,
             out_shape=jax.ShapeDtypeStruct((width, 2 * size * TILE), BF),
@@ -456,16 +465,19 @@
             compiler_params=params(62),
             cost_estimate=cost((5 + 4 * size) * 1e9, 1e5),
             name="attend",
-        )(key_bounds, labels, perm, *([q_tiles] * len(queries)), kt_own, v_own, *chunks, *after)
+        )(key_bounds, labels, perm, q_tiles, kt_own, v_own, *chunks, *after)
 
         gathers.append([attended])
         spread_pieces(stage, bits[:1], None)
+        if stage == 0:
+            ready_weight, _ = lax.optimization_barrier((out_weight, attended))
+            out_weight_t = jnp.transpose(ready_weight)
+        if stage == 1:
+            spread_pieces(0, bits[1:], attended)
         if stage >= 1:
-            spread_pieces(stage - 1, bits[1:], attended)
-    for stage in range(stages):
-        if stage == 1:
-            spread_pieces(stages - 1, bits[1:], layers[0])
-        run_project(stage)
+            run_project(stage - 1)
+            spread_pieces(stage, bits[1:], layers[stage - 1])
+    run_project(stages - 1)
 
     tiles_out = [None] * own_tiles
     for stage in range(stages):
@@ -490,13 +502,13 @@
     away = (owner - row_id) % rows
     info = jnp.stack([away * share + rank, place // base, place % base])
     info = info.reshape(3, own_tiles, piece_groups)
-    halves = 2
+    halves = stages // 2
     info = jnp.stack(
         [
             jnp.concatenate(
                 [
                     info[:, pair_tile(block, which)]
-                    for block in range(h * blocks // 2, (h + 1) * blocks // 2)
+                    for block in (2 * h, 2 * h + 1)
                     for which in range(2)
                 ],
                 axis=1,
@@ -520,7 +532,7 @@
         compiler_params=params(16),
         cost_estimate=cost(1e9, 1e5),
         name="outgoing",
-    )(slots, places, parts[0], parts[-1])
+    )(slots, places, *parts[1::2])
     received = [sent[0]] + [
         lax.ppermute(sent[step], "row", [(i, (i + step) % rows) for i in range(rows)])
         for step in range(1, rows)

time: 163 us -> 175 us (1.074); the launches traced: 161 us -> 175 us
  Pallas kernels: 73.2 us -> 87.5 us
  waiting for transfers between devices: 18 us -> 9.88 us
  starting transfers between devices: 35 us -> 39.9 us
  local copies, waits for them, and re-layouts: 18.8 us -> 22.4 us
    ppermute x3 -> x4, waiting for transfers between devices: 11 us -> 0.51 us  [send_chunk(): lefts.append(lax.ppermute(tail, 'row', forward))]
    pallas_call x3 -> x4, Pallas kernels: 37.3 us -> 45.1 us  [run_project(): pl.pallas_call(functools.partial(project, order, last), grid=(1,), in_spe...]
    pallas_call x3 -> x4, Pallas kernels: 29.6 us -> 36 us  [body(): pl.pallas_call(functools.partial(attend, own, halos, images, base_tile, r...]
    optimization_barrier x0 -> x1, local copies, waits for them, and re-layouts: none -> 6.28 us  [body(): ready_weight, _ = lax.optimization_barrier((out_weight, attended))]
    ppermute x3 -> x4, starting transfers between devices: 12.3 us -> 17 us  [send_chunk(): rights.append(lax.ppermute(head, 'row', backward))]
    unnamed x51 -> x66, local copies, waits for them, and re-layouts: 14.4 us -> 10 us
    ppermute x9 -> x12, starting transfers between devices: 5.32 us -> 7.47 us  [spread_pieces(): pieces = pieces + [lax.ppermute(piece, 'col', pairs) for piece in sources]]
    ppermute x7, starting transfers between devices: 14 us -> 11.9 us  [body(): lax.ppermute(sent[step], 'row', [(i, (i + step) % rows) for i in range(ro...]
  transfers between devices with their start and end apart: 23 -> 28, of which waited for: 5 -> 8; matrix products, arithmetic and copies ran while one was open for 7% -> 7% of each run, Pallas kernels for 35% -> 40%
where the time goes in v1:
time: 175 us
  Pallas kernels  87.5 us (50%)
  starting transfers between devices  39.9 us (23%)
  local copies, waits for them, and re-layouts  22.4 us (13%)
  between operations  14.6 us (8%)
  waiting for transfers between devices  9.88 us (6%)
    pallas_call x4, Pallas kernels, run_project(): pl.pallas_call(functools.partial(project, order, last), grid=(1,), in_spe...  45.1 us
    pallas_call x4, Pallas kernels, body(): pl.pallas_call(functools.partial(attend, own, halos, images, base_tile, r...  36 us
    ppermute x4, starting transfers between devices, send_chunk(): rights.append(lax.ppermute(head, 'row', backward))  17 us
    ppermute x7, starting transfers between devices, body(): lax.ppermute(sent[step], 'row', [(i, (i + step) % rows) for i in range(ro...  11.9 us
    unnamed x66, local copies, waits for them, and re-layouts  10 us
    ppermute x12, starting transfers between devices, spread_pieces(): pieces = pieces + [lax.ppermute(piece, 'col', pairs) for piece in sources]  7.47 us
    optimization_barrier x1, local copies, waits for them, and re-layouts, body(): ready_weight, _ = lax.optimization_barrier((out_weight, attended))  6.28 us
    ppermute x4, waiting for transfers between devices, send_chunk(): rights.append(lax.ppermute(head, 'row', backward))  5.69 us
  transfers between devices with their start and end apart: 28, of which 8 were waited for; matrix products, arithmetic and copies ran while one was open for 7% of the time, Pallas kernels for 40%

profile of v1, /device:TPU:0, one launch (start us, length us, event | category | flops | bytes accessed | tf_op | source)
XLA Modules:
  0.0 175.4 jit_solution(4193724543018845144)
XLA Ops:
  7.2 1.2 fusion.25
  8.5 0.2 fusion.perm_ref
  8.7 0.1 copy-done.3
  8.8 2.7 %reorder_residual.1 = bf16[4,352,512]{2,1,0:T(8,128)(2,1)} custom-call(bf16[512,512]{1,0:T(8,128)(2,1)S(1)} %fusion.perm_ref, bf16[352,2048]{1,0:T(8,128)(2,1)S(1)} %copy-done.3, bf16[352,2048]{1,0:T(8,128)(2,1)S(1)} %copy-done.3), custom_call_target="tpu_custom_call" | custom-call | flops 2000000000 | bytes 100000 | tf_op jit(solution)/shard_map/reorder_residual/pallas_call | solution.py:338
  11.5 3.0 %collective-permute-start = (bf16[2,352,256]{2,1,0:T(8,128)(2,1)S(1)}, bf16[2,352,256]{2,1,0:T(8,128)(2,1)S(1)}, u32[]{:S(2)}, u32[]{:S(2)}) collective-permute-start(bf16[2,352,256]{2,1,0:T(8,128)(2,1)S(1)} %get-tuple-element.77), channel_id=1, source_target_pairs={{0,4},{4,8},{8,12},{12,16},{16,20},{20,24},{24,28},{28,0},{1,5},{5... | collective-permute-start | bytes 1081352 | tf_op jit(solution)/shard_map/ppermute | solution.py:273
  14.5 3.1 %collective-permute-start.1 = (bf16[2,352,256]{2,1,0:T(8,128)(2,1)S(1)}, bf16[2,352,256]{2,1,0:T(8,128)(2,1)S(1)}, u32[]{:S(2)}, u32[]{:S(2)}) collective-permute-start(bf16[2,352,256]{2,1,0:T(8,128)(2,1)S(1)} %get-tuple-element.76), channel_id=1, source_target_pairs={{4,0},{8,4},{12,8},{16,12},{20,16},{24,20},{28,24},{0,28},{5,1},{9... | collective-permute-start | bytes 1081352 | tf_op jit(solution)/shard_map/ppermute | solution.py:274
  17.6 0.1 copy.39
  17.8 0.1 multiply_reduce_fusion
  17.9 0.2 select_reduce_fusion.1
  18.2 1.1 broadcast_in_dim.42.gain_ref
  19.4 0.2 convert_reduce_fusion
  19.6 0.1 stack.35
  19.7 0.1 stack.36
  19.8 0.1 stack.37
  19.9 0.6 stack.34.bounds
  20.7 0.1 convert_reduce_fusion.1
  20.9 2.8 %copy-done = bf16[3,352,2048]{2,1,0:T(8,128)(2,1)S(1)} copy-done((bf16[3,352,2048]{2,1,0:T(8,128)(2,1)S(1)}, bf16[3,352,2048]{2,1,0:T(8,128)(2,1)}, u32[]{:S(2)}) %copy-start) | copy-done | bytes 4325400
  23.7 1.8 %prepare_own.1 = (bf16[8,4,128,256]{3,2,1,0:T(8,128)(2,1)S(1)}, bf16[8,4,256,128]{3,2,1,0:T(8,128)(2,1)S(1)}, bf16[8,4,96,256]{3,2,1,0:T(8,128)(2,1)S(1)}) custom-call(s32[16,1,256]{2,1,0:T(1,128)S(1)} %compare_select_fusion.label_ref, bf16[3,352,2048]{2,1,0:T(8,128)(2,1)S(1)} %copy-done), custom_call_target="tpu_custom_call" | custom-call | flops 2000000000 | bytes 100000 | tf_op jit(solution)/shard_map/prepare_own/pallas_call | solution.py:314
  25.6 1.3 copy-done.4
  26.9 1.3 copy-done.5
  28.2 1.2 copy-done.6
  29.4 0.5 collective-permute-done.refs_3_
  29.9 2.2 %collective-permute-done.1.refs_4_ = bf16[2,352,256]{2,1,0:T(8,128)(2,1)S(1)} collective-permute-done((bf16[2,352,256]{2,1,0:T(8,128)(2,1)S(1)}, bf16[2,352,256]{2,1,0:T(8,128)(2,1)S(1)}, u32[]{:S(2)}, u32[]{:S(2)}) %collective-permute-start.1) | collective-permute-done | bytes 360480 | tf_op jit(solution)/shard_map/ppermute | solution.py:274
  32.2 0.3 collective-permute-start.2
  32.5 4.4 %collective-permute-start.3 = (bf16[2,352,256]{2,1,0:T(8,128)(2,1)S(1)}, bf16[2,352,256]{2,1,0:T(8,128)(2,1)}, u32[]{:S(2)}, u32[]{:S(2)}) collective-permute-start(bf16[2,352,256]{2,1,0:T(8,128)(2,1)S(1)} %get-tuple-element.74), channel_id=1, source_target_pairs={{4,0},{8,4},{12,8},{16,12},{20,16},{24,20},{28,24},{0,28},{5,1},{9... | collective-permute-start | bytes 1081352 | tf_op jit(solution)/shard_map/ppermute | solution.py:274
  36.9 9.2 %attend.4.refs_7_.refs_0_ = bf16[352,512]{1,0:T(8,128)(2,1)} custom-call(s32[2,8]{1,0:T(2,128)} %stack.34.bounds, s32[16,1,256]{2,1,0:T(1,128)} %copy-done.2, bf16[512,512]{1,0:T(8,128)(2,1)} %copy-done.1, bf16[8,4,128,256]{3,2,1,0:T(8,128)(2,1)} %copy-done.4, bf16[8,4,256,128]{3,2,1,0:T(8,128)(2,1)} %copy-done.5, bf16[8,4,96,256]{3,2,1,0:T(8,128)(2,1)} %copy-done.6, ...), custom_call_target="tpu_custom_call" | custom-call | flops 8999999488 | bytes 100000 | tf_op jit(solution)/shard_map/attend/pallas_call | solution.py:440
  46.1 1.6 collective-permute-start.8
  47.7 3.5 %collective-permute-done.3.refs_6_ = bf16[2,352,256]{2,1,0:T(8,128)(2,1)} collective-permute-done((bf16[2,352,256]{2,1,0:T(8,128)(2,1)S(1)}, bf16[2,352,256]{2,1,0:T(8,128)(2,1)}, u32[]{:S(2)}, u32[]{:S(2)}) %collective-permute-start.3) | collective-permute-done | bytes 360480 | tf_op jit(solution)/shard_map/ppermute | solution.py:274
  51.2 1.1 fusion.23
  52.4 4.7 %collective-permute-start.5 = (bf16[2,352,256]{2,1,0:T(8,128)(2,1)S(1)}, bf16[2,352,256]{2,1,0:T(8,128)(2,1)S(1)}, u32[]{:S(2)}, u32[]{:S(2)}) collective-permute-start(bf16[2,352,256]{2,1,0:T(8,128)(2,1)S(1)} %get-tuple-element.72), channel_id=1, source_target_pairs={{4,0},{8,4},{12,8},{16,12},{20,16},{24,20},{28,24},{0,28},{5,1},{9... | collective-permute-start | bytes 1081352 | tf_op jit(solution)/shard_map/ppermute | solution.py:274
  57.1 9.8 %attend.5.refs_4_.refs_9_.refs_0_ = bf16[352,512]{1,0:T(8,128)(2,1)} custom-call(s32[2,8]{1,0:T(2,128)} %stack.34.bounds, s32[16,1,256]{2,1,0:T(1,128)} %copy-done.2, bf16[512,512]{1,0:T(8,128)(2,1)} %copy-done.1, bf16[8,4,128,256]{3,2,1,0:T(8,128)(2,1)} %copy-done.4, bf16[8,4,256,128]{3,2,1,0:T(8,128)(2,1)} %copy-done.5, bf16[8,4,96,256]{3,2,1,0:T(8,128)(2,1)} %copy-done.6, ...), custom_call_target="tpu_custom_call" | custom-call | flops 8999999488 | bytes 100000 | tf_op jit(solution)/shard_map/attend/pallas_call | solution.py:440
  67.0 0.5 collective-permute-start.9
  67.5 6.3 %copy.40 = bf16[1408,1408]{0,1:T(8,128)(2,1)} copy(bf16[1408,1408]{1,0:T(8,128)(2,1)} %param.9) | data formatting | bytes 7929856 | tf_op jit(solution)/shard_map/optimization_barrier | solution.py:473
  73.8 1.5 collective-permute-start.11
  75.2 1.4 fusion.22
  76.7 4.7 %collective-permute-start.7 = (bf16[2,352,256]{2,1,0:T(8,128)(2,1)S(1)}, bf16[2,352,256]{2,1,0:T(8,128)(2,1)}, u32[]{:S(2)}, u32[]{:S(2)}) collective-permute-start(bf16[2,352,256]{2,1,0:T(8,128)(2,1)S(1)} %get-tuple-element.70), channel_id=1, source_target_pairs={{4,0},{8,4},{12,8},{16,12},{20,16},{24,20},{28,24},{0,28},{5,1},{9... | collective-permute-start | bytes 1081352 | tf_op jit(solution)/shard_map/ppermute | solution.py:274
  81.4 10.4 %project.4 = (bf16[352,512]{1,0:T(8,128)(2,1)}, bf16[1408,512]{1,0:T(8,128)(2,1)}) custom-call(s32[1]{0:T(128)} %bitcast.col_ref, bf16[512,512]{1,0:T(8,128)(2,1)} %copy-done.1, f32[1408,1]{1,0:T(8,128)} %broadcast_in_dim.42.gain_ref, bf16[4,4,352,512]{3,2,1,0:T(8,128)(2,1)} %bitcast.57, bf16[1408,1408]{1,0:T(8,128)(2,1)} %bitcast.51, ...), custom_call_target="tpu_custom_call" | custom-call | flops 8000000000 | bytes 100000 | tf_op jit(solution)/shard_map/project/pallas_call | solution.py:387
  92.0 0.5 collective-permute-start.13
  92.5 9.6 %attend.6.refs_5_.refs_11_.refs_0_ = bf16[352,512]{1,0:T(8,128)(2,1)} custom-call(s32[2,8]{1,0:T(2,128)} %stack.34.bounds, s32[16,1,256]{2,1,0:T(1,128)} %copy-done.2, bf16[512,512]{1,0:T(8,128)(2,1)} %copy-done.1, bf16[8,4,128,256]{3,2,1,0:T(8,128)(2,1)} %copy-done.4, bf16[8,4,256,128]{3,2,1,0:T(8,128)(2,1)} %copy-done.5, ...), custom_call_target="tpu_custom_call" | custom-call | flops 8999999488 | bytes 100000 | tf_op jit(solution)/shard_map/attend/pallas_call | solution.py:440
  102.1 0.6 collective-permute-start.15
  102.7 0.7 copy-done.29
  103.5 12.2 %project.5 = (bf16[352,512]{1,0:T(8,128)(2,1)}, bf16[352,256]{1,0:T(8,128)(2,1)}) custom-call(s32[1]{0:T(128)} %bitcast.col_ref, bf16[512,512]{1,0:T(8,128)(2,1)} %copy-done.1, f32[1408,1]{1,0:T(8,128)} %broadcast_in_dim.42.gain_ref, bf16[4,4,352,512]{3,2,1,0:T(8,128)(2,1)} %bitcast.58, bf16[1408,1408]{1,0:T(8,128)(2,1)} %bitcast.52, ...), custom_call_target="tpu_custom_call" | custom-call | flops 8000000000 | bytes 100000 | tf_op jit(solution)/shard_map/project/pallas_call | solution.py:387
  115.7 0.5 collective-permute-start.17
  116.2 0.7 copy-done.22
  117.0 7.5 %attend.7.refs_4_.refs_0_.refs_5_ = bf16[352,512]{1,0:T(8,128)(2,1)} custom-call(s32[2,8]{1,0:T(2,128)} %stack.34.bounds, s32[16,1,256]{2,1,0:T(1,128)} %copy-done.2, bf16[512,512]{1,0:T(8,128)(2,1)} %copy-done.1, bf16[8,4,128,256]{3,2,1,0:T(8,128)(2,1)} %copy-done.4, bf16[8,4,256,128]{3,2,1,0:T(8,128)(2,1)} %copy-done.5, bf16[8,4,96,256]{3,2,1,0:T(8,128)(2,1)} %copy-done.6, ...), custom_call_target="tpu_custom_call" | custom-call | flops 8999999488 | bytes 100000 | tf_op jit(solution)/shard_map/attend/pallas_call | solution.py:440
  124.5 1.5 collective-permute-start.14
  126.0 10.4 %project.6 = (bf16[352,512]{1,0:T(8,128)(2,1)}, bf16[1408,512]{1,0:T(8,128)(2,1)}) custom-call(s32[1]{0:T(128)} %bitcast.col_ref, bf16[512,512]{1,0:T(8,128)(2,1)} %copy-done.1, f32[1408,1]{1,0:T(8,128)} %broadcast_in_dim.42.gain_ref, bf16[4,4,352,512]{3,2,1,0:T(8,128)(2,1)} %bitcast.59, bf16[1408,1408]{1,0:T(8,128)(2,1)} %bitcast.53, ...), custom_call_target="tpu_custom_call" | custom-call | flops 8000000000 | bytes 100000 | tf_op jit(solution)/shard_map/project/pallas_call | solution.py:387
  136.5 0.5 collective-permute-start.19
  137.1 1.1 collective-permute-done.18.refs_2_
  138.2 0.5 collective-permute-done.19.refs_3_
  138.7 0.2 copy-done.27
  138.9 0.5 copy-done.28
  139.5 12.1 %project.7 = (bf16[352,512]{1,0:T(8,128)(2,1)}, bf16[352,256]{1,0:T(8,128)(2,1)}) custom-call(s32[1]{0:T(128)} %bitcast.col_ref, bf16[512,512]{1,0:T(8,128)(2,1)} %copy-done.1, f32[1408,1]{1,0:T(8,128)} %broadcast_in_dim.42.gain_ref, bf16[4,4,352,512]{3,2,1,0:T(8,128)(2,1)} %bitcast.60, bf16[1408,1408]{1,0:T(8,128)(2,1)} %bitcast.54, ...), custom_call_target="tpu_custom_call" | custom-call | flops 8000000000 | bytes 100000 | tf_op jit(solution)/shard_map/project/pallas_call | solution.py:387
  151.6 0.9 copy-done.8
  152.5 0.5 outgoing.1
  153.1 1.7 collective-permute-start.21
  154.8 2.2 %collective-permute-start.22 = (bf16[64,384]{1,0:T(8,128)(2,1)S(1)}, bf16[64,384]{1,0:T(8,128)(2,1)S(1)}, u32[]{:S(2)}, u32[]{:S(2)}) collective-permute-start(bf16[64,384]{1,0:T(8,128)(2,1)S(1)} %get-tuple-element.63), channel_id=1, source_target_pairs={{0,12},{4,16},{8,20},{12,24},{16,28},{20,0},{24,4},{28,8},{1,13},{... | collective-permute-start | bytes 147464 | tf_op jit(solution)/shard_map/ppermute | solution.py:537
  157.0 1.4 collective-permute-start.23
  158.4 1.6 collective-permute-start.24
  160.1 0.3 collective-permute-done.20.refs_1_
  160.4 2.2 %collective-permute-start.25 = (bf16[64,384]{1,0:T(8,128)(2,1)S(1)}, bf16[64,384]{1,0:T(8,128)(2,1)S(1)}, u32[]{:S(2)}, u32[]{:S(2)}) collective-permute-start(bf16[64,384]{1,0:T(8,128)(2,1)S(1)} %get-tuple-element.66), channel_id=1, source_target_pairs={{0,24},{4,28},{8,0},{12,4},{16,8},{20,12},{24,16},{28,20},{1,25},{... | collective-permute-start | bytes 147464 | tf_op jit(solution)/shard_map/ppermute | solution.py:537
  162.6 2.9 %collective-permute-start.26 = (bf16[64,384]{1,0:T(8,128)(2,1)S(1)}, bf16[64,384]{1,0:T(8,128)(2,1)S(1)}, u32[]{:S(2)}, u32[]{:S(2)}) collective-permute-start(bf16[64,384]{1,0:T(8,128)(2,1)S(1)} %get-tuple-element.67), channel_id=1, source_target_pairs={{0,28},{4,0},{8,4},{12,8},{16,12},{20,16},{24,20},{28,24},{1,29},{... | collective-permute-start | bytes 147464 | tf_op jit(solution)/shard_map/ppermute | solution.py:537
  165.6 1.6 collective-permute-done.26.refs_7_
  167.2 1.3 incoming.1
  (107 shorter events, 1.4 us)
Async XLA Ops:
  7.2 1.6 copy-start.3
  7.2 74.3 %all-gather.3.cloned.1.call-start = ((), (), s32[]{:S(2)}) async-start(), calls=%async_computation | async-start | bytes 7208960 | tf_op jit(solution)/shard_map/all_gather | solution.py:352
  8.6 2.8 %copy-start.1 = (bf16[512,512]{1,0:T(8,128)(2,1)}, bf16[512,512]{1,0:T(8,128)(2,1)S(1)}, u32[]{:S(2)}) copy-start(bf16[512,512]{1,0:T(8,128)(2,1)S(1)} %fusion.perm_ref) | copy-start | bytes 1572868
  11.5 6.1 %copy-start.16 = (s32[32]{0:T(128)S(1)}, s32[32]{0:T(128)}, u32[]{:S(2)}) copy-start(s32[32]{0:T(128)} %param.12) | copy-start | bytes 388
  11.5 6.7 %copy-start.14 = (f32[1408]{0:T(1024)S(1)}, f32[1408]{0:T(1024)}, u32[]{:S(2)}) copy-start(f32[1408]{0:T(1024)} %param.11) | copy-start | bytes 16900
  11.5 7.9 %copy-start.15 = (s32[512]{0:T(512)S(1)}, s32[512]{0:T(512)}, u32[]{:S(2)}) copy-start(s32[512]{0:T(512)} %param.13) | copy-start | bytes 6148
  11.5 18.4 %collective-permute-start = (bf16[2,352,256]{2,1,0:T(8,128)(2,1)S(1)}, bf16[2,352,256]{2,1,0:T(8,128)(2,1)S(1)}, u32[]{:S(2)}, u32[]{:S(2)}) collective-permute-start(bf16[2,352,256]{2,1,0:T(8,128)(2,1)S(1)} %get-tuple-element.77), channel_id=1, source_target_pairs={{0,4},{4,8},{8,12},{12,16},{16,20},{20,24},{24,28},{28,0},{1,5},{5... | collective-permute-start | bytes 1081352 | tf_op jit(solution)/shard_map/ppermute | solution.py:273
  14.5 17.6 %collective-permute-start.1 = (bf16[2,352,256]{2,1,0:T(8,128)(2,1)S(1)}, bf16[2,352,256]{2,1,0:T(8,128)(2,1)S(1)}, u32[]{:S(2)}, u32[]{:S(2)}) collective-permute-start(bf16[2,352,256]{2,1,0:T(8,128)(2,1)S(1)} %get-tuple-element.76), channel_id=1, source_target_pairs={{4,0},{8,4},{12,8},{16,12},{20,16},{24,20},{28,24},{0,28},{5,1},{9... | collective-permute-start | bytes 1081352 | tf_op jit(solution)/shard_map/ppermute | solution.py:274
  20.9 2.8 %copy-start = (bf16[3,352,2048]{2,1,0:T(8,128)(2,1)S(1)}, bf16[3,352,2048]{2,1,0:T(8,128)(2,1)}, u32[]{:S(2)}) copy-start(bf16[3,352,2048]{2,1,0:T(8,128)(2,1)} %qkv_ref) | copy-start | bytes 12976132
  23.7 1.9 %copy-start.2 = (s32[16,1,256]{2,1,0:T(1,128)}, s32[16,1,256]{2,1,0:T(1,128)S(1)}, u32[]{:S(2)}) copy-start(s32[16,1,256]{2,1,0:T(1,128)S(1)} %compare_select_fusion.label_ref) | copy-start | bytes 49156
  25.6 1.3 copy-start.4
  26.9 1.3 copy-start.5
  28.2 1.2 copy-start.6
  29.9 7.0 %copy-start.17 = (bf16[2,352,256]{2,1,0:T(8,128)(2,1)}, bf16[2,352,256]{2,1,0:T(8,128)(2,1)S(1)}, u32[]{:S(2)}) copy-start(bf16[2,352,256]{2,1,0:T(8,128)(2,1)S(1)} %collective-permute-done.refs_3_) | copy-start | bytes 1081348
  32.1 4.8 %copy-start.18 = (bf16[2,352,256]{2,1,0:T(8,128)(2,1)}, bf16[2,352,256]{2,1,0:T(8,128)(2,1)S(1)}, u32[]{:S(2)}) copy-start(bf16[2,352,256]{2,1,0:T(8,128)(2,1)S(1)} %collective-permute-done.1.refs_4_) | copy-start | bytes 1081348
  32.2 15.5 %collective-permute-start.2 = (bf16[2,352,256]{2,1,0:T(8,128)(2,1)S(1)}, bf16[2,352,256]{2,1,0:T(8,128)(2,1)S(1)}, u32[]{:S(2)}, u32[]{:S(2)}) collective-permute-start(bf16[2,352,256]{2,1,0:T(8,128)(2,1)S(1)} %get-tuple-element.75), channel_id=1, source_target_pairs={{0,4},{4,8},{8,12},{12,16},{16,20},{20,24},{24,28},{28,0},{1,5},{5... | collective-permute-start | bytes 1081352 | tf_op jit(solution)/shard_map/ppermute | solution.py:273
  32.5 18.7 %collective-permute-start.3 = (bf16[2,352,256]{2,1,0:T(8,128)(2,1)S(1)}, bf16[2,352,256]{2,1,0:T(8,128)(2,1)}, u32[]{:S(2)}, u32[]{:S(2)}) collective-permute-start(bf16[2,352,256]{2,1,0:T(8,128)(2,1)S(1)} %get-tuple-element.74), channel_id=1, source_target_pairs={{4,0},{8,4},{12,8},{16,12},{20,16},{24,20},{28,24},{0,28},{5,1},{9... | collective-permute-start | bytes 1081352 | tf_op jit(solution)/shard_map/ppermute | solution.py:274
  46.1 20.8 %collective-permute-start.8 = (bf16[352,512]{1,0:T(8,128)(2,1)}, bf16[352,512]{1,0:T(8,128)(2,1)}, u32[]{:S(2)}, u32[]{:S(2)}) collective-permute-start(bf16[352,512]{1,0:T(8,128)(2,1)} %attend.4.refs_7_.refs_0_), channel_id=1, source_target_pairs={{0,2},{1,3},{2,0},{3,1},{4,6},{5,7},{6,4},{7,5},{8,10},{9,11},{10,... | collective-permute-start | bytes 1081352 | tf_op jit(solution)/shard_map/ppermute | solution.py:378
  47.7 9.4 %copy-start.19 = (bf16[2,352,256]{2,1,0:T(8,128)(2,1)}, bf16[2,352,256]{2,1,0:T(8,128)(2,1)S(1)}, u32[]{:S(2)}) copy-start(bf16[2,352,256]{2,1,0:T(8,128)(2,1)S(1)} %collective-permute-done.2.refs_5_) | copy-start | bytes 1081348
  52.3 22.9 %collective-permute-start.4 = (bf16[2,352,256]{2,1,0:T(8,128)(2,1)S(1)}, bf16[2,352,256]{2,1,0:T(8,128)(2,1)S(1)}, u32[]{:S(2)}, u32[]{:S(2)}) collective-permute-start(bf16[2,352,256]{2,1,0:T(8,128)(2,1)S(1)} %get-tuple-element.73), channel_id=1, source_target_pairs={{0,4},{4,8},{8,12},{12,16},{16,20},{20,24},{24,28},{28,0},{1,5},{5... | collective-permute-start | bytes 1081352 | tf_op jit(solution)/shard_map/ppermute | solution.py:273
  52.4 22.8 %collective-permute-start.5 = (bf16[2,352,256]{2,1,0:T(8,128)(2,1)S(1)}, bf16[2,352,256]{2,1,0:T(8,128)(2,1)S(1)}, u32[]{:S(2)}, u32[]{:S(2)}) collective-permute-start(bf16[2,352,256]{2,1,0:T(8,128)(2,1)S(1)} %get-tuple-element.72), channel_id=1, source_target_pairs={{4,0},{8,4},{12,8},{16,12},{20,16},{24,20},{28,24},{0,28},{5,1},{9... | collective-permute-start | bytes 1081352 | tf_op jit(solution)/shard_map/ppermute | solution.py:274
  66.9 14.5 %collective-permute-start.10 = (bf16[352,512]{1,0:T(8,128)(2,1)}, bf16[352,512]{1,0:T(8,128)(2,1)}, u32[]{:S(2)}, u32[]{:S(2)}) collective-permute-start(bf16[352,512]{1,0:T(8,128)(2,1)} %collective-permute-done.8.refs_1_), channel_id=1, source_target_pairs={{0,1},{1,0},{2,3},{3,2},{4,5},{5,4},{6,7},{7,6},{8,9},{9,8},{10,11... | collective-permute-start | bytes 1081352 | tf_op jit(solution)/shard_map/ppermute | solution.py:378
  67.0 14.5 %collective-permute-start.9 = (bf16[352,512]{1,0:T(8,128)(2,1)}, bf16[352,512]{1,0:T(8,128)(2,1)}, u32[]{:S(2)}, u32[]{:S(2)}) collective-permute-start(bf16[352,512]{1,0:T(8,128)(2,1)} %attend.4.refs_7_.refs_0_), channel_id=1, source_target_pairs={{0,1},{1,0},{2,3},{3,2},{4,5},{5,4},{6,7},{7,6},{8,9},{9,8},{10,11... | collective-permute-start | bytes 1081352 | tf_op jit(solution)/shard_map/ppermute | solution.py:378
  73.8 18.1 %collective-permute-start.11 = (bf16[352,512]{1,0:T(8,128)(2,1)}, bf16[352,512]{1,0:T(8,128)(2,1)}, u32[]{:S(2)}, u32[]{:S(2)}) collective-permute-start(bf16[352,512]{1,0:T(8,128)(2,1)} %attend.5.refs_4_.refs_9_.refs_0_), channel_id=1, source_target_pairs={{0,2},{1,3},{2,0},{3,1},{4,6},{5,7},{6,4},{7,5},{8,10},{9,11},{10,... | collective-permute-start | bytes 1081352 | tf_op jit(solution)/shard_map/ppermute | solution.py:378
  75.2 16.7 %copy-start.20 = (bf16[2,352,256]{2,1,0:T(8,128)(2,1)}, bf16[2,352,256]{2,1,0:T(8,128)(2,1)S(1)}, u32[]{:S(2)}) copy-start(bf16[2,352,256]{2,1,0:T(8,128)(2,1)S(1)} %collective-permute-done.4.refs_7_) | copy-start | bytes 1081348
  75.2 16.7 %copy-start.21 = (bf16[2,352,256]{2,1,0:T(8,128)(2,1)}, bf16[2,352,256]{2,1,0:T(8,128)(2,1)S(1)}, u32[]{:S(2)}) copy-start(bf16[2,352,256]{2,1,0:T(8,128)(2,1)S(1)} %collective-permute-done.5.refs_8_) | copy-start | bytes 1081348
  76.7 39.6 %collective-permute-start.6 = (bf16[2,352,256]{2,1,0:T(8,128)(2,1)S(1)}, bf16[2,352,256]{2,1,0:T(8,128)(2,1)S(1)}, u32[]{:S(2)}, u32[]{:S(2)}) collective-permute-start(bf16[2,352,256]{2,1,0:T(8,128)(2,1)S(1)} %get-tuple-element.71), channel_id=1, source_target_pairs={{0,4},{4,8},{8,12},{12,16},{16,20},{20,24},{24,28},{28,0},{1,5},{5... | collective-permute-start | bytes 1081352 | tf_op jit(solution)/shard_map/ppermute | solution.py:273
  76.7 39.5 %collective-permute-start.7 = (bf16[2,352,256]{2,1,0:T(8,128)(2,1)S(1)}, bf16[2,352,256]{2,1,0:T(8,128)(2,1)}, u32[]{:S(2)}, u32[]{:S(2)}) collective-permute-start(bf16[2,352,256]{2,1,0:T(8,128)(2,1)S(1)} %get-tuple-element.70), channel_id=1, source_target_pairs={{4,0},{8,4},{12,8},{16,12},{20,16},{24,20},{28,24},{0,28},{5,1},{9... | collective-permute-start | bytes 1081352 | tf_op jit(solution)/shard_map/ppermute | solution.py:274
  91.9 10.8 %collective-permute-start.12 = (bf16[352,512]{1,0:T(8,128)(2,1)}, bf16[352,512]{1,0:T(8,128)(2,1)S(1)}, u32[]{:S(2)}, u32[]{:S(2)}) collective-permute-start(bf16[352,512]{1,0:T(8,128)(2,1)} %attend.5.refs_4_.refs_9_.refs_0_), channel_id=1, source_target_pairs={{0,1},{1,0},{2,3},{3,2},{4,5},{5,4},{6,7},{7,6},{8,9},{9,8},{10,11... | collective-permute-start | bytes 1081352 | tf_op jit(solution)/shard_map/ppermute | solution.py:378
  92.0 10.8 %collective-permute-start.13 = (bf16[352,512]{1,0:T(8,128)(2,1)}, bf16[352,512]{1,0:T(8,128)(2,1)}, u32[]{:S(2)}, u32[]{:S(2)}) collective-permute-start(bf16[352,512]{1,0:T(8,128)(2,1)} %collective-permute-done.11.refs_1_), channel_id=1, source_target_pairs={{0,1},{1,0},{2,3},{3,2},{4,5},{5,4},{6,7},{7,6},{8,9},{9,8},{10,11... | collective-permute-start | bytes 1081352 | tf_op jit(solution)/shard_map/ppermute | solution.py:378
  102.1 13.5 %collective-permute-start.15 = (bf16[352,512]{1,0:T(8,128)(2,1)}, bf16[352,512]{1,0:T(8,128)(2,1)S(1)}, u32[]{:S(2)}, u32[]{:S(2)}) collective-permute-start(bf16[352,512]{1,0:T(8,128)(2,1)} %attend.6.refs_5_.refs_11_.refs_0_), channel_id=1, source_target_pairs={{0,2},{1,3},{2,0},{3,1},{4,6},{5,7},{6,4},{7,5},{8,10},{9,11},{10,... | collective-permute-start | bytes 1081352 | tf_op jit(solution)/shard_map/ppermute | solution.py:378
  102.7 0.7 copy-start.29
  103.5 12.2 %copy-start.24 = (bf16[352,512]{1,0:T(8,128)(2,1)S(1)}, bf16[352,512]{1,0:T(8,128)(2,1)}, u32[]{:S(2)}) copy-start(bf16[352,512]{1,0:T(8,128)(2,1)} %attend.6.refs_5_.refs_11_.refs_0_) | copy-start | bytes 1081348
  115.6 8.8 %copy-start.25 = (bf16[352,512]{1,0:T(8,128)(2,1)}, bf16[352,512]{1,0:T(8,128)(2,1)S(1)}, u32[]{:S(2)}) copy-start(bf16[352,512]{1,0:T(8,128)(2,1)S(1)} %collective-permute-done.15.refs_1_) | copy-start | bytes 1081348
  115.7 10.3 %collective-permute-start.16 = (bf16[352,512]{1,0:T(8,128)(2,1)S(1)}, bf16[352,512]{1,0:T(8,128)(2,1)}, u32[]{:S(2)}, u32[]{:S(2)}) collective-permute-start(bf16[352,512]{1,0:T(8,128)(2,1)S(1)} %copy-done.24), channel_id=1, source_target_pairs={{0,1},{1,0},{2,3},{3,2},{4,5},{5,4},{6,7},{7,6},{8,9},{9,8},{10,11... | collective-permute-start | bytes 1081352 | tf_op jit(solution)/shard_map/ppermute | solution.py:378
  115.7 10.3 %collective-permute-start.17 = (bf16[352,512]{1,0:T(8,128)(2,1)S(1)}, bf16[352,512]{1,0:T(8,128)(2,1)}, u32[]{:S(2)}, u32[]{:S(2)}) collective-permute-start(bf16[352,512]{1,0:T(8,128)(2,1)S(1)} %collective-permute-done.15.refs_1_), channel_id=1, source_target_pairs={{0,1},{1,0},{2,3},{3,2},{4,5},{5,4},{6,7},{7,6},{8,9},{9,8},{10,11... | collective-permute-start | bytes 1081352 | tf_op jit(solution)/shard_map/ppermute | solution.py:378
  116.2 0.7 copy-start.22
  124.5 12.0 %copy-start.23 = (bf16[352,512]{1,0:T(8,128)(2,1)S(1)}, bf16[352,512]{1,0:T(8,128)(2,1)}, u32[]{:S(2)}) copy-start(bf16[352,512]{1,0:T(8,128)(2,1)} %attend.7.refs_4_.refs_0_.refs_5_) | copy-start | bytes 1081348
  124.5 12.0 %collective-permute-start.14 = (bf16[352,512]{1,0:T(8,128)(2,1)}, bf16[352,512]{1,0:T(8,128)(2,1)S(1)}, u32[]{:S(2)}, u32[]{:S(2)}) collective-permute-start(bf16[352,512]{1,0:T(8,128)(2,1)} %attend.7.refs_4_.refs_0_.refs_5_), channel_id=1, source_target_pairs={{0,2},{1,3},{2,0},{3,1},{4,6},{5,7},{6,4},{7,5},{8,10},{9,11},{10,... | collective-permute-start | bytes 1081352 | tf_op jit(solution)/shard_map/ppermute | solution.py:378
  136.4 2.3 %copy-start.26 = (bf16[352,512]{1,0:T(8,128)(2,1)}, bf16[352,512]{1,0:T(8,128)(2,1)S(1)}, u32[]{:S(2)}) copy-start(bf16[352,512]{1,0:T(8,128)(2,1)S(1)} %collective-permute-done.14.refs_1_) | copy-start | bytes 1081348
  136.5 1.7 collective-permute-start.18
  136.5 2.2 %collective-permute-start.19 = (bf16[352,512]{1,0:T(8,128)(2,1)S(1)}, bf16[352,512]{1,0:T(8,128)(2,1)S(1)}, u32[]{:S(2)}, u32[]{:S(2)}) collective-permute-start(bf16[352,512]{1,0:T(8,128)(2,1)S(1)} %collective-permute-done.14.refs_1_), channel_id=1, source_target_pairs={{0,1},{1,0},{2,3},{3,2},{4,5},{5,4},{6,7},{7,6},{8,9},{9,8},{10,11... | collective-permute-start | bytes 1081352 | tf_op jit(solution)/shard_map/ppermute | solution.py:378
  138.2 0.7 copy-start.27
  138.7 0.7 copy-start.28
  139.5 12.1 %copy-start.7 = (bf16[352,256]{1,0:T(8,128)(2,1)S(1)}, bf16[352,256]{1,0:T(8,128)(2,1)}, u32[]{:S(2)}) copy-start(bf16[352,256]{1,0:T(8,128)(2,1)} %get-tuple-element.58.refs_0_) | copy-start | bytes 540676
  151.6 0.9 copy-start.8
  152.5 7.4 %copy-start.12 = (bf16[352,512]{1,0:T(8,128)(2,1)S(1)}, bf16[352,512]{1,0:T(8,128)(2,1)}, u32[]{:S(2)}) copy-start(bf16[352,512]{1,0:T(8,128)(2,1)} %get-tuple-element.57) | copy-start | bytes 1081348
  152.5 7.4 %copy-start.11 = (bf16[352,512]{1,0:T(8,128)(2,1)S(1)}, bf16[352,512]{1,0:T(8,128)(2,1)}, u32[]{:S(2)}) copy-start(bf16[352,512]{1,0:T(8,128)(2,1)} %get-tuple-element.53.refs_6_) | copy-start | bytes 1081348
  152.5 7.4 %copy-start.10 = (bf16[352,512]{1,0:T(8,128)(2,1)S(1)}, bf16[352,512]{1,0:T(8,128)(2,1)}, u32[]{:S(2)}) copy-start(bf16[352,512]{1,0:T(8,128)(2,1)} %get-tuple-element.50.refs_12_.refs_5_) | copy-start | bytes 1081348
  152.5 7.5 %copy-start.9 = (bf16[352,512]{1,0:T(8,128)(2,1)S(1)}, bf16[352,512]{1,0:T(8,128)(2,1)}, u32[]{:S(2)}) copy-start(bf16[352,512]{1,0:T(8,128)(2,1)} %get-tuple-element.46.refs_10_.refs_6_) | copy-start | bytes 1081348
  153.0 7.4 %collective-permute-start.20 = (bf16[64,384]{1,0:T(8,128)(2,1)S(1)}, bf16[64,384]{1,0:T(8,128)(2,1)S(1)}, u32[]{:S(2)}, u32[]{:S(2)}) collective-permute-start(bf16[64,384]{1,0:T(8,128)(2,1)S(1)} %get-tuple-element.61), channel_id=1, source_target_pairs={{0,4},{4,8},{8,12},{12,16},{16,20},{20,24},{24,28},{28,0},{1,5},{5... | collective-permute-start | bytes 147464 | tf_op jit(solution)/shard_map/ppermute | solution.py:537
  153.1 9.5 %collective-permute-start.21 = (bf16[64,384]{1,0:T(8,128)(2,1)S(1)}, bf16[64,384]{1,0:T(8,128)(2,1)S(1)}, u32[]{:S(2)}, u32[]{:S(2)}) collective-permute-start(bf16[64,384]{1,0:T(8,128)(2,1)S(1)} %get-tuple-element.62), channel_id=1, source_target_pairs={{0,8},{4,12},{8,16},{12,20},{16,24},{20,28},{24,0},{28,4},{1,9},{5... | collective-permute-start | bytes 147464 | tf_op jit(solution)/shard_map/ppermute | solution.py:537
  154.8 10.7 %collective-permute-start.22 = (bf16[64,384]{1,0:T(8,128)(2,1)S(1)}, bf16[64,384]{1,0:T(8,128)(2,1)S(1)}, u32[]{:S(2)}, u32[]{:S(2)}) collective-permute-start(bf16[64,384]{1,0:T(8,128)(2,1)S(1)} %get-tuple-element.63), channel_id=1, source_target_pairs={{0,12},{4,16},{8,20},{12,24},{16,28},{20,0},{24,4},{28,8},{1,13},{... | collective-permute-start | bytes 147464 | tf_op jit(solution)/shard_map/ppermute | solution.py:537
  157.0 8.5 %collective-permute-start.23 = (bf16[64,384]{1,0:T(8,128)(2,1)S(1)}, bf16[64,384]{1,0:T(8,128)(2,1)S(1)}, u32[]{:S(2)}, u32[]{:S(2)}) collective-permute-start(bf16[64,384]{1,0:T(8,128)(2,1)S(1)} %get-tuple-element.64), channel_id=1, source_target_pairs={{0,16},{4,20},{8,24},{12,28},{16,0},{20,4},{24,8},{28,12},{1,17},{... | collective-permute-start | bytes 147464 | tf_op jit(solution)/shard_map/ppermute | solution.py:537
  158.4 7.1 %collective-permute-start.24 = (bf16[64,384]{1,0:T(8,128)(2,1)S(1)}, bf16[64,384]{1,0:T(8,128)(2,1)S(1)}, u32[]{:S(2)}, u32[]{:S(2)}) collective-permute-start(bf16[64,384]{1,0:T(8,128)(2,1)S(1)} %get-tuple-element.65), channel_id=1, source_target_pairs={{0,20},{4,24},{8,28},{12,0},{16,4},{20,8},{24,12},{28,16},{1,21},{... | collective-permute-start | bytes 147464 | tf_op jit(solution)/shard_map/ppermute | solution.py:537
  160.4 5.2 %collective-permute-start.25 = (bf16[64,384]{1,0:T(8,128)(2,1)S(1)}, bf16[64,384]{1,0:T(8,128)(2,1)S(1)}, u32[]{:S(2)}, u32[]{:S(2)}) collective-permute-start(bf16[64,384]{1,0:T(8,128)(2,1)S(1)} %get-tuple-element.66), channel_id=1, source_target_pairs={{0,24},{4,28},{8,0},{12,4},{16,8},{20,12},{24,16},{28,20},{1,25},{... | collective-permute-start | bytes 147464 | tf_op jit(solution)/shard_map/ppermute | solution.py:537
  162.6 4.6 %collective-permute-start.26 = (bf16[64,384]{1,0:T(8,128)(2,1)S(1)}, bf16[64,384]{1,0:T(8,128)(2,1)S(1)}, u32[]{:S(2)}, u32[]{:S(2)}) collective-permute-start(bf16[64,384]{1,0:T(8,128)(2,1)S(1)} %get-tuple-element.67), channel_id=1, source_target_pairs={{0,28},{4,0},{8,4},{12,8},{16,12},{20,16},{24,20},{28,24},{1,29},{... | collective-permute-start | bytes 147464 | tf_op jit(solution)/shard_map/ppermute | solution.py:537
  165.5 3.1 %copy-start.13 = (bf16[352,2048]{1,0:T(8,128)(2,1)}, bf16[352,2048]{1,0:T(8,128)(2,1)S(1)}, u32[]{:S(2)}) copy-start(bf16[352,2048]{1,0:T(8,128)(2,1)S(1)} %slice_dynamic-update-slice_fusion) | copy-start | bytes 4325380
Sparse Core Ops, SparseCore 0:
  11.6 53.6 all-gather.2

commit v2 on v1

--- a/solution.py
+++ b/solution.py
@@ -65,13 +65,13 @@
     out_ref[0] = jnp.dot(both, perm_ref[...], preferred_element_type=F32).astype(BF)
 
 
-def attend(own, halos, images, base, rate, first_query, bounds, label_ref, perm_ref, *refs):
+def attend(own, halos, images, base, rate, first_query, bounds, label_ref, *refs):
     count = len(halos)
-    q_ref, kt_ref, v_ref, chunk_refs = refs[0], refs[1], refs[2], refs[3 : 3 + count]
-    refs = refs[-(9 + count) :]
-    out_ref, kt_s, v_s, scores_s, acc, top, att = refs[:7]
-    raw_s, sems, own_sems = refs[7 : 7 + count], refs[-2], refs[-1]
-    queries, heads = q_ref.shape[:2]
+    perm_hbm, q_hbm, kt_ref, v_ref, chunk_refs = *refs[:4], refs[4 : 4 + count]
+    refs = refs[-(11 + count) :]
+    out_ref, perm_ref, q_ref, kt_s, v_s, scores_s, acc, top, att = refs[:9]
+    raw_s, sems, own_sems = refs[9 : 9 + count], refs[-2], refs[-1]
+    queries, heads = q_ref.shape[0], q_ref.shape[1]
     depth = kt_s.shape[3]
     slots = pl.ds(own[0] - base, len(own))
     chunk_copies = [
@@ -80,7 +80,9 @@
     ]
     kt_copy = pltpu.make_async_copy(kt_ref, kt_s.at[slots], own_sems.at[0])
     v_copy = pltpu.make_async_copy(v_ref, v_s.at[slots], own_sems.at[1])
-    for copy in chunk_copies + [kt_copy, v_copy]:
+    q_copy = pltpu.make_async_copy(q_hbm.at[pl.ds(first_query, queries)], q_ref, own_sems.at[2])
+    perm_copy = pltpu.make_async_copy(perm_hbm, perm_ref, own_sems.at[3])
+    for copy in chunk_copies + [q_copy, kt_copy, v_copy, perm_copy]:
         copy.start()
     for tiles, copy, raw in zip(halos, chunk_copies, raw_s):
         copy.wait()
@@ -89,6 +91,7 @@
             slot = pl.ds(tile - base, 1)
             key_tile(raw[0, :, lanes].astype(F32), label_ref[tile], images, depth, kt_s.at[slot])
             value_tile(raw[1, :, lanes].astype(F32), v_s.at[slot])
+    q_copy.wait()
     kt_copy.wait()
 
     def attend_tile(side, carry):
@@ -144,6 +147,7 @@
         return carry
 
     lax.fori_loop(0, queries, attend_tile, 0)
+    perm_copy.wait()
     for at in range(queries // 2):
         lanes = slice(2 * at * TILE, 2 * (at + 1) * TILE)
         out_ref[:, lanes] = jnp.dot(
@@ -151,20 +155,26 @@
         ).astype(BF)
 
 
-def project(order, last, col_ref, perm_ref, gain_ref, res_ref, wt_ref, mw_ref, *refs):
+def project(order, first, col_ref, gain_ref, perm_hbm, res_ref, wt_ref, mw_ref, *refs):
     count = len(order)
-    att_refs, refs = refs[:count], refs[count:]
-    if last:
-        before_ref = refs[0]
-    layer_ref, out_ref, gathered, layer_s, wt_s, mw_s, merged_s, att_sem, wt_sem, mw_sem = refs[-10:]
+    att_refs = refs[:count]
+    layer_ref, out_ref, gathered, layer_s, res_s, wt_s, mw_s, merged_s, perm_ref = refs[-13:-4]
+    att_sem, wt_sem, res_sem, sems = refs[-4:]
     width = att_refs[0].shape[0]
     full = wt_ref.shape[0]
-    groups = layer_s.shape[1] // 4
+    block = 2 * TILE
+    blocks = layer_s.shape[1] // block
+    groups = block // 4
     col = col_ref[0]
 
-    def wt_copy(part):
+    def part_copies(part):
         rows = pl.ds(pl.multiple_of(part * width, 16), width)
-        return pltpu.make_async_copy(wt_ref.at[rows, :], wt_s.at[rows, :], wt_sem.at[part])
+        return (
+            pltpu.make_async_copy(wt_ref.at[rows, :], wt_s.at[rows, :], wt_sem.at[part]),
+            pltpu.make_async_copy(
+                res_ref.at[part, pl.ds(first, blocks)], res_s.at[part], res_sem.at[part]
+            ),
+        )
 
     att_copies = []
     for part, (bit, att_ref) in enumerate(zip(order, att_refs)):
@@ -172,45 +182,58 @@
         att_copies.append(
             pltpu.make_async_copy(att_ref, gathered.at[pl.ds(row, width), :], att_sem.at[part])
         )
-    mw_copy = pltpu.make_async_copy(mw_ref, mw_s, mw_sem.at[0])
-    for copy in att_copies + [wt_copy(part) for part in range(count)] + [mw_copy] * last:
+    late = [
+        pltpu.make_async_copy(perm_hbm, perm_ref, sems.at[0]),
+        pltpu.make_async_copy(mw_ref, mw_s, sems.at[1]),
+    ]
+    for copy in att_copies:
+        copy.start()
+    for part in range(count):
+        for copy in part_copies(part):
+            copy.start()
+    for copy in late:
         copy.start()
     for copy in att_copies:
         copy.wait()
 
     def project_part(part, carry):
         rows = pl.ds(pl.multiple_of(part * width, 16), width)
-        wt_copy(part).wait()
-        projected = jnp.dot(wt_s[rows, :], gathered[...], preferred_element_type=F32)
-        layer_s[rows, :] = (res_ref[part, 0].astype(F32) + projected).astype(BF)
+        for copy in part_copies(part):
+            copy.wait()
+        for at in range(blocks):
+            lanes = slice(at * block, (at + 1) * block)
+            projected = jnp.dot(wt_s[rows, :], gathered[:, lanes], preferred_element_type=F32)
+            layer_s[rows, lanes] = (res_s[part, at].astype(F32) + projected).astype(BF)
         return carry
 
     lax.fori_loop(0, count, project_part, 0)
+    for copy in late:
+        copy.wait()
     own = pl.ds(pl.multiple_of(col * width, 16), width)
-    layer_ref[...] = lax.dot_general(
-        layer_s[own, :], perm_ref[...], (((1,), (1,)), ((), ())), preferred_element_type=F32
-    ).astype(BF)
-    if last:
-        mw_copy.wait()
-        merged_s[...] = jnp.zeros_like(merged_s)
+    for at in range(blocks):
+        lanes = slice(at * block, (at + 1) * block)
+        layer_ref[:, lanes] = lax.dot_general(
+            layer_s[own, lanes], perm_ref[...], (((1,), (1,)), ((), ())), preferred_element_type=F32
+        ).astype(BF)
+    merged_s[...] = jnp.zeros_like(merged_s)
 
     def merge_part(j, carry):
-        lanes = pl.ds(pl.multiple_of(j * groups, groups), groups)
-        values = layer_s[:, lanes].astype(F32)
-        values = values - jnp.sum(values, axis=0, keepdims=True) / full
-        spread = jnp.sum(jnp.square(values), axis=0, keepdims=True) / full
-        normed = (values * lax.rsqrt(spread + 1e-06) * gain_ref[...]).astype(BF)
-        if last:
-            both = jnp.concatenate([before_ref[:, lanes], normed], axis=1)
-            weights = mw_s[:, pl.ds(pl.multiple_of(j * full, 128), full)]
-            merged_s[...] += jnp.dot(weights, both, preferred_element_type=F32)
-        else:
-            out_ref[:, lanes] = normed
+        columns = []
+        for at in range(blocks):
+            lanes = pl.ds(pl.multiple_of(at * block + j * groups, groups), groups)
+            values = layer_s[:, lanes].astype(F32)
+            values = values - jnp.sum(values, axis=0, keepdims=True) / full
+            spread = jnp.sum(jnp.square(values), axis=0, keepdims=True) / full
+            normed = (values * lax.rsqrt(spread + 1e-06) * gain_ref[...]).astype(BF)
+            columns.append(normed)
+        weights = mw_s[:, pl.ds(pl.multiple_of(j * full, 128), full)]
+        merged_s[...] += jnp.dot(
+            weights, jnp.concatenate(columns, axis=1), preferred_element_type=F32
+        )
         return carry
 
     lax.fori_loop(0, 4, merge_part, 0)
-    if last:
-        out_ref[...] = merged_s[...].astype(BF)
+    out_ref[...] = merged_s[...].astype(BF)
 
 
 def outgoing(pieces, slot_ref, place_ref, *refs):
@@ -251,7 +274,7 @@
     own_tiles = tokens // TILE
     far_tiles = reach // TILE
     half = own_tiles // 2
-    plan = [1] * half
+    plan = [half // 2, half - half // 2]
     begins = [sum(plan[:s]) for s in range(len(plan))]
     stages = len(plan)
     depth = round_up(HEAD_DIM + images, 128)
@@ -304,7 +327,9 @@
         return jnp.where(block < inner, near, mirrored)
 
     def stage_order(tile):
-        return jnp.where(tile >= half, 2 * (tile - half) + 1, 2 * (half - 1 - tile))
+        mirrored = jnp.where(tile >= half, 2 * (tile - half) + 1, 2 * (half - 1 - tile))
+        near = tile - (half - inner)
+        return jnp.where((near >= 0) & (near < 2 * inner), near, mirrored)
 
     at = jnp.arange(2 * TILE, dtype=jnp.int32)
     perm = (((at % 4) * (TILE // 2) + at // 4)[:, None] == at[None, :]).astype(BF)
@@ -351,6 +376,7 @@
     )(perm, residual_in, residual_in)
     residual = lax.all_gather(residual, "col", axis=0)
     tile_order = [pair_tile(block, which) for block in range(blocks) for which in range(2)]
+    out_weight_t = jnp.transpose(out_weight)
     key_bounds = jnp.stack([low, high])
     key_bounds = jnp.stack([key_bounds[:, tile] for tile in tile_order], axis=1)
     gain = merge_gain[:, None]
@@ -380,53 +406,41 @@
 
     def run_project(stage):
         size = plan[stage]
-        last = stage % 2 == 1
-        before = [parts[stage - 1]] if last else []
-        columns = 2 * size * TILE
+        columns, merged_columns = 2 * size * TILE, size * TILE // 2
         after = [gathers[-1][0]] + layers[-1:]
         layer, part = pl.pallas_call(
-            functools.partial(project, order, last),
+            functools.partial(project, order, begins[stage]),
             grid=(1,),
-            in_specs=[
-                smem_spec,
-                vmem_spec,
-                vmem_spec,
-                pl.BlockSpec(
-                    (cols, size, width, 2 * TILE),
-                    functools.partial(lambda s, i: (0, s, 0, 0), begins[stage] // size),
-                ),
-                any_spec,
-                any_spec,
-            ]
-            + [any_spec] * cols
-            + [vmem_spec] * last
-            + [any_spec] * len(after),
+            in_specs=[smem_spec, vmem_spec] + [any_spec] * (4 + cols + len(after)),
             out_specs=[vmem_spec, vmem_spec],
             out_shape=[
                 jax.ShapeDtypeStruct((width, columns), BF),
-                jax.ShapeDtypeStruct((width, TILE) if last else (full, columns), BF),
+                jax.ShapeDtypeStruct((width, merged_columns), BF),
             ],
             scratch_shapes=[
                 pltpu.VMEM((full, columns), BF),
                 pltpu.VMEM((full, columns), BF),
+                pltpu.VMEM((cols, size, width, 2 * TILE), BF),
                 pltpu.VMEM((full, full), BF),
                 pltpu.VMEM((width, 4 * full), BF),
-                pltpu.VMEM((width, TILE), F32),
+                pltpu.VMEM((width, merged_columns), F32),
+                pltpu.VMEM(perm.shape, BF),
                 pltpu.SemaphoreType.DMA((cols,)),
                 pltpu.SemaphoreType.DMA((cols,)),
-                pltpu.SemaphoreType.DMA((1,)),
+                pltpu.SemaphoreType.DMA((cols,)),
+                pltpu.SemaphoreType.DMA((2,)),
             ],
             compiler_params=params(62),
             cost_estimate=cost((4 + 4 * size) * 1e9, 1e5),
             name="project",
-        )(col_value, perm, gain, residual, out_weight_t, merge_weight, *gathers[stage], *before, *after)
+        )(col_value, gain, perm, residual, out_weight_t, merge_weight, *gathers[stage], *after)
         layers.append(layer)
         parts.append(part)
 
     for stage in range(stages):
+        size, near = plan[stage], begins[stage]
         if stage + 1 < stages:
             send_chunk(stage + 1, (lefts[stage], rights[stage]))
-        size, near = plan[stage], begins[stage]
         own = list(range(far_tiles, far_tiles + own_tiles))
         base_tile = far_tiles - near - size
         tiles = own_tiles + 2 * (near + size)
@@ -436,23 +450,16 @@
             halos.append(list(range(far_tiles - outer_edge, far_tiles - inner_edge)))
             halos.append([far_tiles + own_tiles + at for at in range(inner_edge, outer_edge)])
             chunks += [lefts[before], rights[before]]
-        after = [g[0] for g in gathers[-1:]] + layers[-1:]
+        after = [gathers[-1][0] if gathers else out_weight_t]
         attended = pl.pallas_call(
             functools.partial(attend, own, halos, images, base_tile, rate, 2 * near),
             grid=(1,),
-            in_specs=[
-                smem_spec,
-                vmem_spec,
-                vmem_spec,
-                pl.BlockSpec(
-                    (2 * size, heads, depth, TILE),
-                    functools.partial(lambda s, i: (s, 0, 0, 0), near // size),
-                ),
-            ]
-            + [any_spec] * (2 + len(chunks) + len(after)),
+            in_specs=[smem_spec, vmem_spec] + [any_spec] * (4 + len(chunks) + len(after)),
             out_specs=vmem_spec,
             out_shape=jax.ShapeDtypeStruct((width, 2 * size * TILE), BF),
             scratch_shapes=[
+                pltpu.VMEM(perm.shape, BF),
+                pltpu.VMEM((2 * size, heads, depth, TILE), BF),
                 pltpu.VMEM((tiles,) + kt_shape, BF),
                 pltpu.VMEM((tiles,) + v_shape, BF),
                 pltpu.VMEM((2 * far_tiles + 1, heads, TILE, TILE), F32),
@@ -461,7 +468,7 @@
                 pltpu.VMEM((width, 2 * size * TILE), BF),
             ]
             + [pltpu.VMEM(chunk.shape, BF) for chunk in chunks]
-            + [pltpu.SemaphoreType.DMA((len(chunks),)), pltpu.SemaphoreType.DMA((2,))],
+            + [pltpu.SemaphoreType.DMA((len(chunks),)), pltpu.SemaphoreType.DMA((4,))],
             compiler_params=params(62),
             cost_estimate=cost((5 + 4 * size) * 1e9, 1e5),
             name="attend",
@@ -469,15 +476,10 @@
 
         gathers.append([attended])
         spread_pieces(stage, bits[:1], None)
-        if stage == 0:
-            ready_weight, _ = lax.optimization_barrier((out_weight, attended))
-            out_weight_t = jnp.transpose(ready_weight)
-        if stage == 1:
-            spread_pieces(0, bits[1:], attended)
-        if stage >= 1:
-            run_project(stage - 1)
-            spread_pieces(stage, bits[1:], layers[stage - 1])
-    run_project(stages - 1)
+    spread_pieces(0, bits[1:], gathers[1][0])
+    run_project(0)
+    spread_pieces(1, bits[1:], layers[0])
+    run_project(1)
 
     tiles_out = [None] * own_tiles
     for stage in range(stages):
@@ -502,18 +504,18 @@
     away = (owner - row_id) % rows
     info = jnp.stack([away * share + rank, place // base, place % base])
     info = info.reshape(3, own_tiles, piece_groups)
-    halves = stages // 2
+    merges = [list(range(b, b + n)) for b, n in zip(begins, plan)]
     info = jnp.stack(
         [
             jnp.concatenate(
                 [
                     info[:, pair_tile(block, which)]
-                    for block in (2 * h, 2 * h + 1)
+                    for block in merge
                     for which in range(2)
                 ],
                 axis=1,
             )
-            for h in range(halves)
+            for merge in merges
         ],
         axis=1,
     )
@@ -522,7 +524,7 @@
     places = jnp.concatenate(
         [
             jnp.stack([info[1], info[2]], axis=1).astype(BF),
-            jnp.zeros((halves, wide - width - 2, 4 * piece_groups), BF),
+            jnp.zeros((len(merges), wide - width - 2, 4 * piece_groups), BF),
         ],
         axis=1,
     )
@@ -532,7 +534,7 @@
         compiler_params=params(16),
         cost_estimate=cost(1e9, 1e5),
         name="outgoing",
-    )(slots, places, *parts[1::2])
+    )(slots, places, *parts)
     received = [sent[0]] + [
         lax.ppermute(sent[step], "row", [(i, (i + step) % rows) for i in range(rows)])
         for step in range(1, rows)

time: 175 us -> 163 us (0.931); the launches traced: 175 us -> 161 us
  Pallas kernels: 87.5 us -> 62.2 us
  waiting for transfers between devices: 9.88 us -> 34.9 us
  starting transfers between devices: 39.9 us -> 28.3 us
  local copies, waits for them, and re-layouts: 22.4 us -> 20.5 us
    ppermute x4 -> x2, waiting for transfers between devices: 0.51 us -> 25.2 us  [send_chunk(): lefts.append(lax.ppermute(tail, 'row', forward))]
    pallas_call x4 -> x2, Pallas kernels: 45.1 us -> 30.1 us  [run_project(): pl.pallas_call(functools.partial(project, order, begins[stage]), grid=(1,...]
    pallas_call x4 -> x2, Pallas kernels: 36 us -> 25.8 us  [body(): pl.pallas_call(functools.partial(attend, own, halos, images, base_tile, r...]
    ppermute x4 -> x2, starting transfers between devices: 17 us -> 6.75 us  [send_chunk(): rights.append(lax.ppermute(head, 'row', backward))]
    optimization_barrier x1 -> x0, local copies, waits for them, and re-layouts: 6.28 us -> none  [body(): ready_weight, _ = lax.optimization_barrier((out_weight, attended))]
    unnamed x66 -> x47, local copies, waits for them, and re-layouts: 10 us -> 15.2 us
    ppermute x12 -> x6, starting transfers between devices: 7.47 us -> 4.43 us  [spread_pieces(): pieces = pieces + [lax.ppermute(piece, 'col', pairs) for piece in sources]]
    ppermute x4 -> x2, waiting for transfers between devices: 5.69 us -> 4.57 us  [send_chunk(): rights.append(lax.ppermute(head, 'row', backward))]
  transfers between devices with their start and end apart: 28 -> 18, of which waited for: 8 -> 10; matrix products, arithmetic and copies ran while one was open for 7% -> 7% of each run, Pallas kernels for 40% -> 26%
where the time goes in v2:
time: 163 us; the launch traced here: 161 us
  Pallas kernels  62.2 us (38%)
  waiting for transfers between devices  34.9 us (21%)
  starting transfers between devices  28.3 us (17%)
  local copies, waits for them, and re-layouts  20.5 us (13%)
  between operations  14.4 us (9%)
    pallas_call x2, Pallas kernels, run_project(): pl.pallas_call(functools.partial(project, order, begins[stage]), grid=(1,...  30.1 us
    pallas_call x2, Pallas kernels, body(): pl.pallas_call(functools.partial(attend, own, halos, images, base_tile, r...  25.8 us
    ppermute x2, waiting for transfers between devices, send_chunk(): lefts.append(lax.ppermute(tail, 'row', forward))  25.2 us
    unnamed x47, local copies, waits for them, and re-layouts  15.2 us
    ppermute x7, starting transfers between devices, body(): lax.ppermute(sent[step], 'row', [(i, (i + step) % rows) for i in range(ro...  12.9 us
    ppermute x2, starting transfers between devices, send_chunk(): rights.append(lax.ppermute(head, 'row', backward))  6.75 us
    ppermute x2, waiting for transfers between devices, send_chunk(): rights.append(lax.ppermute(head, 'row', backward))  4.57 us
    ppermute x6, starting transfers between devices, spread_pieces(): pieces = pieces + [lax.ppermute(piece, 'col', pairs) for piece in sources]  4.43 us
  transfers between devices with their start and end apart: 18, of which 10 were waited for; matrix products, arithmetic and copies ran while one was open for 7% of the time, Pallas kernels for 26%

profile of v2, /device:TPU:0, one launch (start us, length us, event | category | flops | bytes accessed | tf_op | source)
XLA Modules:
  0.0 161.4 jit_solution(14848593338593522559)
XLA Ops:
  7.2 0.0 all-gather.3.cloned.1.call-start
  7.2 1.5 fusion.23
  8.8 0.2 fusion.perm_ref.refs_0_.perm_hbm
  8.9 0.1 copy-done.3
  9.0 2.7 %reorder_residual.1 = bf16[4,352,512]{2,1,0:T(8,128)(2,1)} custom-call(bf16[512,512]{1,0:T(8,128)(2,1)S(1)} %fusion.perm_ref.refs_0_.perm_hbm, bf16[352,2048]{1,0:T(8,128)(2,1)S(1)} %copy-done.3, bf16[352,2048]{1,0:T(8,128)(2,1)S(1)} %copy-done.3), custom_call_target="tpu_custom_call" | custom-call | flops 2000000000 | bytes 100000 | tf_op jit(solution)/shard_map/reorder_residual/pallas_call | solution.py:363
  11.8 0.0 all-gather.3.cloned.1.call-update
  11.8 3.0 %collective-permute-start = (bf16[2,352,512]{2,1,0:T(8,128)(2,1)S(1)}, bf16[2,352,512]{2,1,0:T(8,128)(2,1)S(1)}, u32[]{:S(2)}, u32[]{:S(2)}) collective-permute-start(bf16[2,352,512]{2,1,0:T(8,128)(2,1)S(1)} %get-tuple-element.51), channel_id=1, source_target_pairs={{0,4},{4,8},{8,12},{12,16},{16,20},{20,24},{24,28},{28,0},{1,5},{5... | collective-permute-start | bytes 2162696 | tf_op jit(solution)/shard_map/ppermute | solution.py:296
  14.8 3.1 %collective-permute-start.1 = (bf16[2,352,512]{2,1,0:T(8,128)(2,1)S(1)}, bf16[2,352,512]{2,1,0:T(8,128)(2,1)}, u32[]{:S(2)}, u32[]{:S(2)}) collective-permute-start(bf16[2,352,512]{2,1,0:T(8,128)(2,1)S(1)} %get-tuple-element.50), channel_id=1, source_target_pairs={{4,0},{8,4},{12,8},{16,12},{20,16},{24,20},{28,24},{0,28},{5,1},{9... | collective-permute-start | bytes 2162696 | tf_op jit(solution)/shard_map/ppermute | solution.py:297
  17.9 0.1 copy.34
  18.0 0.1 reduce-window.8
  18.0 0.1 multiply_reduce_fusion
  18.1 0.2 select_reduce_fusion.1
  18.4 0.1 fusion.24
  18.5 0.1 slice.85
  18.6 6.4 %copy.33 = bf16[1408,1408]{0,1:T(8,128)(2,1)} copy(bf16[1408,1408]{1,0:T(8,128)(2,1)} %param.9) | data formatting | bytes 7929856 | tf_op args[2]
  24.9 0.7 stack.34.bounds
  25.6 0.1 convert_reduce_fusion.1
  25.8 2.2 %copy-done = bf16[3,352,2048]{2,1,0:T(8,128)(2,1)S(1)} copy-done((bf16[3,352,2048]{2,1,0:T(8,128)(2,1)S(1)}, bf16[3,352,2048]{2,1,0:T(8,128)(2,1)}, u32[]{:S(2)}) %copy-start) | copy-done | bytes 4325400
  28.0 1.8 %prepare_own.1 = (bf16[8,4,128,256]{3,2,1,0:T(8,128)(2,1)S(1)}, bf16[8,4,256,128]{3,2,1,0:T(8,128)(2,1)S(1)}, bf16[8,4,96,256]{3,2,1,0:T(8,128)(2,1)S(1)}) custom-call(s32[16,1,256]{2,1,0:T(1,128)S(1)} %compare_select_fusion.label_ref, bf16[3,352,2048]{2,1,0:T(8,128)(2,1)S(1)} %copy-done), custom_call_target="tpu_custom_call" | custom-call | flops 2000000000 | bytes 100000 | tf_op jit(solution)/shard_map/prepare_own/pallas_call | solution.py:339
  29.9 1.4 copy-done.5
  31.3 1.1 copy-done.6
  32.4 13.2 %collective-permute-done.refs_4_ = bf16[2,352,512]{2,1,0:T(8,128)(2,1)S(1)} collective-permute-done((bf16[2,352,512]{2,1,0:T(8,128)(2,1)S(1)}, bf16[2,352,512]{2,1,0:T(8,128)(2,1)S(1)}, u32[]{:S(2)}, u32[]{:S(2)}) %collective-permute-start) | collective-permute-done | bytes 720928 | tf_op jit(solution)/shard_map/ppermute | solution.py:296
  45.6 0.9 copy-done.16
  46.5 1.4 collective-permute-done.1.refs_5_
  47.9 1.4 fusion.22
  49.4 1.1 collective-permute-start.2
  50.5 3.6 %collective-permute-start.3 = (bf16[2,352,512]{2,1,0:T(8,128)(2,1)S(1)}, bf16[2,352,512]{2,1,0:T(8,128)(2,1)}, u32[]{:S(2)}, u32[]{:S(2)}) collective-permute-start(bf16[2,352,512]{2,1,0:T(8,128)(2,1)S(1)} %get-tuple-element.48), channel_id=1, source_target_pairs={{4,0},{8,4},{12,8},{16,12},{20,16},{24,20},{28,24},{0,28},{5,1},{9... | collective-permute-start | bytes 2162696 | tf_op jit(solution)/shard_map/ppermute | solution.py:297
  54.1 12.7 %attend.2.refs_8_.refs_0_ = bf16[352,1024]{1,0:T(8,128)(2,1)} custom-call(s32[2,8]{1,0:T(2,128)} %stack.34.bounds, s32[16,1,256]{2,1,0:T(1,128)} %copy-done.2, bf16[512,512]{1,0:T(8,128)(2,1)} %copy-done.1, bf16[8,4,128,256]{3,2,1,0:T(8,128)(2,1)} %copy-done.4, bf16[8,4,256,128]{3,2,1,0:T(8,128)(2,1)} %copy-done.5, bf16[8,4,96,256]{3,2,1,0:T(8,128)(2,1)} %copy-done.6, ...), custom_call_target="tpu_custom_call" | custom-call | flops 12999999488 | bytes 100000 | tf_op jit(solution)/shard_map/attend/pallas_call | solution.py:454
  66.8 1.7 %collective-permute-start.5 = (bf16[352,1024]{1,0:T(8,128)(2,1)}, bf16[352,1024]{1,0:T(8,128)(2,1)}, u32[]{:S(2)}, u32[]{:S(2)}) collective-permute-start(bf16[352,1024]{1,0:T(8,128)(2,1)} %attend.2.refs_8_.refs_0_), channel_id=1, source_target_pairs={{0,2},{1,3},{2,0},{3,1},{4,6},{5,7},{6,4},{7,5},{8,10},{9,11},{10,... | collective-permute-start | bytes 2162696 | tf_op jit(solution)/shard_map/ppermute | solution.py:404
  68.5 12.0 %collective-permute-done.2.refs_6_ = bf16[2,352,512]{2,1,0:T(8,128)(2,1)} collective-permute-done((bf16[2,352,512]{2,1,0:T(8,128)(2,1)S(1)}, bf16[2,352,512]{2,1,0:T(8,128)(2,1)}, u32[]{:S(2)}, u32[]{:S(2)}) %collective-permute-start.2) | collective-permute-done | bytes 720928 | tf_op jit(solution)/shard_map/ppermute | solution.py:296
  80.6 3.2 %collective-permute-done.3.refs_7_ = bf16[2,352,512]{2,1,0:T(8,128)(2,1)} collective-permute-done((bf16[2,352,512]{2,1,0:T(8,128)(2,1)S(1)}, bf16[2,352,512]{2,1,0:T(8,128)(2,1)}, u32[]{:S(2)}, u32[]{:S(2)}) %collective-permute-start.3) | collective-permute-done | bytes 720928 | tf_op jit(solution)/shard_map/ppermute | solution.py:297
  83.7 13.1 %attend.3.refs_4_.refs_0_ = bf16[352,1024]{1,0:T(8,128)(2,1)} custom-call(s32[2,8]{1,0:T(2,128)} %stack.34.bounds, s32[16,1,256]{2,1,0:T(1,128)} %copy-done.2, bf16[512,512]{1,0:T(8,128)(2,1)} %copy-done.1, bf16[8,4,128,256]{3,2,1,0:T(8,128)(2,1)} %copy-done.4, bf16[8,4,256,128]{3,2,1,0:T(8,128)(2,1)} %copy-done.5, bf16[8,4,96,256]{3,2,1,0:T(8,128)(2,1)} %copy-done.6, ...), custom_call_target="tpu_custom_call" | custom-call | flops 12999999488 | bytes 100000 | tf_op jit(solution)/shard_map/attend/pallas_call | solution.py:454
  96.9 0.1 collective-permute-start.6
  96.9 0.5 collective-permute-start.7
  97.4 1.1 broadcast_in_dim.42.gain_ref
  98.6 0.2 convert_reduce_fusion
  98.9 0.1 stack.35
  98.9 0.1 stack.36
  99.0 0.1 stack.37
  99.1 1.6 %collective-permute-start.4 = (bf16[352,1024]{1,0:T(8,128)(2,1)}, bf16[352,1024]{1,0:T(8,128)(2,1)S(1)}, u32[]{:S(2)}, u32[]{:S(2)}) collective-permute-start(bf16[352,1024]{1,0:T(8,128)(2,1)} %attend.3.refs_4_.refs_0_), channel_id=1, source_target_pairs={{0,2},{1,3},{2,0},{3,1},{4,6},{5,7},{6,4},{7,5},{8,10},{9,11},{10,... | collective-permute-start | bytes 2162696 | tf_op jit(solution)/shard_map/ppermute | solution.py:404
  100.8 0.0 all-gather.3.cloned.1.call-done
  100.8 0.8 copy-done.19
  101.6 0.3 copy-done.20
  101.9 15.1 %project.2 = (bf16[352,1024]{1,0:T(8,128)(2,1)}, bf16[352,256]{1,0:T(8,128)(2,1)}) custom-call(s32[1]{0:T(128)} %bitcast.col_ref, f32[1408,1]{1,0:T(8,128)} %broadcast_in_dim.42.gain_ref, bf16[512,512]{1,0:T(8,128)(2,1)} %copy-done.1, bf16[4,4,352,512]{3,2,1,0:T(8,128)(2,1)} %bitcast.56, bf16[1408,1408]{1,0:T(8,128)(2,1)} %bitcast.52, ...), custom_call_target="tpu_custom_call" | custom-call | flops 12000000000 | bytes 100000 | tf_op jit(solution)/shard_map/project/pallas_call | solution.py:411
  117.0 0.5 collective-permute-done.4.refs_1_
  117.5 0.5 collective-permute-start.9
  118.1 0.1 add_bitcast_fusion
  118.2 1.9 %collective-permute-done.8.refs_2_ = bf16[352,1024]{1,0:T(8,128)(2,1)S(1)} collective-permute-done((bf16[352,1024]{1,0:T(8,128)(2,1)S(1)}, bf16[352,1024]{1,0:T(8,128)(2,1)S(1)}, u32[]{:S(2)}, u32[]{:S(2)}) %collective-permute-start.8) | collective-permute-done | bytes 720928 | tf_op jit(solution)/shard_map/ppermute | solution.py:404
  120.1 0.9 copy-done.18
  120.9 15.0 %project.3 = (bf16[352,1024]{1,0:T(8,128)(2,1)}, bf16[352,256]{1,0:T(8,128)(2,1)}) custom-call(s32[1]{0:T(128)} %bitcast.col_ref, f32[1408,1]{1,0:T(8,128)} %broadcast_in_dim.42.gain_ref, bf16[512,512]{1,0:T(8,128)(2,1)} %copy-done.1, bf16[4,4,352,512]{3,2,1,0:T(8,128)(2,1)} %bitcast.57, bf16[1408,1408]{1,0:T(8,128)(2,1)} %bitcast.53, ...), custom_call_target="tpu_custom_call" | custom-call | flops 12000000000 | bytes 100000 | tf_op jit(solution)/shard_map/project/pallas_call | solution.py:411
  136.0 0.9 copy-done.8
  136.9 0.5 outgoing.1
  137.4 0.1 collective-permute-start.10
  137.4 4.0 %collective-permute-start.11 = (bf16[64,384]{1,0:T(8,128)(2,1)S(1)}, bf16[64,384]{1,0:T(8,128)(2,1)S(1)}, u32[]{:S(2)}, u32[]{:S(2)}) collective-permute-start(bf16[64,384]{1,0:T(8,128)(2,1)S(1)} %get-tuple-element.40), channel_id=1, source_target_pairs={{0,8},{4,12},{8,16},{12,20},{16,24},{20,28},{24,0},{28,4},{1,9},{5... | collective-permute-start | bytes 147464 | tf_op jit(solution)/shard_map/ppermute | solution.py:539
  141.4 3.5 %collective-permute-start.12 = (bf16[64,384]{1,0:T(8,128)(2,1)S(1)}, bf16[64,384]{1,0:T(8,128)(2,1)S(1)}, u32[]{:S(2)}, u32[]{:S(2)}) collective-permute-start(bf16[64,384]{1,0:T(8,128)(2,1)S(1)} %get-tuple-element.41), channel_id=1, source_target_pairs={{0,12},{4,16},{8,20},{12,24},{16,28},{20,0},{24,4},{28,8},{1,13},{... | collective-permute-start | bytes 147464 | tf_op jit(solution)/shard_map/ppermute | solution.py:539
  144.9 0.2 collective-permute-start.13
  145.1 2.2 %collective-permute-start.14 = (bf16[64,384]{1,0:T(8,128)(2,1)S(1)}, bf16[64,384]{1,0:T(8,128)(2,1)S(1)}, u32[]{:S(2)}, u32[]{:S(2)}) collective-permute-start(bf16[64,384]{1,0:T(8,128)(2,1)S(1)} %get-tuple-element.43), channel_id=1, source_target_pairs={{0,20},{4,24},{8,28},{12,0},{16,4},{20,8},{24,12},{28,16},{1,21},{... | collective-permute-start | bytes 147464 | tf_op jit(solution)/shard_map/ppermute | solution.py:539
  147.5 1.6 %collective-permute-start.15 = (bf16[64,384]{1,0:T(8,128)(2,1)S(1)}, bf16[64,384]{1,0:T(8,128)(2,1)S(1)}, u32[]{:S(2)}, u32[]{:S(2)}) collective-permute-start(bf16[64,384]{1,0:T(8,128)(2,1)S(1)} %get-tuple-element.44), channel_id=1, source_target_pairs={{0,24},{4,28},{8,0},{12,4},{16,8},{20,12},{24,16},{28,20},{1,25},{... | collective-permute-start | bytes 147464 | tf_op jit(solution)/shard_map/ppermute | solution.py:539
  149.1 1.4 collective-permute-start.16
  150.5 0.3 collective-permute-done.13.refs_4_
  150.9 0.4 collective-permute-done.14.refs_5_
  151.3 1.5 collective-permute-done.15.refs_6_
  152.7 0.5 collective-permute-done.16.refs_7_
  153.2 1.3 incoming.1
  (61 shorter events, 0.4 us)
Async XLA Ops:
  7.2 93.7 %all-gather.3.cloned.1.call-start = ((), (), s32[]{:S(2)}) async-start(), calls=%async_computation | async-start | bytes 7208960 | tf_op jit(solution)/shard_map/all_gather | solution.py:377
  7.2 1.8 %copy-start.3 = (bf16[352,2048]{1,0:T(8,128)(2,1)S(1)}, bf16[352,2048]{1,0:T(8,128)(2,1)}, u32[]{:S(2)}) copy-start(bf16[352,2048]{1,0:T(8,128)(2,1)} %high_ref) | copy-start | bytes 4325380
  8.9 2.8 %copy-start.1 = (bf16[512,512]{1,0:T(8,128)(2,1)}, bf16[512,512]{1,0:T(8,128)(2,1)S(1)}, u32[]{:S(2)}) copy-start(bf16[512,512]{1,0:T(8,128)(2,1)S(1)} %fusion.perm_ref.refs_0_.perm_hbm) | copy-start | bytes 1572868
  11.7 6.1 %copy-start.14 = (s32[32]{0:T(128)S(1)}, s32[32]{0:T(128)}, u32[]{:S(2)}) copy-start(s32[32]{0:T(128)} %param.12) | copy-start | bytes 388
  11.8 33.8 %collective-permute-start = (bf16[2,352,512]{2,1,0:T(8,128)(2,1)S(1)}, bf16[2,352,512]{2,1,0:T(8,128)(2,1)S(1)}, u32[]{:S(2)}, u32[]{:S(2)}) collective-permute-start(bf16[2,352,512]{2,1,0:T(8,128)(2,1)S(1)} %get-tuple-element.51), channel_id=1, source_target_pairs={{0,4},{4,8},{8,12},{12,16},{16,20},{20,24},{24,28},{28,0},{1,5},{5... | collective-permute-start | bytes 2162696 | tf_op jit(solution)/shard_map/ppermute | solution.py:296
  14.8 33.1 %collective-permute-start.1 = (bf16[2,352,512]{2,1,0:T(8,128)(2,1)S(1)}, bf16[2,352,512]{2,1,0:T(8,128)(2,1)}, u32[]{:S(2)}, u32[]{:S(2)}) collective-permute-start(bf16[2,352,512]{2,1,0:T(8,128)(2,1)S(1)} %get-tuple-element.50), channel_id=1, source_target_pairs={{4,0},{8,4},{12,8},{16,12},{20,16},{24,20},{28,24},{0,28},{5,1},{9... | collective-permute-start | bytes 2162696 | tf_op jit(solution)/shard_map/ppermute | solution.py:297
  25.8 2.2 %copy-start = (bf16[3,352,2048]{2,1,0:T(8,128)(2,1)S(1)}, bf16[3,352,2048]{2,1,0:T(8,128)(2,1)}, u32[]{:S(2)}) copy-start(bf16[3,352,2048]{2,1,0:T(8,128)(2,1)} %qkv_ref) | copy-start | bytes 12976132
  28.0 1.8 %copy-start.2 = (s32[16,1,256]{2,1,0:T(1,128)}, s32[16,1,256]{2,1,0:T(1,128)S(1)}, u32[]{:S(2)}) copy-start(s32[16,1,256]{2,1,0:T(1,128)S(1)} %compare_select_fusion.label_ref) | copy-start | bytes 49156
  29.9 1.4 copy-start.5
  31.3 1.2 copy-start.6
  32.4 16.9 %copy-start.4 = (bf16[8,4,128,256]{3,2,1,0:T(8,128)(2,1)}, bf16[8,4,128,256]{3,2,1,0:T(8,128)(2,1)S(1)}, u32[]{:S(2)}) copy-start(bf16[8,4,128,256]{3,2,1,0:T(8,128)(2,1)S(1)} %get-tuple-element.26.refs_1_) | copy-start | bytes 6291460
  45.6 0.9 copy-start.16
  49.4 31.2 %collective-permute-start.2 = (bf16[2,352,512]{2,1,0:T(8,128)(2,1)S(1)}, bf16[2,352,512]{2,1,0:T(8,128)(2,1)}, u32[]{:S(2)}, u32[]{:S(2)}) collective-permute-start(bf16[2,352,512]{2,1,0:T(8,128)(2,1)S(1)} %get-tuple-element.49), channel_id=1, source_target_pairs={{0,4},{4,8},{8,12},{12,16},{16,20},{20,24},{24,28},{28,0},{1,5},{5... | collective-permute-start | bytes 2162696 | tf_op jit(solution)/shard_map/ppermute | solution.py:296
  50.5 33.2 %collective-permute-start.3 = (bf16[2,352,512]{2,1,0:T(8,128)(2,1)S(1)}, bf16[2,352,512]{2,1,0:T(8,128)(2,1)}, u32[]{:S(2)}, u32[]{:S(2)}) collective-permute-start(bf16[2,352,512]{2,1,0:T(8,128)(2,1)S(1)} %get-tuple-element.48), channel_id=1, source_target_pairs={{4,0},{8,4},{12,8},{16,12},{20,16},{24,20},{28,24},{0,28},{5,1},{9... | collective-permute-start | bytes 2162696 | tf_op jit(solution)/shard_map/ppermute | solution.py:297
  66.8 30.6 %copy-start.12 = (f32[1408]{0:T(1024)S(1)}, f32[1408]{0:T(1024)}, u32[]{:S(2)}) copy-start(f32[1408]{0:T(1024)} %param.11) | copy-start | bytes 16900
  66.8 31.8 %copy-start.13 = (s32[512]{0:T(512)S(1)}, s32[512]{0:T(512)}, u32[]{:S(2)}) copy-start(s32[512]{0:T(512)} %param.13) | copy-start | bytes 6148
  66.8 30.0 %collective-permute-start.5 = (bf16[352,1024]{1,0:T(8,128)(2,1)}, bf16[352,1024]{1,0:T(8,128)(2,1)}, u32[]{:S(2)}, u32[]{:S(2)}) collective-permute-start(bf16[352,1024]{1,0:T(8,128)(2,1)} %attend.2.refs_8_.refs_0_), channel_id=1, source_target_pairs={{0,2},{1,3},{2,0},{3,1},{4,6},{5,7},{6,4},{7,5},{8,10},{9,11},{10,... | collective-permute-start | bytes 2162696 | tf_op jit(solution)/shard_map/ppermute | solution.py:404
  96.9 3.9 %collective-permute-start.6 = (bf16[352,1024]{1,0:T(8,128)(2,1)}, bf16[352,1024]{1,0:T(8,128)(2,1)S(1)}, u32[]{:S(2)}, u32[]{:S(2)}) collective-permute-start(bf16[352,1024]{1,0:T(8,128)(2,1)} %attend.2.refs_8_.refs_0_), channel_id=1, source_target_pairs={{0,1},{1,0},{2,3},{3,2},{4,5},{5,4},{6,7},{7,6},{8,9},{9,8},{10,11... | collective-permute-start | bytes 2162696 | tf_op jit(solution)/shard_map/ppermute | solution.py:404
  96.9 3.9 %collective-permute-start.7 = (bf16[352,1024]{1,0:T(8,128)(2,1)}, bf16[352,1024]{1,0:T(8,128)(2,1)S(1)}, u32[]{:S(2)}, u32[]{:S(2)}) collective-permute-start(bf16[352,1024]{1,0:T(8,128)(2,1)} %collective-permute-done.5.refs_1_), channel_id=1, source_target_pairs={{0,1},{1,0},{2,3},{3,2},{4,5},{5,4},{6,7},{7,6},{8,9},{9,8},{10,11... | collective-permute-start | bytes 2162696 | tf_op jit(solution)/shard_map/ppermute | solution.py:404
  99.1 18.4 %collective-permute-start.4 = (bf16[352,1024]{1,0:T(8,128)(2,1)}, bf16[352,1024]{1,0:T(8,128)(2,1)S(1)}, u32[]{:S(2)}, u32[]{:S(2)}) collective-permute-start(bf16[352,1024]{1,0:T(8,128)(2,1)} %attend.3.refs_4_.refs_0_), channel_id=1, source_target_pairs={{0,2},{1,3},{2,0},{3,1},{4,6},{5,7},{6,4},{7,5},{8,10},{9,11},{10,... | collective-permute-start | bytes 2162696 | tf_op jit(solution)/shard_map/ppermute | solution.py:404
  100.8 0.9 copy-start.19
  100.8 1.1 copy-start.20
  101.9 15.6 %copy-start.15 = (bf16[352,1024]{1,0:T(8,128)(2,1)S(1)}, bf16[352,1024]{1,0:T(8,128)(2,1)}, u32[]{:S(2)}) copy-start(bf16[352,1024]{1,0:T(8,128)(2,1)} %attend.3.refs_4_.refs_0_) | copy-start | bytes 2162692
  117.5 3.4 %copy-start.17 = (bf16[352,1024]{1,0:T(8,128)(2,1)}, bf16[352,1024]{1,0:T(8,128)(2,1)S(1)}, u32[]{:S(2)}) copy-start(bf16[352,1024]{1,0:T(8,128)(2,1)S(1)} %collective-permute-done.4.refs_1_) | copy-start | bytes 2162692
  117.5 2.5 %collective-permute-start.8 = (bf16[352,1024]{1,0:T(8,128)(2,1)S(1)}, bf16[352,1024]{1,0:T(8,128)(2,1)S(1)}, u32[]{:S(2)}, u32[]{:S(2)}) collective-permute-start(bf16[352,1024]{1,0:T(8,128)(2,1)S(1)} %copy-done.15), channel_id=1, source_target_pairs={{0,1},{1,0},{2,3},{3,2},{4,5},{5,4},{6,7},{7,6},{8,9},{9,8},{10,11... | collective-permute-start | bytes 2162696 | tf_op jit(solution)/shard_map/ppermute | solution.py:404
  117.5 3.4 %collective-permute-start.9 = (bf16[352,1024]{1,0:T(8,128)(2,1)S(1)}, bf16[352,1024]{1,0:T(8,128)(2,1)}, u32[]{:S(2)}, u32[]{:S(2)}) collective-permute-start(bf16[352,1024]{1,0:T(8,128)(2,1)S(1)} %collective-permute-done.4.refs_1_), channel_id=1, source_target_pairs={{0,1},{1,0},{2,3},{3,2},{4,5},{5,4},{6,7},{7,6},{8,9},{9,8},{10,11... | collective-permute-start | bytes 2162696 | tf_op jit(solution)/shard_map/ppermute | solution.py:404
  118.2 17.8 %copy-start.7 = (bf16[352,256]{1,0:T(8,128)(2,1)S(1)}, bf16[352,256]{1,0:T(8,128)(2,1)}, u32[]{:S(2)}) copy-start(bf16[352,256]{1,0:T(8,128)(2,1)} %get-tuple-element.36.refs_0_) | copy-start | bytes 540676
  120.1 0.9 copy-start.18
  136.0 0.9 copy-start.8
  136.9 10.4 %copy-start.10 = (bf16[352,1024]{1,0:T(8,128)(2,1)S(1)}, bf16[352,1024]{1,0:T(8,128)(2,1)}, u32[]{:S(2)}) copy-start(bf16[352,1024]{1,0:T(8,128)(2,1)} %get-tuple-element.35) | copy-start | bytes 2162692
  136.9 10.5 %copy-start.9 = (bf16[352,1024]{1,0:T(8,128)(2,1)S(1)}, bf16[352,1024]{1,0:T(8,128)(2,1)}, u32[]{:S(2)}) copy-start(bf16[352,1024]{1,0:T(8,128)(2,1)} %get-tuple-element.32.refs_5_) | copy-start | bytes 2162692
  137.4 10.1 %collective-permute-start.10 = (bf16[64,384]{1,0:T(8,128)(2,1)S(1)}, bf16[64,384]{1,0:T(8,128)(2,1)S(1)}, u32[]{:S(2)}, u32[]{:S(2)}) collective-permute-start(bf16[64,384]{1,0:T(8,128)(2,1)S(1)} %get-tuple-element.39), channel_id=1, source_target_pairs={{0,4},{4,8},{8,12},{12,16},{16,20},{20,24},{24,28},{28,0},{1,5},{5... | collective-permute-start | bytes 147464 | tf_op jit(solution)/shard_map/ppermute | solution.py:539
  137.4 11.7 %collective-permute-start.11 = (bf16[64,384]{1,0:T(8,128)(2,1)S(1)}, bf16[64,384]{1,0:T(8,128)(2,1)S(1)}, u32[]{:S(2)}, u32[]{:S(2)}) collective-permute-start(bf16[64,384]{1,0:T(8,128)(2,1)S(1)} %get-tuple-element.40), channel_id=1, source_target_pairs={{0,8},{4,12},{8,16},{12,20},{16,24},{20,28},{24,0},{28,4},{1,9},{5... | collective-permute-start | bytes 147464 | tf_op jit(solution)/shard_map/ppermute | solution.py:539
  141.4 9.1 %collective-permute-start.12 = (bf16[64,384]{1,0:T(8,128)(2,1)S(1)}, bf16[64,384]{1,0:T(8,128)(2,1)S(1)}, u32[]{:S(2)}, u32[]{:S(2)}) collective-permute-start(bf16[64,384]{1,0:T(8,128)(2,1)S(1)} %get-tuple-element.41), channel_id=1, source_target_pairs={{0,12},{4,16},{8,20},{12,24},{16,28},{20,0},{24,4},{28,8},{1,13},{... | collective-permute-start | bytes 147464 | tf_op jit(solution)/shard_map/ppermute | solution.py:539
  144.9 6.0 %collective-permute-start.13 = (bf16[64,384]{1,0:T(8,128)(2,1)S(1)}, bf16[64,384]{1,0:T(8,128)(2,1)S(1)}, u32[]{:S(2)}, u32[]{:S(2)}) collective-permute-start(bf16[64,384]{1,0:T(8,128)(2,1)S(1)} %get-tuple-element.42), channel_id=1, source_target_pairs={{0,16},{4,20},{8,24},{12,28},{16,0},{20,4},{24,8},{28,12},{1,17},{... | collective-permute-start | bytes 147464 | tf_op jit(solution)/shard_map/ppermute | solution.py:539
  145.1 6.2 %collective-permute-start.14 = (bf16[64,384]{1,0:T(8,128)(2,1)S(1)}, bf16[64,384]{1,0:T(8,128)(2,1)S(1)}, u32[]{:S(2)}, u32[]{:S(2)}) collective-permute-start(bf16[64,384]{1,0:T(8,128)(2,1)S(1)} %get-tuple-element.43), channel_id=1, source_target_pairs={{0,20},{4,24},{8,28},{12,0},{16,4},{20,8},{24,12},{28,16},{1,21},{... | collective-permute-start | bytes 147464 | tf_op jit(solution)/shard_map/ppermute | solution.py:539
  147.5 5.2 %collective-permute-start.15 = (bf16[64,384]{1,0:T(8,128)(2,1)S(1)}, bf16[64,384]{1,0:T(8,128)(2,1)S(1)}, u32[]{:S(2)}, u32[]{:S(2)}) collective-permute-start(bf16[64,384]{1,0:T(8,128)(2,1)S(1)} %get-tuple-element.44), channel_id=1, source_target_pairs={{0,24},{4,28},{8,0},{12,4},{16,8},{20,12},{24,16},{28,20},{1,25},{... | collective-permute-start | bytes 147464 | tf_op jit(solution)/shard_map/ppermute | solution.py:539
  149.1 4.1 %collective-permute-start.16 = (bf16[64,384]{1,0:T(8,128)(2,1)S(1)}, bf16[64,384]{1,0:T(8,128)(2,1)S(1)}, u32[]{:S(2)}, u32[]{:S(2)}) collective-permute-start(bf16[64,384]{1,0:T(8,128)(2,1)S(1)} %get-tuple-element.45), channel_id=1, source_target_pairs={{0,28},{4,0},{8,4},{12,8},{16,12},{20,16},{24,20},{28,24},{1,29},{... | collective-permute-start | bytes 147464 | tf_op jit(solution)/shard_map/ppermute | solution.py:539
  150.5 4.0 %copy-start.11 = (bf16[352,2048]{1,0:T(8,128)(2,1)}, bf16[352,2048]{1,0:T(8,128)(2,1)S(1)}, u32[]{:S(2)}) copy-start(bf16[352,2048]{1,0:T(8,128)(2,1)S(1)} %slice_dynamic-update-slice_fusion) | copy-start | bytes 4325380
Sparse Core Ops, SparseCore 0:
  11.9 46.0 all-gather.2

commit v3 on v2

--- a/solution.py
+++ b/solution.py
@@ -155,9 +155,9 @@
         ).astype(BF)
 
 
-def project(order, first, col_ref, gain_ref, perm_hbm, res_ref, wt_ref, mw_ref, *refs):
+def project(order, first, parts, col_ref, gain_ref, perm_hbm, res_ref, wt_ref, mw_ref, *refs):
     count = len(order)
-    att_refs = refs[:count]
+    att_refs = refs[: count * parts]
     layer_ref, out_ref, gathered, layer_s, res_s, wt_s, mw_s, merged_s, perm_ref = refs[-13:-4]
     att_sem, wt_sem, res_sem, sems = refs[-4:]
     width = att_refs[0].shape[0]
@@ -177,10 +177,12 @@
         )
 
     att_copies = []
-    for part, (bit, att_ref) in enumerate(zip(order, att_refs)):
-        row = pl.multiple_of((col ^ bit) * width, 16)
+    for at, att_ref in enumerate(att_refs):
+        row = pl.multiple_of((col ^ order[at % count]) * width, 16)
+        span = att_ref.shape[1]
+        lanes = pl.ds(at // count * span, span)
         att_copies.append(
-            pltpu.make_async_copy(att_ref, gathered.at[pl.ds(row, width), :], att_sem.at[part])
+            pltpu.make_async_copy(att_ref, gathered.at[pl.ds(row, width), lanes], att_sem.at[at])
         )
     late = [
         pltpu.make_async_copy(perm_hbm, perm_ref, sems.at[0]),
@@ -274,7 +276,7 @@
     own_tiles = tokens // TILE
     far_tiles = reach // TILE
     half = own_tiles // 2
-    plan = [half // 2, half - half // 2]
+    plan = [half // 2] + [1] * (half - half // 2)
     begins = [sum(plan[:s]) for s in range(len(plan))]
     stages = len(plan)
     depth = round_up(HEAD_DIM + images, 128)
@@ -404,14 +406,15 @@
             pieces = pieces + [lax.ppermute(piece, "col", pairs) for piece in sources]
         gathers[stage] = pieces
 
-    def run_project(stage):
-        size = plan[stage]
+    def run_project(first, members):
+        size = sum(plan[stage] for stage in members)
+        pieces = [piece for stage in members for piece in gathers[stage]]
         columns, merged_columns = 2 * size * TILE, size * TILE // 2
         after = [gathers[-1][0]] + layers[-1:]
         layer, part = pl.pallas_call(
-            functools.partial(project, order, begins[stage]),
+            functools.partial(project, order, first, len(members)),
             grid=(1,),
-            in_specs=[smem_spec, vmem_spec] + [any_spec] * (4 + cols + len(after)),
+            in_specs=[smem_spec, vmem_spec] + [any_spec] * (4 + len(pieces) + len(after)),
             out_specs=[vmem_spec, vmem_spec],
             out_shape=[
                 jax.ShapeDtypeStruct((width, columns), BF),
@@ -425,7 +428,7 @@
                 pltpu.VMEM((width, 4 * full), BF),
                 pltpu.VMEM((width, merged_columns), F32),
                 pltpu.VMEM(perm.shape, BF),
-                pltpu.SemaphoreType.DMA((cols,)),
+                pltpu.SemaphoreType.DMA((len(pieces),)),
                 pltpu.SemaphoreType.DMA((cols,)),
                 pltpu.SemaphoreType.DMA((cols,)),
                 pltpu.SemaphoreType.DMA((2,)),
@@ -433,7 +436,7 @@
             compiler_params=params(62),
             cost_estimate=cost((4 + 4 * size) * 1e9, 1e5),
             name="project",
-        )(col_value, gain, perm, residual, out_weight_t, merge_weight, *gathers[stage], *after)
+        )(col_value, gain, perm, residual, out_weight_t, merge_weight, *pieces, *after)
         layers.append(layer)
         parts.append(part)
 
@@ -476,18 +479,18 @@
 
         gathers.append([attended])
         spread_pieces(stage, bits[:1], None)
-    spread_pieces(0, bits[1:], gathers[1][0])
-    run_project(0)
-    spread_pieces(1, bits[1:], layers[0])
-    run_project(1)
+        if stage >= 1:
+            spread_pieces(stage - 1, bits[1:], attended)
+    run_project(0, [0])
+    spread_pieces(stages - 1, bits[1:], layers[0])
+    run_project(inner, list(range(1, stages)))
 
     tiles_out = [None] * own_tiles
-    for stage in range(stages):
-        for block in range(plan[stage]):
+    for layer, first in zip(layers, (0, inner)):
+        for block in range(layer.shape[1] // (2 * TILE)):
             for which in range(2):
                 lane = (2 * block + which) * TILE
-                tile = pair_tile(begins[stage] + block, which)
-                tiles_out[tile] = layers[stage][:, lane : lane + TILE]
+                tiles_out[pair_tile(first + block, which)] = layer[:, lane : lane + TILE]
     layer_out = jnp.concatenate(tiles_out, axis=1)
 
     groups = tokens // 4
@@ -504,7 +507,7 @@
     away = (owner - row_id) % rows
     info = jnp.stack([away * share + rank, place // base, place % base])
     info = info.reshape(3, own_tiles, piece_groups)
-    merges = [list(range(b, b + n)) for b, n in zip(begins, plan)]
+    merges = [list(range(inner)), list(range(inner, half))]
     info = jnp.stack(
         [
             jnp.concatenate(

time: 163 us -> 156 us (0.957)
  waiting for transfers between devices: 34.9 us -> 15.8 us
  Pallas kernels: 62.2 us -> 70.3 us
  starting transfers between devices: 28.3 us -> 34.5 us
    ppermute x2 -> x3, waiting for transfers between devices: 25.2 us -> 10 us  [send_chunk(): lefts.append(lax.ppermute(tail, 'row', forward))]
    pallas_call x2 -> x3, Pallas kernels: 25.8 us -> 33.9 us  [body(): pl.pallas_call(functools.partial(attend, own, halos, images, base_tile, r...]
    ppermute x2 -> x3, starting transfers between devices: 6.75 us -> 12.3 us  [send_chunk(): rights.append(lax.ppermute(head, 'row', backward))]
    ppermute x2 -> x3, waiting for transfers between devices: 4.57 us -> 3 us  [send_chunk(): rights.append(lax.ppermute(head, 'row', backward))]
    ppermute x2 -> x3, starting transfers between devices: 4.12 us -> 3.28 us  [send_chunk(): lefts.append(lax.ppermute(tail, 'row', forward))]
    unnamed x47 -> x51, local copies, waits for them, and re-layouts: 15.2 us -> 14.4 us
    ppermute x6 -> x9, starting transfers between devices: 4.43 us -> 4.64 us  [spread_pieces(): pieces = pieces + [lax.ppermute(piece, 'col', pairs) for piece in sources]]
  transfers between devices with their start and end apart: 18 -> 23, of which waited for: 10 -> 5; matrix products, arithmetic and copies ran while one was open for 7% -> 7% of each run, Pallas kernels for 26% -> 33%
where the time goes in v3:
time: 156 us
  Pallas kernels  70.3 us (45%)
  starting transfers between devices  34.5 us (22%)
  local copies, waits for them, and re-layouts  19.6 us (13%)
  waiting for transfers between devices  15.8 us (10%)
  between operations  14.4 us (9%)
    pallas_call x3, Pallas kernels, body(): pl.pallas_call(functools.partial(attend, own, halos, images, base_tile, r...  33.9 us
    pallas_call x2, Pallas kernels, run_project(): pl.pallas_call(functools.partial(project, order, first, len(members)), gr...  30.1 us
    unnamed x51, local copies, waits for them, and re-layouts  14.4 us
    ppermute x7, starting transfers between devices, body(): lax.ppermute(sent[step], 'row', [(i, (i + step) % rows) for i in range(ro...  14.2 us
    ppermute x3, starting transfers between devices, send_chunk(): rights.append(lax.ppermute(head, 'row', backward))  12.3 us
    ppermute x3, waiting for transfers between devices, send_chunk(): lefts.append(lax.ppermute(tail, 'row', forward))  10 us
    ppermute x9, starting transfers between devices, spread_pieces(): pieces = pieces + [lax.ppermute(piece, 'col', pairs) for piece in sources]  4.64 us
    ppermute x3, starting transfers between devices, send_chunk(): lefts.append(lax.ppermute(tail, 'row', forward))  3.28 us
  transfers between devices with their start and end apart: 23, of which 5 were waited for; matrix products, arithmetic and copies ran while one was open for 7% of the time, Pallas kernels for 33%

profile of v3, /device:TPU:0, one launch (start us, length us, event | category | flops | bytes accessed | tf_op | source)
XLA Modules:
  0.0 155.9 jit_solution(2947575044444830059)
XLA Ops:
  7.2 0.0 all-gather.3.cloned.1.call-start
  7.2 0.0 copy-start.3
  7.2 1.5 fusion.24
  8.8 0.2 fusion.perm_ref.refs_0_.perm_hbm
  8.9 0.1 copy-done.3
  9.0 2.7 %reorder_residual.1 = bf16[4,352,512]{2,1,0:T(8,128)(2,1)} custom-call(bf16[512,512]{1,0:T(8,128)(2,1)S(1)} %fusion.perm_ref.refs_0_.perm_hbm, bf16[352,2048]{1,0:T(8,128)(2,1)S(1)} %copy-done.3, bf16[352,2048]{1,0:T(8,128)(2,1)S(1)} %copy-done.3), custom_call_target="tpu_custom_call" | custom-call | flops 2000000000 | bytes 100000 | tf_op jit(solution)/shard_map/reorder_residual/pallas_call | solution.py:365
  11.8 0.0 all-gather.3.cloned.1.call-update
  11.8 3.0 %collective-permute-start = (bf16[2,352,512]{2,1,0:T(8,128)(2,1)S(1)}, bf16[2,352,512]{2,1,0:T(8,128)(2,1)S(1)}, u32[]{:S(2)}, u32[]{:S(2)}) collective-permute-start(bf16[2,352,512]{2,1,0:T(8,128)(2,1)S(1)} %get-tuple-element.59), channel_id=1, source_target_pairs={{0,4},{4,8},{8,12},{12,16},{16,20},{20,24},{24,28},{28,0},{1,5},{5... | collective-permute-start | bytes 2162696 | tf_op jit(solution)/shard_map/ppermute | solution.py:298
  14.8 3.1 %collective-permute-start.1 = (bf16[2,352,512]{2,1,0:T(8,128)(2,1)S(1)}, bf16[2,352,512]{2,1,0:T(8,128)(2,1)}, u32[]{:S(2)}, u32[]{:S(2)}) collective-permute-start(bf16[2,352,512]{2,1,0:T(8,128)(2,1)S(1)} %get-tuple-element.58), channel_id=1, source_target_pairs={{4,0},{8,4},{12,8},{16,12},{20,16},{24,20},{28,24},{0,28},{5,1},{9... | collective-permute-start | bytes 2162696 | tf_op jit(solution)/shard_map/ppermute | solution.py:299
  17.9 0.1 copy.34
  18.0 0.1 reduce-window.8
  18.0 0.1 multiply_reduce_fusion
  18.1 0.2 select_reduce_fusion.1
  18.4 0.1 slice.91
  18.5 6.4 %copy.33 = bf16[1408,1408]{0,1:T(8,128)(2,1)} copy(bf16[1408,1408]{1,0:T(8,128)(2,1)} %param.9) | data formatting | bytes 7929856 | tf_op args[2]
  24.9 1.1 broadcast_in_dim.42.gain_ref
  26.1 0.2 convert_reduce_fusion
  26.3 0.1 stack.35
  26.4 0.1 stack.36
  26.5 0.1 stack.37
  26.6 0.1 fusion.25
  26.7 0.7 stack.34.bounds
  27.4 0.1 add_bitcast_fusion
  27.5 0.1 convert_reduce_fusion.1
  27.7 0.0 copy-start
  27.7 2.2 %copy-done = bf16[3,352,2048]{2,1,0:T(8,128)(2,1)S(1)} copy-done((bf16[3,352,2048]{2,1,0:T(8,128)(2,1)S(1)}, bf16[3,352,2048]{2,1,0:T(8,128)(2,1)}, u32[]{:S(2)}) %copy-start) | copy-done | bytes 4325400
  29.9 1.8 %prepare_own.1 = (bf16[8,4,128,256]{3,2,1,0:T(8,128)(2,1)S(1)}, bf16[8,4,256,128]{3,2,1,0:T(8,128)(2,1)S(1)}, bf16[8,4,96,256]{3,2,1,0:T(8,128)(2,1)S(1)}) custom-call(s32[16,1,256]{2,1,0:T(1,128)S(1)} %compare_select_fusion.label_ref, bf16[3,352,2048]{2,1,0:T(8,128)(2,1)S(1)} %copy-done), custom_call_target="tpu_custom_call" | custom-call | flops 2000000000 | bytes 100000 | tf_op jit(solution)/shard_map/prepare_own/pallas_call | solution.py:341
  31.8 1.3 copy-done.4
  33.1 1.4 copy-done.5
  34.4 1.2 copy-done.6
  35.6 10.0 %collective-permute-done.refs_4_ = bf16[2,352,512]{2,1,0:T(8,128)(2,1)S(1)} collective-permute-done((bf16[2,352,512]{2,1,0:T(8,128)(2,1)S(1)}, bf16[2,352,512]{2,1,0:T(8,128)(2,1)S(1)}, u32[]{:S(2)}, u32[]{:S(2)}) %collective-permute-start) | collective-permute-done | bytes 720928 | tf_op jit(solution)/shard_map/ppermute | solution.py:298
  45.6 2.3 %collective-permute-done.1.refs_5_ = bf16[2,352,512]{2,1,0:T(8,128)(2,1)} collective-permute-done((bf16[2,352,512]{2,1,0:T(8,128)(2,1)S(1)}, bf16[2,352,512]{2,1,0:T(8,128)(2,1)}, u32[]{:S(2)}, u32[]{:S(2)}) %collective-permute-start.1) | collective-permute-done | bytes 720928 | tf_op jit(solution)/shard_map/ppermute | solution.py:299
  47.9 0.1 fusion.23
  48.0 0.2 collective-permute-start.2
  48.2 4.5 %collective-permute-start.3 = (bf16[2,352,256]{2,1,0:T(8,128)(2,1)S(1)}, bf16[2,352,256]{2,1,0:T(8,128)(2,1)}, u32[]{:S(2)}, u32[]{:S(2)}) collective-permute-start(bf16[2,352,256]{2,1,0:T(8,128)(2,1)S(1)} %get-tuple-element.56), channel_id=1, source_target_pairs={{4,0},{8,4},{12,8},{16,12},{20,16},{24,20},{28,24},{0,28},{5,1},{9... | collective-permute-start | bytes 1081352 | tf_op jit(solution)/shard_map/ppermute | solution.py:299
  52.8 16.0 %attend.3.refs_8_.refs_0_ = bf16[352,1024]{1,0:T(8,128)(2,1)} custom-call(s32[2,8]{1,0:T(2,128)} %stack.34.bounds, s32[16,1,256]{2,1,0:T(1,128)} %copy-done.2, bf16[512,512]{1,0:T(8,128)(2,1)} %copy-done.1, bf16[8,4,128,256]{3,2,1,0:T(8,128)(2,1)} %copy-done.4, bf16[8,4,256,128]{3,2,1,0:T(8,128)(2,1)} %copy-done.5, bf16[8,4,96,256]{3,2,1,0:T(8,128)(2,1)} %copy-done.6, ...), custom_call_target="tpu_custom_call" | custom-call | flops 12999999488 | bytes 100000 | tf_op jit(solution)/shard_map/attend/pallas_call | solution.py:457
  68.7 1.6 %collective-permute-start.10 = (bf16[352,1024]{1,0:T(8,128)(2,1)}, bf16[352,1024]{1,0:T(8,128)(2,1)}, u32[]{:S(2)}, u32[]{:S(2)}) collective-permute-start(bf16[352,1024]{1,0:T(8,128)(2,1)} %attend.3.refs_8_.refs_0_), channel_id=1, source_target_pairs={{0,2},{1,3},{2,0},{3,1},{4,6},{5,7},{6,4},{7,5},{8,10},{9,11},{10,... | collective-permute-start | bytes 2162696 | tf_op jit(solution)/shard_map/ppermute | solution.py:406
  70.3 1.3 fusion.22
  71.6 0.1 collective-permute-start.5
  71.7 4.7 %collective-permute-start.6 = (bf16[2,352,256]{2,1,0:T(8,128)(2,1)S(1)}, bf16[2,352,256]{2,1,0:T(8,128)(2,1)}, u32[]{:S(2)}, u32[]{:S(2)}) collective-permute-start(bf16[2,352,256]{2,1,0:T(8,128)(2,1)S(1)} %get-tuple-element.54), channel_id=1, source_target_pairs={{4,0},{8,4},{12,8},{16,12},{20,16},{24,20},{28,24},{0,28},{5,1},{9... | collective-permute-start | bytes 1081352 | tf_op jit(solution)/shard_map/ppermute | solution.py:299
  76.4 9.7 %attend.4.refs_10_.refs_0_ = bf16[352,512]{1,0:T(8,128)(2,1)} custom-call(s32[2,8]{1,0:T(2,128)} %stack.34.bounds, s32[16,1,256]{2,1,0:T(1,128)} %copy-done.2, bf16[512,512]{1,0:T(8,128)(2,1)} %copy-done.1, bf16[8,4,128,256]{3,2,1,0:T(8,128)(2,1)} %copy-done.4, bf16[8,4,256,128]{3,2,1,0:T(8,128)(2,1)} %copy-done.5, bf16[8,4,96,256]{3,2,1,0:T(8,128)(2,1)} %copy-done.6, ...), custom_call_target="tpu_custom_call" | custom-call | flops 8999999488 | bytes 100000 | tf_op jit(solution)/shard_map/attend/pallas_call | solution.py:457
  86.1 0.6 collective-permute-start.4
  86.7 0.5 collective-permute-start.12
  87.2 0.7 collective-permute-done.6.refs_9_
  87.9 8.2 %attend.5.refs_4_.refs_8_ = bf16[352,512]{1,0:T(8,128)(2,1)} custom-call(s32[2,8]{1,0:T(2,128)} %stack.34.bounds, s32[16,1,256]{2,1,0:T(1,128)} %copy-done.2, bf16[512,512]{1,0:T(8,128)(2,1)} %copy-done.1, bf16[8,4,128,256]{3,2,1,0:T(8,128)(2,1)} %copy-done.4, bf16[8,4,256,128]{3,2,1,0:T(8,128)(2,1)} %copy-done.5, bf16[8,4,96,256]{3,2,1,0:T(8,128)(2,1)} %copy-done.6, ...), custom_call_target="tpu_custom_call" | custom-call | flops 8999999488 | bytes 100000 | tf_op jit(solution)/shard_map/attend/pallas_call | solution.py:457
  96.1 0.9 collective-permute-start.9
  97.0 0.5 collective-permute-start.8
  97.5 15.1 %project.2 = (bf16[352,1024]{1,0:T(8,128)(2,1)}, bf16[352,256]{1,0:T(8,128)(2,1)}) custom-call(s32[1]{0:T(128)} %bitcast.col_ref, f32[1408,1]{1,0:T(8,128)} %broadcast_in_dim.42.gain_ref, bf16[512,512]{1,0:T(8,128)(2,1)} %copy-done.1, bf16[4,4,352,512]{3,2,1,0:T(8,128)(2,1)} %bitcast.56, bf16[1408,1408]{1,0:T(8,128)(2,1)} %bitcast.52, ...), custom_call_target="tpu_custom_call" | custom-call | flops 12000000000 | bytes 100000 | tf_op jit(solution)/shard_map/project/pallas_call | solution.py:414
  112.6 0.1 collective-permute-start.13
  112.8 0.4 collective-permute-start.14
  113.3 1.1 collective-permute-done.13.refs_6_
  114.4 0.7 copy-done.22
  115.1 15.0 %project.3 = (bf16[352,1024]{1,0:T(8,128)(2,1)}, bf16[352,256]{1,0:T(8,128)(2,1)}) custom-call(s32[1]{0:T(128)} %bitcast.col_ref, f32[1408,1]{1,0:T(8,128)} %broadcast_in_dim.42.gain_ref, bf16[512,512]{1,0:T(8,128)(2,1)} %copy-done.1, bf16[4,4,352,512]{3,2,1,0:T(8,128)(2,1)} %bitcast.57, bf16[1408,1408]{1,0:T(8,128)(2,1)} %bitcast.53, ...), custom_call_target="tpu_custom_call" | custom-call | flops 12000000000 | bytes 100000 | tf_op jit(solution)/shard_map/project/pallas_call | solution.py:414
  130.2 0.9 copy-done.8
  131.1 0.5 outgoing.1
  131.6 2.8 %collective-permute-start.15 = (bf16[64,384]{1,0:T(8,128)(2,1)S(1)}, bf16[64,384]{1,0:T(8,128)(2,1)S(1)}, u32[]{:S(2)}, u32[]{:S(2)}) collective-permute-start(bf16[64,384]{1,0:T(8,128)(2,1)S(1)} %get-tuple-element.45), channel_id=1, source_target_pairs={{0,4},{4,8},{8,12},{12,16},{16,20},{20,24},{24,28},{28,0},{1,5},{5... | collective-permute-start | bytes 147464 | tf_op jit(solution)/shard_map/ppermute | solution.py:542
  134.3 3.2 %collective-permute-start.17 = (bf16[64,384]{1,0:T(8,128)(2,1)S(1)}, bf16[64,384]{1,0:T(8,128)(2,1)S(1)}, u32[]{:S(2)}, u32[]{:S(2)}) collective-permute-start(bf16[64,384]{1,0:T(8,128)(2,1)S(1)} %get-tuple-element.47), channel_id=1, source_target_pairs={{0,12},{4,16},{8,20},{12,24},{16,28},{20,0},{24,4},{28,8},{1,13},{... | collective-permute-start | bytes 147464 | tf_op jit(solution)/shard_map/ppermute | solution.py:542
  137.6 1.9 %collective-permute-start.18 = (bf16[64,384]{1,0:T(8,128)(2,1)S(1)}, bf16[64,384]{1,0:T(8,128)(2,1)S(1)}, u32[]{:S(2)}, u32[]{:S(2)}) collective-permute-start(bf16[64,384]{1,0:T(8,128)(2,1)S(1)} %get-tuple-element.48), channel_id=1, source_target_pairs={{0,16},{4,20},{8,24},{12,28},{16,0},{20,4},{24,8},{28,12},{1,17},{... | collective-permute-start | bytes 147464 | tf_op jit(solution)/shard_map/ppermute | solution.py:542
  139.5 1.0 collective-permute-start.19
  140.7 2.5 %collective-permute-start.20 = (bf16[64,384]{1,0:T(8,128)(2,1)S(1)}, bf16[64,384]{1,0:T(8,128)(2,1)S(1)}, u32[]{:S(2)}, u32[]{:S(2)}) collective-permute-start(bf16[64,384]{1,0:T(8,128)(2,1)S(1)} %get-tuple-element.50), channel_id=1, source_target_pairs={{0,24},{4,28},{8,0},{12,4},{16,8},{20,12},{24,16},{28,20},{1,25},{... | collective-permute-start | bytes 147464 | tf_op jit(solution)/shard_map/ppermute | solution.py:542
  143.1 2.9 %collective-permute-start.21 = (bf16[64,384]{1,0:T(8,128)(2,1)S(1)}, bf16[64,384]{1,0:T(8,128)(2,1)S(1)}, u32[]{:S(2)}, u32[]{:S(2)}) collective-permute-start(bf16[64,384]{1,0:T(8,128)(2,1)S(1)} %get-tuple-element.51), channel_id=1, source_target_pairs={{0,28},{4,0},{8,4},{12,8},{16,12},{20,16},{24,20},{28,24},{1,29},{... | collective-permute-start | bytes 147464 | tf_op jit(solution)/shard_map/ppermute | solution.py:542
  146.0 0.0 copy-start.11
  146.1 1.7 %collective-permute-done.21.refs_7_ = bf16[64,384]{1,0:T(8,128)(2,1)S(1)} collective-permute-done((bf16[64,384]{1,0:T(8,128)(2,1)S(1)}, bf16[64,384]{1,0:T(8,128)(2,1)S(1)}, u32[]{:S(2)}, u32[]{:S(2)}) %collective-permute-start.21) | collective-permute-done | bytes 49184 | tf_op jit(solution)/shard_map/ppermute | solution.py:542
  147.8 1.3 incoming.1
  (77 shorter events, 0.4 us)
Async XLA Ops:
  7.2 90.4 %all-gather.3.cloned.1.call-start = ((), (), s32[]{:S(2)}) async-start(), calls=%async_computation | async-start | bytes 7208960 | tf_op jit(solution)/shard_map/all_gather | solution.py:379
  7.2 1.8 %copy-start.3 = (bf16[352,2048]{1,0:T(8,128)(2,1)S(1)}, bf16[352,2048]{1,0:T(8,128)(2,1)}, u32[]{:S(2)}) copy-start(bf16[352,2048]{1,0:T(8,128)(2,1)} %high_ref) | copy-start | bytes 4325380
  8.9 2.8 %copy-start.1 = (bf16[512,512]{1,0:T(8,128)(2,1)}, bf16[512,512]{1,0:T(8,128)(2,1)S(1)}, u32[]{:S(2)}) copy-start(bf16[512,512]{1,0:T(8,128)(2,1)S(1)} %fusion.perm_ref.refs_0_.perm_hbm) | copy-start | bytes 1572868
  11.7 6.1 %copy-start.14 = (s32[32]{0:T(128)S(1)}, s32[32]{0:T(128)}, u32[]{:S(2)}) copy-start(s32[32]{0:T(128)} %param.12) | copy-start | bytes 388
  11.8 33.8 %collective-permute-start = (bf16[2,352,512]{2,1,0:T(8,128)(2,1)S(1)}, bf16[2,352,512]{2,1,0:T(8,128)(2,1)S(1)}, u32[]{:S(2)}, u32[]{:S(2)}) collective-permute-start(bf16[2,352,512]{2,1,0:T(8,128)(2,1)S(1)} %get-tuple-element.59), channel_id=1, source_target_pairs={{0,4},{4,8},{8,12},{12,16},{16,20},{20,24},{24,28},{28,0},{1,5},{5... | collective-permute-start | bytes 2162696 | tf_op jit(solution)/shard_map/ppermute | solution.py:298
  14.8 33.2 %collective-permute-start.1 = (bf16[2,352,512]{2,1,0:T(8,128)(2,1)S(1)}, bf16[2,352,512]{2,1,0:T(8,128)(2,1)}, u32[]{:S(2)}, u32[]{:S(2)}) collective-permute-start(bf16[2,352,512]{2,1,0:T(8,128)(2,1)S(1)} %get-tuple-element.58), channel_id=1, source_target_pairs={{4,0},{8,4},{12,8},{16,12},{20,16},{24,20},{28,24},{0,28},{5,1},{9... | collective-permute-start | bytes 2162696 | tf_op jit(solution)/shard_map/ppermute | solution.py:299
  18.5 6.5 %copy-start.12 = (f32[1408]{0:T(1024)S(1)}, f32[1408]{0:T(1024)}, u32[]{:S(2)}) copy-start(f32[1408]{0:T(1024)} %param.11) | copy-start | bytes 16900
  18.5 7.6 %copy-start.13 = (s32[512]{0:T(512)S(1)}, s32[512]{0:T(512)}, u32[]{:S(2)}) copy-start(s32[512]{0:T(512)} %param.13) | copy-start | bytes 6148
  27.7 2.2 %copy-start = (bf16[3,352,2048]{2,1,0:T(8,128)(2,1)S(1)}, bf16[3,352,2048]{2,1,0:T(8,128)(2,1)}, u32[]{:S(2)}) copy-start(bf16[3,352,2048]{2,1,0:T(8,128)(2,1)} %qkv_ref) | copy-start | bytes 12976132
  29.9 1.8 %copy-start.2 = (s32[16,1,256]{2,1,0:T(1,128)}, s32[16,1,256]{2,1,0:T(1,128)S(1)}, u32[]{:S(2)}) copy-start(s32[16,1,256]{2,1,0:T(1,128)S(1)} %compare_select_fusion.label_ref) | copy-start | bytes 49156
  31.8 1.3 copy-start.4
  33.1 1.4 copy-start.5
  34.4 1.2 copy-start.6
  45.6 7.1 %copy-start.15 = (bf16[2,352,512]{2,1,0:T(8,128)(2,1)}, bf16[2,352,512]{2,1,0:T(8,128)(2,1)S(1)}, u32[]{:S(2)}) copy-start(bf16[2,352,512]{2,1,0:T(8,128)(2,1)S(1)} %collective-permute-done.refs_4_) | copy-start | bytes 2162692
  48.0 22.3 %collective-permute-start.2 = (bf16[2,352,256]{2,1,0:T(8,128)(2,1)S(1)}, bf16[2,352,256]{2,1,0:T(8,128)(2,1)S(1)}, u32[]{:S(2)}, u32[]{:S(2)}) collective-permute-start(bf16[2,352,256]{2,1,0:T(8,128)(2,1)S(1)} %get-tuple-element.57), channel_id=1, source_target_pairs={{0,4},{4,8},{8,12},{12,16},{16,20},{20,24},{24,28},{28,0},{1,5},{5... | collective-permute-start | bytes 1081352 | tf_op jit(solution)/shard_map/ppermute | solution.py:298
  48.2 22.1 %collective-permute-start.3 = (bf16[2,352,256]{2,1,0:T(8,128)(2,1)S(1)}, bf16[2,352,256]{2,1,0:T(8,128)(2,1)}, u32[]{:S(2)}, u32[]{:S(2)}) collective-permute-start(bf16[2,352,256]{2,1,0:T(8,128)(2,1)S(1)} %get-tuple-element.56), channel_id=1, source_target_pairs={{4,0},{8,4},{12,8},{16,12},{20,16},{24,20},{28,24},{0,28},{5,1},{9... | collective-permute-start | bytes 1081352 | tf_op jit(solution)/shard_map/ppermute | solution.py:299
  68.7 18.0 %collective-permute-start.10 = (bf16[352,1024]{1,0:T(8,128)(2,1)}, bf16[352,1024]{1,0:T(8,128)(2,1)}, u32[]{:S(2)}, u32[]{:S(2)}) collective-permute-start(bf16[352,1024]{1,0:T(8,128)(2,1)} %attend.3.refs_8_.refs_0_), channel_id=1, source_target_pairs={{0,2},{1,3},{2,0},{3,1},{4,6},{5,7},{6,4},{7,5},{8,10},{9,11},{10,... | collective-permute-start | bytes 2162696 | tf_op jit(solution)/shard_map/ppermute | solution.py:406
  70.3 6.1 %copy-start.21 = (bf16[2,352,256]{2,1,0:T(8,128)(2,1)}, bf16[2,352,256]{2,1,0:T(8,128)(2,1)S(1)}, u32[]{:S(2)}) copy-start(bf16[2,352,256]{2,1,0:T(8,128)(2,1)S(1)} %collective-permute-done.2.refs_6_) | copy-start | bytes 1081348
  71.6 15.6 %collective-permute-start.5 = (bf16[2,352,256]{2,1,0:T(8,128)(2,1)S(1)}, bf16[2,352,256]{2,1,0:T(8,128)(2,1)}, u32[]{:S(2)}, u32[]{:S(2)}) collective-permute-start(bf16[2,352,256]{2,1,0:T(8,128)(2,1)S(1)} %get-tuple-element.55), channel_id=1, source_target_pairs={{0,4},{4,8},{8,12},{12,16},{16,20},{20,24},{24,28},{28,0},{1,5},{5... | collective-permute-start | bytes 1081352 | tf_op jit(solution)/shard_map/ppermute | solution.py:298
  71.7 15.0 %copy-start.16 = (bf16[352,1024]{1,0:T(8,128)(2,1)S(1)}, bf16[352,1024]{1,0:T(8,128)(2,1)}, u32[]{:S(2)}) copy-start(bf16[352,1024]{1,0:T(8,128)(2,1)} %attend.3.refs_8_.refs_0_) | copy-start | bytes 2162692
  71.7 16.2 %collective-permute-start.6 = (bf16[2,352,256]{2,1,0:T(8,128)(2,1)S(1)}, bf16[2,352,256]{2,1,0:T(8,128)(2,1)}, u32[]{:S(2)}, u32[]{:S(2)}) collective-permute-start(bf16[2,352,256]{2,1,0:T(8,128)(2,1)S(1)} %get-tuple-element.54), channel_id=1, source_target_pairs={{4,0},{8,4},{12,8},{16,12},{20,16},{24,20},{28,24},{0,28},{5,1},{9... | collective-permute-start | bytes 1081352 | tf_op jit(solution)/shard_map/ppermute | solution.py:299
  86.1 10.9 %copy-start.17 = (bf16[352,512]{1,0:T(8,128)(2,1)S(1)}, bf16[352,512]{1,0:T(8,128)(2,1)}, u32[]{:S(2)}) copy-start(bf16[352,512]{1,0:T(8,128)(2,1)} %attend.4.refs_10_.refs_0_) | copy-start | bytes 1081348
  86.1 10.9 %collective-permute-start.4 = (bf16[352,512]{1,0:T(8,128)(2,1)}, bf16[352,512]{1,0:T(8,128)(2,1)}, u32[]{:S(2)}, u32[]{:S(2)}) collective-permute-start(bf16[352,512]{1,0:T(8,128)(2,1)} %attend.4.refs_10_.refs_0_), channel_id=1, source_target_pairs={{0,2},{1,3},{2,0},{3,1},{4,6},{5,7},{6,4},{7,5},{8,10},{9,11},{10,... | collective-permute-start | bytes 1081352 | tf_op jit(solution)/shard_map/ppermute | solution.py:406
  86.7 10.8 %collective-permute-start.11 = (bf16[352,1024]{1,0:T(8,128)(2,1)S(1)}, bf16[352,1024]{1,0:T(8,128)(2,1)}, u32[]{:S(2)}, u32[]{:S(2)}) collective-permute-start(bf16[352,1024]{1,0:T(8,128)(2,1)S(1)} %copy-done.16), channel_id=1, source_target_pairs={{0,1},{1,0},{2,3},{3,2},{4,5},{5,4},{6,7},{7,6},{8,9},{9,8},{10,11... | collective-permute-start | bytes 2162696 | tf_op jit(solution)/shard_map/ppermute | solution.py:406
  86.7 10.8 %collective-permute-start.12 = (bf16[352,1024]{1,0:T(8,128)(2,1)}, bf16[352,1024]{1,0:T(8,128)(2,1)}, u32[]{:S(2)}, u32[]{:S(2)}) collective-permute-start(bf16[352,1024]{1,0:T(8,128)(2,1)} %collective-permute-done.10.refs_1_), channel_id=1, source_target_pairs={{0,1},{1,0},{2,3},{3,2},{4,5},{5,4},{6,7},{7,6},{8,9},{9,8},{10,11... | collective-permute-start | bytes 2162696 | tf_op jit(solution)/shard_map/ppermute | solution.py:406
  96.1 16.5 %collective-permute-start.9 = (bf16[352,512]{1,0:T(8,128)(2,1)}, bf16[352,512]{1,0:T(8,128)(2,1)S(1)}, u32[]{:S(2)}, u32[]{:S(2)}) collective-permute-start(bf16[352,512]{1,0:T(8,128)(2,1)} %attend.5.refs_4_.refs_8_), channel_id=1, source_target_pairs={{0,2},{1,3},{2,0},{3,1},{4,6},{5,7},{6,4},{7,5},{8,10},{9,11},{10,... | collective-permute-start | bytes 1081352 | tf_op jit(solution)/shard_map/ppermute | solution.py:406
  97.0 16.3 %collective-permute-start.7 = (bf16[352,512]{1,0:T(8,128)(2,1)S(1)}, bf16[352,512]{1,0:T(8,128)(2,1)S(1)}, u32[]{:S(2)}, u32[]{:S(2)}) collective-permute-start(bf16[352,512]{1,0:T(8,128)(2,1)S(1)} %copy-done.17), channel_id=1, source_target_pairs={{0,1},{1,0},{2,3},{3,2},{4,5},{5,4},{6,7},{7,6},{8,9},{9,8},{10,11... | collective-permute-start | bytes 1081352 | tf_op jit(solution)/shard_map/ppermute | solution.py:406
  97.0 16.3 %collective-permute-start.8 = (bf16[352,512]{1,0:T(8,128)(2,1)}, bf16[352,512]{1,0:T(8,128)(2,1)}, u32[]{:S(2)}, u32[]{:S(2)}) collective-permute-start(bf16[352,512]{1,0:T(8,128)(2,1)} %collective-permute-done.4.refs_1_), channel_id=1, source_target_pairs={{0,1},{1,0},{2,3},{3,2},{4,5},{5,4},{6,7},{7,6},{8,9},{9,8},{10,11... | collective-permute-start | bytes 1081352 | tf_op jit(solution)/shard_map/ppermute | solution.py:406
  97.5 15.1 %copy-start.18 = (bf16[352,512]{1,0:T(8,128)(2,1)S(1)}, bf16[352,512]{1,0:T(8,128)(2,1)}, u32[]{:S(2)}) copy-start(bf16[352,512]{1,0:T(8,128)(2,1)} %attend.5.refs_4_.refs_8_) | copy-start | bytes 1081348
  112.6 2.5 %copy-start.19 = (bf16[352,512]{1,0:T(8,128)(2,1)}, bf16[352,512]{1,0:T(8,128)(2,1)S(1)}, u32[]{:S(2)}) copy-start(bf16[352,512]{1,0:T(8,128)(2,1)S(1)} %collective-permute-done.9.refs_5_) | copy-start | bytes 1081348
  112.6 1.7 %collective-permute-start.13 = (bf16[352,512]{1,0:T(8,128)(2,1)S(1)}, bf16[352,512]{1,0:T(8,128)(2,1)S(1)}, u32[]{:S(2)}, u32[]{:S(2)}) collective-permute-start(bf16[352,512]{1,0:T(8,128)(2,1)S(1)} %copy-done.18), channel_id=1, source_target_pairs={{0,1},{1,0},{2,3},{3,2},{4,5},{5,4},{6,7},{7,6},{8,9},{9,8},{10,11... | collective-permute-start | bytes 1081352 | tf_op jit(solution)/shard_map/ppermute | solution.py:406
  112.8 2.3 %collective-permute-start.14 = (bf16[352,512]{1,0:T(8,128)(2,1)S(1)}, bf16[352,512]{1,0:T(8,128)(2,1)}, u32[]{:S(2)}, u32[]{:S(2)}) collective-permute-start(bf16[352,512]{1,0:T(8,128)(2,1)S(1)} %collective-permute-done.9.refs_5_), channel_id=1, source_target_pairs={{0,1},{1,0},{2,3},{3,2},{4,5},{5,4},{6,7},{7,6},{8,9},{9,8},{10,11... | collective-permute-start | bytes 1081352 | tf_op jit(solution)/shard_map/ppermute | solution.py:406
  113.3 16.9 %copy-start.7 = (bf16[352,256]{1,0:T(8,128)(2,1)S(1)}, bf16[352,256]{1,0:T(8,128)(2,1)}, u32[]{:S(2)}) copy-start(bf16[352,256]{1,0:T(8,128)(2,1)} %get-tuple-element.42.refs_0_) | copy-start | bytes 540676
  113.3 1.9 %copy-start.20 = (bf16[352,512]{1,0:T(8,128)(2,1)}, bf16[352,512]{1,0:T(8,128)(2,1)S(1)}, u32[]{:S(2)}) copy-start(bf16[352,512]{1,0:T(8,128)(2,1)S(1)} %collective-permute-done.7.refs_2_) | copy-start | bytes 1081348
  114.4 0.7 copy-start.22
  130.2 0.9 copy-start.8
  131.1 9.4 %copy-start.10 = (bf16[352,1024]{1,0:T(8,128)(2,1)S(1)}, bf16[352,1024]{1,0:T(8,128)(2,1)}, u32[]{:S(2)}) copy-start(bf16[352,1024]{1,0:T(8,128)(2,1)} %get-tuple-element.41) | copy-start | bytes 2162692
  131.1 9.4 %copy-start.9 = (bf16[352,1024]{1,0:T(8,128)(2,1)S(1)}, bf16[352,1024]{1,0:T(8,128)(2,1)}, u32[]{:S(2)}) copy-start(bf16[352,1024]{1,0:T(8,128)(2,1)} %get-tuple-element.38.refs_9_) | copy-start | bytes 2162692
  131.6 9.1 %collective-permute-start.15 = (bf16[64,384]{1,0:T(8,128)(2,1)S(1)}, bf16[64,384]{1,0:T(8,128)(2,1)S(1)}, u32[]{:S(2)}, u32[]{:S(2)}) collective-permute-start(bf16[64,384]{1,0:T(8,128)(2,1)S(1)} %get-tuple-element.45), channel_id=1, source_target_pairs={{0,4},{4,8},{8,12},{12,16},{16,20},{20,24},{24,28},{28,0},{1,5},{5... | collective-permute-start | bytes 147464 | tf_op jit(solution)/shard_map/ppermute | solution.py:542
  134.3 8.8 %collective-permute-start.16 = (bf16[64,384]{1,0:T(8,128)(2,1)S(1)}, bf16[64,384]{1,0:T(8,128)(2,1)S(1)}, u32[]{:S(2)}, u32[]{:S(2)}) collective-permute-start(bf16[64,384]{1,0:T(8,128)(2,1)S(1)} %get-tuple-element.46), channel_id=1, source_target_pairs={{0,8},{4,12},{8,16},{12,20},{16,24},{20,28},{24,0},{28,4},{1,9},{5... | collective-permute-start | bytes 147464 | tf_op jit(solution)/shard_map/ppermute | solution.py:542
  134.3 11.7 %collective-permute-start.17 = (bf16[64,384]{1,0:T(8,128)(2,1)S(1)}, bf16[64,384]{1,0:T(8,128)(2,1)S(1)}, u32[]{:S(2)}, u32[]{:S(2)}) collective-permute-start(bf16[64,384]{1,0:T(8,128)(2,1)S(1)} %get-tuple-element.47), channel_id=1, source_target_pairs={{0,12},{4,16},{8,20},{12,24},{16,28},{20,0},{24,4},{28,8},{1,13},{... | collective-permute-start | bytes 147464 | tf_op jit(solution)/shard_map/ppermute | solution.py:542
  137.6 8.5 %collective-permute-start.18 = (bf16[64,384]{1,0:T(8,128)(2,1)S(1)}, bf16[64,384]{1,0:T(8,128)(2,1)S(1)}, u32[]{:S(2)}, u32[]{:S(2)}) collective-permute-start(bf16[64,384]{1,0:T(8,128)(2,1)S(1)} %get-tuple-element.48), channel_id=1, source_target_pairs={{0,16},{4,20},{8,24},{12,28},{16,0},{20,4},{24,8},{28,12},{1,17},{... | collective-permute-start | bytes 147464 | tf_op jit(solution)/shard_map/ppermute | solution.py:542
  139.5 6.6 %collective-permute-start.19 = (bf16[64,384]{1,0:T(8,128)(2,1)S(1)}, bf16[64,384]{1,0:T(8,128)(2,1)S(1)}, u32[]{:S(2)}, u32[]{:S(2)}) collective-permute-start(bf16[64,384]{1,0:T(8,128)(2,1)S(1)} %get-tuple-element.49), channel_id=1, source_target_pairs={{0,20},{4,24},{8,28},{12,0},{16,4},{20,8},{24,12},{28,16},{1,21},{... | collective-permute-start | bytes 147464 | tf_op jit(solution)/shard_map/ppermute | solution.py:542
  140.7 5.4 %collective-permute-start.20 = (bf16[64,384]{1,0:T(8,128)(2,1)S(1)}, bf16[64,384]{1,0:T(8,128)(2,1)S(1)}, u32[]{:S(2)}, u32[]{:S(2)}) collective-permute-start(bf16[64,384]{1,0:T(8,128)(2,1)S(1)} %get-tuple-element.50), channel_id=1, source_target_pairs={{0,24},{4,28},{8,0},{12,4},{16,8},{20,12},{24,16},{28,20},{1,25},{... | collective-permute-start | bytes 147464 | tf_op jit(solution)/shard_map/ppermute | solution.py:542
  143.1 4.6 %collective-permute-start.21 = (bf16[64,384]{1,0:T(8,128)(2,1)S(1)}, bf16[64,384]{1,0:T(8,128)(2,1)S(1)}, u32[]{:S(2)}, u32[]{:S(2)}) collective-permute-start(bf16[64,384]{1,0:T(8,128)(2,1)S(1)} %get-tuple-element.51), channel_id=1, source_target_pairs={{0,28},{4,0},{8,4},{12,8},{16,12},{20,16},{24,20},{28,24},{1,29},{... | collective-permute-start | bytes 147464 | tf_op jit(solution)/shard_map/ppermute | solution.py:542
  146.0 3.0 %copy-start.11 = (bf16[352,2048]{1,0:T(8,128)(2,1)}, bf16[352,2048]{1,0:T(8,128)(2,1)S(1)}, u32[]{:S(2)}) copy-start(bf16[352,2048]{1,0:T(8,128)(2,1)S(1)} %slice_dynamic-update-slice_fusion) | copy-start | bytes 4325380
Sparse Core Ops, SparseCore 0:
  11.9 46.0 all-gather.2

commit v4 on v3

--- a/solution.py
+++ b/solution.py
@@ -208,7 +208,7 @@
             layer_s[rows, lanes] = (res_s[part, at].astype(F32) + projected).astype(BF)
         return carry
 
-    lax.fori_loop(0, count, project_part, 0)
+    lax.fori_loop(0, count, project_part, 0, unroll=True)
     for copy in late:
         copy.wait()
     own = pl.ds(pl.multiple_of(col * width, 16), width)
@@ -234,7 +234,7 @@
         )
         return carry
 
-    lax.fori_loop(0, 4, merge_part, 0)
+    lax.fori_loop(0, 4, merge_part, 0, unroll=True)
     out_ref[...] = merged_s[...].astype(BF)
 
 

time: 156 us -> 157 us (level)
  waiting for transfers between devices: 15.8 us -> 19.1 us
  Pallas kernels: 70.3 us -> 68.2 us
    ppermute x3, waiting for transfers between devices: 3 us -> 5.56 us  [send_chunk(): rights.append(lax.ppermute(head, 'row', backward))]
    pallas_call x3, Pallas kernels: 33.9 us -> 31.4 us  [body(): pl.pallas_call(functools.partial(attend, own, halos, images, base_tile, r...]
    ppermute x7, starting transfers between devices: 14.2 us -> 12 us  [body(): lax.ppermute(sent[step], 'row', [(i, (i + step) % rows) for i in range(ro...]
  transfers between devices with their start and end apart: 23 -> 23, of which waited for: 5 -> 7; matrix products, arithmetic and copies ran while one was open for 7% -> 7% of each run, Pallas kernels for 33% -> 31%
where the time goes in v4:
time: 157 us; the launch traced here: 156 us
  Pallas kernels  68.2 us (43%)
  starting transfers between devices  33 us (21%)
  local copies, waits for them, and re-layouts  19.6 us (12%)
  waiting for transfers between devices  19.1 us (12%)
  between operations  14.4 us (9%)
    pallas_call x3, Pallas kernels, body(): pl.pallas_call(functools.partial(attend, own, halos, images, base_tile, r...  31.4 us
    pallas_call x2, Pallas kernels, run_project(): pl.pallas_call(functools.partial(project, order, first, len(members)), gr...  30.5 us
    unnamed x51, local copies, waits for them, and re-layouts  14.4 us
    ppermute x3, starting transfers between devices, send_chunk(): rights.append(lax.ppermute(head, 'row', backward))  12.3 us
    ppermute x7, starting transfers between devices, body(): lax.ppermute(sent[step], 'row', [(i, (i + step) % rows) for i in range(ro...  12 us
    ppermute x3, waiting for transfers between devices, send_chunk(): lefts.append(lax.ppermute(tail, 'row', forward))  10 us
    ppermute x3, waiting for transfers between devices, send_chunk(): rights.append(lax.ppermute(head, 'row', backward))  5.56 us
    ppermute x9, starting transfers between devices, spread_pieces(): pieces = pieces + [lax.ppermute(piece, 'col', pairs) for piece in sources]  5.32 us
  transfers between devices with their start and end apart: 23, of which 7 were waited for; matrix products, arithmetic and copies ran while one was open for 7% of the time, Pallas kernels for 31%

profile of v4, /device:TPU:0, one launch (start us, length us, event | category | flops | bytes accessed | tf_op | source)
XLA Modules:
  0.0 155.6 jit_solution(4245199730267819213)
XLA Ops:
  7.2 0.0 all-gather.3.cloned.1.call-start
  7.2 1.5 fusion.24
  8.8 0.2 fusion.perm_ref.refs_0_.perm_hbm
  8.9 0.1 copy-done.3
  9.0 2.7 %reorder_residual.1 = bf16[4,352,512]{2,1,0:T(8,128)(2,1)} custom-call(bf16[512,512]{1,0:T(8,128)(2,1)S(1)} %fusion.perm_ref.refs_0_.perm_hbm, bf16[352,2048]{1,0:T(8,128)(2,1)S(1)} %copy-done.3, bf16[352,2048]{1,0:T(8,128)(2,1)S(1)} %copy-done.3), custom_call_target="tpu_custom_call" | custom-call | flops 2000000000 | bytes 100000 | tf_op jit(solution)/shard_map/reorder_residual/pallas_call | solution.py:365
  11.8 0.0 all-gather.3.cloned.1.call-update
  11.8 3.0 %collective-permute-start = (bf16[2,352,512]{2,1,0:T(8,128)(2,1)S(1)}, bf16[2,352,512]{2,1,0:T(8,128)(2,1)S(1)}, u32[]{:S(2)}, u32[]{:S(2)}) collective-permute-start(bf16[2,352,512]{2,1,0:T(8,128)(2,1)S(1)} %get-tuple-element.59), channel_id=1, source_target_pairs={{0,4},{4,8},{8,12},{12,16},{16,20},{20,24},{24,28},{28,0},{1,5},{5... | collective-permute-start | bytes 2162696 | tf_op jit(solution)/shard_map/ppermute | solution.py:298
  14.8 3.1 %collective-permute-start.1 = (bf16[2,352,512]{2,1,0:T(8,128)(2,1)S(1)}, bf16[2,352,512]{2,1,0:T(8,128)(2,1)}, u32[]{:S(2)}, u32[]{:S(2)}) collective-permute-start(bf16[2,352,512]{2,1,0:T(8,128)(2,1)S(1)} %get-tuple-element.58), channel_id=1, source_target_pairs={{4,0},{8,4},{12,8},{16,12},{20,16},{24,20},{28,24},{0,28},{5,1},{9... | collective-permute-start | bytes 2162696 | tf_op jit(solution)/shard_map/ppermute | solution.py:299
  17.9 0.1 copy.34
  18.0 0.1 reduce-window.8
  18.0 0.1 multiply_reduce_fusion
  18.1 0.2 select_reduce_fusion.1
  18.4 0.1 slice.91
  18.5 6.4 %copy.33 = bf16[1408,1408]{0,1:T(8,128)(2,1)} copy(bf16[1408,1408]{1,0:T(8,128)(2,1)} %param.9) | data formatting | bytes 7929856 | tf_op args[2]
  24.9 1.1 broadcast_in_dim.42.gain_ref
  26.1 0.2 convert_reduce_fusion
  26.3 0.1 stack.35
  26.4 0.1 stack.36
  26.5 0.1 stack.37
  26.6 0.1 fusion.25
  26.7 0.7 stack.34.bounds
  27.4 0.1 add_bitcast_fusion
  27.5 0.1 convert_reduce_fusion.1
  27.7 2.2 %copy-done = bf16[3,352,2048]{2,1,0:T(8,128)(2,1)S(1)} copy-done((bf16[3,352,2048]{2,1,0:T(8,128)(2,1)S(1)}, bf16[3,352,2048]{2,1,0:T(8,128)(2,1)}, u32[]{:S(2)}) %copy-start) | copy-done | bytes 4325400
  29.9 1.8 %prepare_own.1 = (bf16[8,4,128,256]{3,2,1,0:T(8,128)(2,1)S(1)}, bf16[8,4,256,128]{3,2,1,0:T(8,128)(2,1)S(1)}, bf16[8,4,96,256]{3,2,1,0:T(8,128)(2,1)S(1)}) custom-call(s32[16,1,256]{2,1,0:T(1,128)S(1)} %compare_select_fusion.label_ref, bf16[3,352,2048]{2,1,0:T(8,128)(2,1)S(1)} %copy-done), custom_call_target="tpu_custom_call" | custom-call | flops 2000000000 | bytes 100000 | tf_op jit(solution)/shard_map/prepare_own/pallas_call | solution.py:341
  31.8 1.3 copy-done.4
  33.1 1.4 copy-done.5
  34.4 1.2 copy-done.6
  35.6 10.0 %collective-permute-done.refs_4_ = bf16[2,352,512]{2,1,0:T(8,128)(2,1)S(1)} collective-permute-done((bf16[2,352,512]{2,1,0:T(8,128)(2,1)S(1)}, bf16[2,352,512]{2,1,0:T(8,128)(2,1)S(1)}, u32[]{:S(2)}, u32[]{:S(2)}) %collective-permute-start) | collective-permute-done | bytes 720928 | tf_op jit(solution)/shard_map/ppermute | solution.py:298
  45.6 2.3 %collective-permute-done.1.refs_5_ = bf16[2,352,512]{2,1,0:T(8,128)(2,1)} collective-permute-done((bf16[2,352,512]{2,1,0:T(8,128)(2,1)S(1)}, bf16[2,352,512]{2,1,0:T(8,128)(2,1)}, u32[]{:S(2)}, u32[]{:S(2)}) %collective-permute-start.1) | collective-permute-done | bytes 720928 | tf_op jit(solution)/shard_map/ppermute | solution.py:299
  47.9 0.1 fusion.23
  48.0 0.2 collective-permute-start.2
  48.2 4.5 %collective-permute-start.3 = (bf16[2,352,256]{2,1,0:T(8,128)(2,1)S(1)}, bf16[2,352,256]{2,1,0:T(8,128)(2,1)}, u32[]{:S(2)}, u32[]{:S(2)}) collective-permute-start(bf16[2,352,256]{2,1,0:T(8,128)(2,1)S(1)} %get-tuple-element.56), channel_id=1, source_target_pairs={{4,0},{8,4},{12,8},{16,12},{20,16},{24,20},{28,24},{0,28},{5,1},{9... | collective-permute-start | bytes 1081352 | tf_op jit(solution)/shard_map/ppermute | solution.py:299
  52.8 13.3 %attend.3.refs_8_.refs_0_ = bf16[352,1024]{1,0:T(8,128)(2,1)} custom-call(s32[2,8]{1,0:T(2,128)} %stack.34.bounds, s32[16,1,256]{2,1,0:T(1,128)} %copy-done.2, bf16[512,512]{1,0:T(8,128)(2,1)} %copy-done.1, bf16[8,4,128,256]{3,2,1,0:T(8,128)(2,1)} %copy-done.4, bf16[8,4,256,128]{3,2,1,0:T(8,128)(2,1)} %copy-done.5, bf16[8,4,96,256]{3,2,1,0:T(8,128)(2,1)} %copy-done.6, ...), custom_call_target="tpu_custom_call" | custom-call | flops 12999999488 | bytes 100000 | tf_op jit(solution)/shard_map/attend/pallas_call | solution.py:457
  66.0 1.6 %collective-permute-start.10 = (bf16[352,1024]{1,0:T(8,128)(2,1)}, bf16[352,1024]{1,0:T(8,128)(2,1)}, u32[]{:S(2)}, u32[]{:S(2)}) collective-permute-start(bf16[352,1024]{1,0:T(8,128)(2,1)} %attend.3.refs_8_.refs_0_), channel_id=1, source_target_pairs={{0,2},{1,3},{2,0},{3,1},{4,6},{5,7},{6,4},{7,5},{8,10},{9,11},{10,... | collective-permute-start | bytes 2162696 | tf_op jit(solution)/shard_map/ppermute | solution.py:406
  67.6 1.3 fusion.22
  68.9 0.1 collective-permute-start.5
  69.0 4.7 %collective-permute-start.6 = (bf16[2,352,256]{2,1,0:T(8,128)(2,1)S(1)}, bf16[2,352,256]{2,1,0:T(8,128)(2,1)}, u32[]{:S(2)}, u32[]{:S(2)}) collective-permute-start(bf16[2,352,256]{2,1,0:T(8,128)(2,1)S(1)} %get-tuple-element.54), channel_id=1, source_target_pairs={{4,0},{8,4},{12,8},{16,12},{20,16},{24,20},{28,24},{0,28},{5,1},{9... | collective-permute-start | bytes 1081352 | tf_op jit(solution)/shard_map/ppermute | solution.py:299
  73.7 9.1 %attend.4.refs_10_.refs_0_ = bf16[352,512]{1,0:T(8,128)(2,1)} custom-call(s32[2,8]{1,0:T(2,128)} %stack.34.bounds, s32[16,1,256]{2,1,0:T(1,128)} %copy-done.2, bf16[512,512]{1,0:T(8,128)(2,1)} %copy-done.1, bf16[8,4,128,256]{3,2,1,0:T(8,128)(2,1)} %copy-done.4, bf16[8,4,256,128]{3,2,1,0:T(8,128)(2,1)} %copy-done.5, bf16[8,4,96,256]{3,2,1,0:T(8,128)(2,1)} %copy-done.6, ...), custom_call_target="tpu_custom_call" | custom-call | flops 8999999488 | bytes 100000 | tf_op jit(solution)/shard_map/attend/pallas_call | solution.py:457
  82.8 0.7 collective-permute-start.4
  83.6 0.5 collective-permute-start.12
  84.1 3.3 %collective-permute-done.6.refs_9_ = bf16[2,352,256]{2,1,0:T(8,128)(2,1)} collective-permute-done((bf16[2,352,256]{2,1,0:T(8,128)(2,1)S(1)}, bf16[2,352,256]{2,1,0:T(8,128)(2,1)}, u32[]{:S(2)}, u32[]{:S(2)}) %collective-permute-start.6) | collective-permute-done | bytes 360480 | tf_op jit(solution)/shard_map/ppermute | solution.py:299
  87.3 9.0 %attend.5.refs_4_.refs_8_ = bf16[352,512]{1,0:T(8,128)(2,1)} custom-call(s32[2,8]{1,0:T(2,128)} %stack.34.bounds, s32[16,1,256]{2,1,0:T(1,128)} %copy-done.2, bf16[512,512]{1,0:T(8,128)(2,1)} %copy-done.1, bf16[8,4,128,256]{3,2,1,0:T(8,128)(2,1)} %copy-done.4, bf16[8,4,256,128]{3,2,1,0:T(8,128)(2,1)} %copy-done.5, bf16[8,4,96,256]{3,2,1,0:T(8,128)(2,1)} %copy-done.6, ...), custom_call_target="tpu_custom_call" | custom-call | flops 8999999488 | bytes 100000 | tf_op jit(solution)/shard_map/attend/pallas_call | solution.py:457
  96.3 1.4 collective-permute-start.9
  97.7 0.5 collective-permute-start.8
  98.3 15.2 %project.2 = (bf16[352,1024]{1,0:T(8,128)(2,1)}, bf16[352,256]{1,0:T(8,128)(2,1)}) custom-call(s32[1]{0:T(128)} %bitcast.col_ref, f32[1408,1]{1,0:T(8,128)} %broadcast_in_dim.42.gain_ref, bf16[512,512]{1,0:T(8,128)(2,1)} %copy-done.1, bf16[4,4,352,512]{3,2,1,0:T(8,128)(2,1)} %bitcast.56, bf16[1408,1408]{1,0:T(8,128)(2,1)} %bitcast.52, ...), custom_call_target="tpu_custom_call" | custom-call | flops 12000000000 | bytes 100000 | tf_op jit(solution)/shard_map/project/pallas_call | solution.py:414
  113.5 0.1 collective-permute-start.13
  113.6 0.4 collective-permute-start.14
  114.1 1.1 collective-permute-done.13.refs_6_
  115.2 0.7 copy-done.22
  116.0 15.4 %project.3 = (bf16[352,1024]{1,0:T(8,128)(2,1)}, bf16[352,256]{1,0:T(8,128)(2,1)}) custom-call(s32[1]{0:T(128)} %bitcast.col_ref, f32[1408,1]{1,0:T(8,128)} %broadcast_in_dim.42.gain_ref, bf16[512,512]{1,0:T(8,128)(2,1)} %copy-done.1, bf16[4,4,352,512]{3,2,1,0:T(8,128)(2,1)} %bitcast.57, bf16[1408,1408]{1,0:T(8,128)(2,1)} %bitcast.53, ...), custom_call_target="tpu_custom_call" | custom-call | flops 12000000000 | bytes 100000 | tf_op jit(solution)/shard_map/project/pallas_call | solution.py:414
  131.4 0.9 copy-done.8
  132.3 0.5 outgoing.1
  132.8 0.1 collective-permute-start.15
  132.8 2.1 %collective-permute-start.16 = (bf16[64,384]{1,0:T(8,128)(2,1)S(1)}, bf16[64,384]{1,0:T(8,128)(2,1)S(1)}, u32[]{:S(2)}, u32[]{:S(2)}) collective-permute-start(bf16[64,384]{1,0:T(8,128)(2,1)S(1)} %get-tuple-element.46), channel_id=1, source_target_pairs={{0,8},{4,12},{8,16},{12,20},{16,24},{20,28},{24,0},{28,4},{1,9},{5... | collective-permute-start | bytes 147464 | tf_op jit(solution)/shard_map/ppermute | solution.py:542
  134.9 4.2 %collective-permute-start.17 = (bf16[64,384]{1,0:T(8,128)(2,1)S(1)}, bf16[64,384]{1,0:T(8,128)(2,1)S(1)}, u32[]{:S(2)}, u32[]{:S(2)}) collective-permute-start(bf16[64,384]{1,0:T(8,128)(2,1)S(1)} %get-tuple-element.47), channel_id=1, source_target_pairs={{0,12},{4,16},{8,20},{12,24},{16,28},{20,0},{24,4},{28,8},{1,13},{... | collective-permute-start | bytes 147464 | tf_op jit(solution)/shard_map/ppermute | solution.py:542
  139.1 1.0 collective-permute-start.18
  140.1 1.4 collective-permute-start.19
  141.7 1.0 collective-permute-start.20
  142.7 2.2 %collective-permute-start.21 = (bf16[64,384]{1,0:T(8,128)(2,1)S(1)}, bf16[64,384]{1,0:T(8,128)(2,1)S(1)}, u32[]{:S(2)}, u32[]{:S(2)}) collective-permute-start(bf16[64,384]{1,0:T(8,128)(2,1)S(1)} %get-tuple-element.51), channel_id=1, source_target_pairs={{0,28},{4,0},{8,4},{12,8},{16,12},{20,16},{24,20},{28,24},{1,29},{... | collective-permute-start | bytes 147464 | tf_op jit(solution)/shard_map/ppermute | solution.py:542
  145.0 0.4 collective-permute-done.18.refs_4_
  145.4 0.5 collective-permute-done.19.refs_5_
  145.9 1.5 collective-permute-done.20.refs_6_
  147.4 1.3 incoming.1
  (77 shorter events, 0.4 us)
Async XLA Ops:
  7.2 91.1 %all-gather.3.cloned.1.call-start = ((), (), s32[]{:S(2)}) async-start(), calls=%async_computation | async-start | bytes 7208960 | tf_op jit(solution)/shard_map/all_gather | solution.py:379
  7.2 1.8 %copy-start.3 = (bf16[352,2048]{1,0:T(8,128)(2,1)S(1)}, bf16[352,2048]{1,0:T(8,128)(2,1)}, u32[]{:S(2)}) copy-start(bf16[352,2048]{1,0:T(8,128)(2,1)} %high_ref) | copy-start | bytes 4325380
  8.9 2.8 %copy-start.1 = (bf16[512,512]{1,0:T(8,128)(2,1)}, bf16[512,512]{1,0:T(8,128)(2,1)S(1)}, u32[]{:S(2)}) copy-start(bf16[512,512]{1,0:T(8,128)(2,1)S(1)} %fusion.perm_ref.refs_0_.perm_hbm) | copy-start | bytes 1572868
  11.7 6.1 %copy-start.14 = (s32[32]{0:T(128)S(1)}, s32[32]{0:T(128)}, u32[]{:S(2)}) copy-start(s32[32]{0:T(128)} %param.12) | copy-start | bytes 388
  11.8 33.8 %collective-permute-start = (bf16[2,352,512]{2,1,0:T(8,128)(2,1)S(1)}, bf16[2,352,512]{2,1,0:T(8,128)(2,1)S(1)}, u32[]{:S(2)}, u32[]{:S(2)}) collective-permute-start(bf16[2,352,512]{2,1,0:T(8,128)(2,1)S(1)} %get-tuple-element.59), channel_id=1, source_target_pairs={{0,4},{4,8},{8,12},{12,16},{16,20},{20,24},{24,28},{28,0},{1,5},{5... | collective-permute-start | bytes 2162696 | tf_op jit(solution)/shard_map/ppermute | solution.py:298
  14.8 33.2 %collective-permute-start.1 = (bf16[2,352,512]{2,1,0:T(8,128)(2,1)S(1)}, bf16[2,352,512]{2,1,0:T(8,128)(2,1)}, u32[]{:S(2)}, u32[]{:S(2)}) collective-permute-start(bf16[2,352,512]{2,1,0:T(8,128)(2,1)S(1)} %get-tuple-element.58), channel_id=1, source_target_pairs={{4,0},{8,4},{12,8},{16,12},{20,16},{24,20},{28,24},{0,28},{5,1},{9... | collective-permute-start | bytes 2162696 | tf_op jit(solution)/shard_map/ppermute | solution.py:299
  18.5 6.5 %copy-start.12 = (f32[1408]{0:T(1024)S(1)}, f32[1408]{0:T(1024)}, u32[]{:S(2)}) copy-start(f32[1408]{0:T(1024)} %param.11) | copy-start | bytes 16900
  18.5 7.6 %copy-start.13 = (s32[512]{0:T(512)S(1)}, s32[512]{0:T(512)}, u32[]{:S(2)}) copy-start(s32[512]{0:T(512)} %param.13) | copy-start | bytes 6148
  27.7 2.2 %copy-start = (bf16[3,352,2048]{2,1,0:T(8,128)(2,1)S(1)}, bf16[3,352,2048]{2,1,0:T(8,128)(2,1)}, u32[]{:S(2)}) copy-start(bf16[3,352,2048]{2,1,0:T(8,128)(2,1)} %qkv_ref) | copy-start | bytes 12976132
  29.9 1.8 %copy-start.2 = (s32[16,1,256]{2,1,0:T(1,128)}, s32[16,1,256]{2,1,0:T(1,128)S(1)}, u32[]{:S(2)}) copy-start(s32[16,1,256]{2,1,0:T(1,128)S(1)} %compare_select_fusion.label_ref) | copy-start | bytes 49156
  31.8 1.3 copy-start.4
  33.1 1.4 copy-start.5
  34.4 1.2 copy-start.6
  45.6 7.1 %copy-start.15 = (bf16[2,352,512]{2,1,0:T(8,128)(2,1)}, bf16[2,352,512]{2,1,0:T(8,128)(2,1)S(1)}, u32[]{:S(2)}) copy-start(bf16[2,352,512]{2,1,0:T(8,128)(2,1)S(1)} %collective-permute-done.refs_4_) | copy-start | bytes 2162692
  48.0 19.6 %collective-permute-start.2 = (bf16[2,352,256]{2,1,0:T(8,128)(2,1)S(1)}, bf16[2,352,256]{2,1,0:T(8,128)(2,1)S(1)}, u32[]{:S(2)}, u32[]{:S(2)}) collective-permute-start(bf16[2,352,256]{2,1,0:T(8,128)(2,1)S(1)} %get-tuple-element.57), channel_id=1, source_target_pairs={{0,4},{4,8},{8,12},{12,16},{16,20},{20,24},{24,28},{28,0},{1,5},{5... | collective-permute-start | bytes 1081352 | tf_op jit(solution)/shard_map/ppermute | solution.py:298
  48.2 19.4 %collective-permute-start.3 = (bf16[2,352,256]{2,1,0:T(8,128)(2,1)S(1)}, bf16[2,352,256]{2,1,0:T(8,128)(2,1)}, u32[]{:S(2)}, u32[]{:S(2)}) collective-permute-start(bf16[2,352,256]{2,1,0:T(8,128)(2,1)S(1)} %get-tuple-element.56), channel_id=1, source_target_pairs={{4,0},{8,4},{12,8},{16,12},{20,16},{24,20},{28,24},{0,28},{5,1},{9... | collective-permute-start | bytes 1081352 | tf_op jit(solution)/shard_map/ppermute | solution.py:299
  66.0 17.5 %collective-permute-start.10 = (bf16[352,1024]{1,0:T(8,128)(2,1)}, bf16[352,1024]{1,0:T(8,128)(2,1)}, u32[]{:S(2)}, u32[]{:S(2)}) collective-permute-start(bf16[352,1024]{1,0:T(8,128)(2,1)} %attend.3.refs_8_.refs_0_), channel_id=1, source_target_pairs={{0,2},{1,3},{2,0},{3,1},{4,6},{5,7},{6,4},{7,5},{8,10},{9,11},{10,... | collective-permute-start | bytes 2162696 | tf_op jit(solution)/shard_map/ppermute | solution.py:406
  67.6 6.1 %copy-start.21 = (bf16[2,352,256]{2,1,0:T(8,128)(2,1)}, bf16[2,352,256]{2,1,0:T(8,128)(2,1)S(1)}, u32[]{:S(2)}) copy-start(bf16[2,352,256]{2,1,0:T(8,128)(2,1)S(1)} %collective-permute-done.2.refs_6_) | copy-start | bytes 1081348
  68.9 15.2 %collective-permute-start.5 = (bf16[2,352,256]{2,1,0:T(8,128)(2,1)S(1)}, bf16[2,352,256]{2,1,0:T(8,128)(2,1)}, u32[]{:S(2)}, u32[]{:S(2)}) collective-permute-start(bf16[2,352,256]{2,1,0:T(8,128)(2,1)S(1)} %get-tuple-element.55), channel_id=1, source_target_pairs={{0,4},{4,8},{8,12},{12,16},{16,20},{20,24},{24,28},{28,0},{1,5},{5... | collective-permute-start | bytes 1081352 | tf_op jit(solution)/shard_map/ppermute | solution.py:298
  69.0 14.6 %copy-start.16 = (bf16[352,1024]{1,0:T(8,128)(2,1)S(1)}, bf16[352,1024]{1,0:T(8,128)(2,1)}, u32[]{:S(2)}) copy-start(bf16[352,1024]{1,0:T(8,128)(2,1)} %attend.3.refs_8_.refs_0_) | copy-start | bytes 2162692
  69.0 18.4 %collective-permute-start.6 = (bf16[2,352,256]{2,1,0:T(8,128)(2,1)S(1)}, bf16[2,352,256]{2,1,0:T(8,128)(2,1)}, u32[]{:S(2)}, u32[]{:S(2)}) collective-permute-start(bf16[2,352,256]{2,1,0:T(8,128)(2,1)S(1)} %get-tuple-element.54), channel_id=1, source_target_pairs={{4,0},{8,4},{12,8},{16,12},{20,16},{24,20},{28,24},{0,28},{5,1},{9... | collective-permute-start | bytes 1081352 | tf_op jit(solution)/shard_map/ppermute | solution.py:299
  82.8 14.9 %copy-start.17 = (bf16[352,512]{1,0:T(8,128)(2,1)S(1)}, bf16[352,512]{1,0:T(8,128)(2,1)}, u32[]{:S(2)}) copy-start(bf16[352,512]{1,0:T(8,128)(2,1)} %attend.4.refs_10_.refs_0_) | copy-start | bytes 1081348
  82.8 14.9 %collective-permute-start.4 = (bf16[352,512]{1,0:T(8,128)(2,1)}, bf16[352,512]{1,0:T(8,128)(2,1)}, u32[]{:S(2)}, u32[]{:S(2)}) collective-permute-start(bf16[352,512]{1,0:T(8,128)(2,1)} %attend.4.refs_10_.refs_0_), channel_id=1, source_target_pairs={{0,2},{1,3},{2,0},{3,1},{4,6},{5,7},{6,4},{7,5},{8,10},{9,11},{10,... | collective-permute-start | bytes 1081352 | tf_op jit(solution)/shard_map/ppermute | solution.py:406
  83.6 14.7 %collective-permute-start.11 = (bf16[352,1024]{1,0:T(8,128)(2,1)S(1)}, bf16[352,1024]{1,0:T(8,128)(2,1)}, u32[]{:S(2)}, u32[]{:S(2)}) collective-permute-start(bf16[352,1024]{1,0:T(8,128)(2,1)S(1)} %copy-done.16), channel_id=1, source_target_pairs={{0,1},{1,0},{2,3},{3,2},{4,5},{5,4},{6,7},{7,6},{8,9},{9,8},{10,11... | collective-permute-start | bytes 2162696 | tf_op jit(solution)/shard_map/ppermute | solution.py:406
  83.6 14.7 %collective-permute-start.12 = (bf16[352,1024]{1,0:T(8,128)(2,1)}, bf16[352,1024]{1,0:T(8,128)(2,1)}, u32[]{:S(2)}, u32[]{:S(2)}) collective-permute-start(bf16[352,1024]{1,0:T(8,128)(2,1)} %collective-permute-done.10.refs_1_), channel_id=1, source_target_pairs={{0,1},{1,0},{2,3},{3,2},{4,5},{5,4},{6,7},{7,6},{8,9},{9,8},{10,11... | collective-permute-start | bytes 2162696 | tf_op jit(solution)/shard_map/ppermute | solution.py:406
  96.3 17.1 %collective-permute-start.9 = (bf16[352,512]{1,0:T(8,128)(2,1)}, bf16[352,512]{1,0:T(8,128)(2,1)S(1)}, u32[]{:S(2)}, u32[]{:S(2)}) collective-permute-start(bf16[352,512]{1,0:T(8,128)(2,1)} %attend.5.refs_4_.refs_8_), channel_id=1, source_target_pairs={{0,2},{1,3},{2,0},{3,1},{4,6},{5,7},{6,4},{7,5},{8,10},{9,11},{10,... | collective-permute-start | bytes 1081352 | tf_op jit(solution)/shard_map/ppermute | solution.py:406
  97.7 16.4 %collective-permute-start.7 = (bf16[352,512]{1,0:T(8,128)(2,1)S(1)}, bf16[352,512]{1,0:T(8,128)(2,1)S(1)}, u32[]{:S(2)}, u32[]{:S(2)}) collective-permute-start(bf16[352,512]{1,0:T(8,128)(2,1)S(1)} %copy-done.17), channel_id=1, source_target_pairs={{0,1},{1,0},{2,3},{3,2},{4,5},{5,4},{6,7},{7,6},{8,9},{9,8},{10,11... | collective-permute-start | bytes 1081352 | tf_op jit(solution)/shard_map/ppermute | solution.py:406
  97.7 16.4 %collective-permute-start.8 = (bf16[352,512]{1,0:T(8,128)(2,1)}, bf16[352,512]{1,0:T(8,128)(2,1)}, u32[]{:S(2)}, u32[]{:S(2)}) collective-permute-start(bf16[352,512]{1,0:T(8,128)(2,1)} %collective-permute-done.4.refs_1_), channel_id=1, source_target_pairs={{0,1},{1,0},{2,3},{3,2},{4,5},{5,4},{6,7},{7,6},{8,9},{9,8},{10,11... | collective-permute-start | bytes 1081352 | tf_op jit(solution)/shard_map/ppermute | solution.py:406
  98.3 15.2 %copy-start.18 = (bf16[352,512]{1,0:T(8,128)(2,1)S(1)}, bf16[352,512]{1,0:T(8,128)(2,1)}, u32[]{:S(2)}) copy-start(bf16[352,512]{1,0:T(8,128)(2,1)} %attend.5.refs_4_.refs_8_) | copy-start | bytes 1081348
  113.4 2.5 %copy-start.19 = (bf16[352,512]{1,0:T(8,128)(2,1)}, bf16[352,512]{1,0:T(8,128)(2,1)S(1)}, u32[]{:S(2)}) copy-start(bf16[352,512]{1,0:T(8,128)(2,1)S(1)} %collective-permute-done.9.refs_5_) | copy-start | bytes 1081348
  113.5 1.7 %collective-permute-start.13 = (bf16[352,512]{1,0:T(8,128)(2,1)S(1)}, bf16[352,512]{1,0:T(8,128)(2,1)S(1)}, u32[]{:S(2)}, u32[]{:S(2)}) collective-permute-start(bf16[352,512]{1,0:T(8,128)(2,1)S(1)} %copy-done.18), channel_id=1, source_target_pairs={{0,1},{1,0},{2,3},{3,2},{4,5},{5,4},{6,7},{7,6},{8,9},{9,8},{10,11... | collective-permute-start | bytes 1081352 | tf_op jit(solution)/shard_map/ppermute | solution.py:406
  113.6 2.4 %collective-permute-start.14 = (bf16[352,512]{1,0:T(8,128)(2,1)S(1)}, bf16[352,512]{1,0:T(8,128)(2,1)}, u32[]{:S(2)}, u32[]{:S(2)}) collective-permute-start(bf16[352,512]{1,0:T(8,128)(2,1)S(1)} %collective-permute-done.9.refs_5_), channel_id=1, source_target_pairs={{0,1},{1,0},{2,3},{3,2},{4,5},{5,4},{6,7},{7,6},{8,9},{9,8},{10,11... | collective-permute-start | bytes 1081352 | tf_op jit(solution)/shard_map/ppermute | solution.py:406
  114.1 17.3 %copy-start.7 = (bf16[352,256]{1,0:T(8,128)(2,1)S(1)}, bf16[352,256]{1,0:T(8,128)(2,1)}, u32[]{:S(2)}) copy-start(bf16[352,256]{1,0:T(8,128)(2,1)} %get-tuple-element.42.refs_0_) | copy-start | bytes 540676
  114.1 1.9 %copy-start.20 = (bf16[352,512]{1,0:T(8,128)(2,1)}, bf16[352,512]{1,0:T(8,128)(2,1)S(1)}, u32[]{:S(2)}) copy-start(bf16[352,512]{1,0:T(8,128)(2,1)S(1)} %collective-permute-done.7.refs_2_) | copy-start | bytes 1081348
  115.2 0.7 copy-start.22
  131.4 0.9 copy-start.8
  132.3 9.3 %copy-start.10 = (bf16[352,1024]{1,0:T(8,128)(2,1)S(1)}, bf16[352,1024]{1,0:T(8,128)(2,1)}, u32[]{:S(2)}) copy-start(bf16[352,1024]{1,0:T(8,128)(2,1)} %get-tuple-element.41) | copy-start | bytes 2162692
  132.3 9.3 %copy-start.9 = (bf16[352,1024]{1,0:T(8,128)(2,1)S(1)}, bf16[352,1024]{1,0:T(8,128)(2,1)}, u32[]{:S(2)}) copy-start(bf16[352,1024]{1,0:T(8,128)(2,1)} %get-tuple-element.38.refs_9_) | copy-start | bytes 2162692
  132.8 8.9 %collective-permute-start.15 = (bf16[64,384]{1,0:T(8,128)(2,1)S(1)}, bf16[64,384]{1,0:T(8,128)(2,1)S(1)}, u32[]{:S(2)}, u32[]{:S(2)}) collective-permute-start(bf16[64,384]{1,0:T(8,128)(2,1)S(1)} %get-tuple-element.45), channel_id=1, source_target_pairs={{0,4},{4,8},{8,12},{12,16},{16,20},{20,24},{24,28},{28,0},{1,5},{5... | collective-permute-start | bytes 147464 | tf_op jit(solution)/shard_map/ppermute | solution.py:542
  132.8 9.9 %collective-permute-start.16 = (bf16[64,384]{1,0:T(8,128)(2,1)S(1)}, bf16[64,384]{1,0:T(8,128)(2,1)S(1)}, u32[]{:S(2)}, u32[]{:S(2)}) collective-permute-start(bf16[64,384]{1,0:T(8,128)(2,1)S(1)} %get-tuple-element.46), channel_id=1, source_target_pairs={{0,8},{4,12},{8,16},{12,20},{16,24},{20,28},{24,0},{28,4},{1,9},{5... | collective-permute-start | bytes 147464 | tf_op jit(solution)/shard_map/ppermute | solution.py:542
  134.9 10.1 %collective-permute-start.17 = (bf16[64,384]{1,0:T(8,128)(2,1)S(1)}, bf16[64,384]{1,0:T(8,128)(2,1)S(1)}, u32[]{:S(2)}, u32[]{:S(2)}) collective-permute-start(bf16[64,384]{1,0:T(8,128)(2,1)S(1)} %get-tuple-element.47), channel_id=1, source_target_pairs={{0,12},{4,16},{8,20},{12,24},{16,28},{20,0},{24,4},{28,8},{1,13},{... | collective-permute-start | bytes 147464 | tf_op jit(solution)/shard_map/ppermute | solution.py:542
  139.1 6.3 %collective-permute-start.18 = (bf16[64,384]{1,0:T(8,128)(2,1)S(1)}, bf16[64,384]{1,0:T(8,128)(2,1)S(1)}, u32[]{:S(2)}, u32[]{:S(2)}) collective-permute-start(bf16[64,384]{1,0:T(8,128)(2,1)S(1)} %get-tuple-element.48), channel_id=1, source_target_pairs={{0,16},{4,20},{8,24},{12,28},{16,0},{20,4},{24,8},{28,12},{1,17},{... | collective-permute-start | bytes 147464 | tf_op jit(solution)/shard_map/ppermute | solution.py:542
  140.1 5.8 %collective-permute-start.19 = (bf16[64,384]{1,0:T(8,128)(2,1)S(1)}, bf16[64,384]{1,0:T(8,128)(2,1)S(1)}, u32[]{:S(2)}, u32[]{:S(2)}) collective-permute-start(bf16[64,384]{1,0:T(8,128)(2,1)S(1)} %get-tuple-element.49), channel_id=1, source_target_pairs={{0,20},{4,24},{8,28},{12,0},{16,4},{20,8},{24,12},{28,16},{1,21},{... | collective-permute-start | bytes 147464 | tf_op jit(solution)/shard_map/ppermute | solution.py:542
  141.7 5.7 %collective-permute-start.20 = (bf16[64,384]{1,0:T(8,128)(2,1)S(1)}, bf16[64,384]{1,0:T(8,128)(2,1)S(1)}, u32[]{:S(2)}, u32[]{:S(2)}) collective-permute-start(bf16[64,384]{1,0:T(8,128)(2,1)S(1)} %get-tuple-element.50), channel_id=1, source_target_pairs={{0,24},{4,28},{8,0},{12,4},{16,8},{20,12},{24,16},{28,20},{1,25},{... | collective-permute-start | bytes 147464 | tf_op jit(solution)/shard_map/ppermute | solution.py:542
  142.7 4.6 %collective-permute-start.21 = (bf16[64,384]{1,0:T(8,128)(2,1)S(1)}, bf16[64,384]{1,0:T(8,128)(2,1)S(1)}, u32[]{:S(2)}, u32[]{:S(2)}) collective-permute-start(bf16[64,384]{1,0:T(8,128)(2,1)S(1)} %get-tuple-element.51), channel_id=1, source_target_pairs={{0,28},{4,0},{8,4},{12,8},{16,12},{20,16},{24,20},{28,24},{1,29},{... | collective-permute-start | bytes 147464 | tf_op jit(solution)/shard_map/ppermute | solution.py:542
  145.0 3.7 %copy-start.11 = (bf16[352,2048]{1,0:T(8,128)(2,1)}, bf16[352,2048]{1,0:T(8,128)(2,1)S(1)}, u32[]{:S(2)}) copy-start(bf16[352,2048]{1,0:T(8,128)(2,1)S(1)} %slice_dynamic-update-slice_fusion) | copy-start | bytes 4325380
Sparse Core Ops, SparseCore 0:
  11.9 46.0 all-gather.2
